TPU v7x, 32 devices: a whole 2x2x4 slice. The times are simulated.
32 devices in a mesh: dp: 8 (over y, x, core), tensor: 4 (over z).
Axes of the slice: x: 2, y: 2, z: 4, core: 2. Of those that a mesh axis runs over, the one named last changes fastest.
Arguments:
- tokens: bfloat16 [16384, 1024], P(('dp', 'tensor')), may hold values from -6 to 6
- gate_value_weight: bfloat16 [2, 1024, 2, 2048], P(None, 'dp', None, 'tensor'), may hold values from -0.1875 to 0.1875
- w_bc: bfloat16 [2, 1024, 256], P(None, 'dp'), may hold values from -0.1875 to 0.1875
- w_dt: bfloat16 [2, 1024, 32], P(None, 'dp', 'tensor'), may hold values from -0.1875 to 0.1875
- w_out: bfloat16 [2, 1024, 2048], P(None, 'dp', 'tensor'), may hold values from -0.125 to 0.125
- norm_gain: float32 [2, 1024], replicated, may hold values from 0.5 to 1.5
- conv_value_w: float32 [2, 4, 2048], P(None, None, 'tensor'), may hold values from -3 to 3
- conv_value_b: float32 [2, 2048], P(None, 'tensor'), may hold values from -2 to 2
- conv_shared_w: float32 [2, 4, 256], replicated, may hold values from -3 to 3
- conv_shared_b: float32 [2, 256], replicated, may hold values from -2 to 2
- step_bias: float32 [2, 32], P(None, 'tensor'), may hold values from -7 to -3
- decay_log: float32 [2, 32], P(None, 'tensor'), may hold values from 0 to 2.77
- skip_gain: float32 [2, 32], P(None, 'tensor'), may hold values from 0.5 to 1.5
- gate_gain: float32 [2, 2048], P(None, 'tensor'), may hold values from 0.5 to 1.5
- starts: int32 [8, 4], P('dp'), may hold values from 0 to 2047, as said below
- cotangent: bfloat16 [16384, 1024], P(('dp', 'tensor')), may hold values from -6 to 6
Outputs:
- output: bfloat16 [16384, 1024], P(('dp', 'tensor'))
- grad_input: float32 [16384, 1024], P(('dp', 'tensor'))
- grad_w_zx: float32 [2, 1024, 2, 2048], P(None, 'dp', None, 'tensor')
- grad_w_bc: float32 [2, 1024, 256], P(None, 'dp')
- grad_w_dt: float32 [2, 1024, 32], P(None, 'dp', 'tensor')
- grad_w_out: float32 [2, 1024, 2048], P(None, 'dp', 'tensor')
- grad_norm_gain: float32 [2, 1024], replicated
- grad_conv_value_w: float32 [2, 4, 2048], P(None, None, 'tensor')
- grad_conv_value_b: float32 [2, 2048], P(None, 'tensor')
- grad_conv_shared_w: float32 [2, 4, 256], replicated
- grad_conv_shared_b: float32 [2, 256], replicated
- grad_step_bias: float32 [2, 32], P(None, 'tensor')
- grad_decay_log: float32 [2, 32], P(None, 'tensor')
- grad_skip_gain: float32 [2, 32], P(None, 'tensor')
- grad_gate_gain: float32 [2, 2048], P(None, 'tensor')
Inputs may be any that keep to these rules, and one draw needn't show every extreme that they name: Each row lists the first positions of its 4 documents in increasing order, the first being 0; in each row one document starts before position 512 and ends at position 1536 or later.
All inputs are finite; a program needn't handle non-finite values.
Results may differ from a plain program's by a relative error of at most 0.013.
Values may be sent and summed in bfloat16 or wider, within the bound.
A program may use at most 256 MiB of HBM per device.

v0:
```python
from functools import partial

import jax
import jax.numpy as jnp
from jax import lax
from jax.sharding import PartitionSpec as P

INNER = 2048
SPAN = 256
LAYERS = 2


norm_eps = 1e-05
highest_precision = lax.Precision.HIGHEST


def causal_conv(values, weight, bias, segment):
    length = values.shape[0]
    total = jnp.zeros_like(values) + bias
    for shift in range(weight.shape[0]):
        moved = jnp.pad(values, ((shift, 0), (0, 0)))[:length]
        moved_label = jnp.pad(segment, (shift, 0), constant_values=-1)[:length]
        keep = (moved_label == segment).astype(values.dtype)
        total = total + weight[shift] * moved * keep[:, None]
    return total


def span_scan(per_head, steps, decays, in_map, out_map, segment):
    length, heads, width = per_head.shape
    count = length // SPAN
    blocks = (
        per_head.reshape(count, SPAN, heads, width),
        steps.reshape(count, SPAN, heads),
        decays.reshape(count, SPAN, heads),
        in_map.reshape(count, SPAN, -1),
        out_map.reshape(count, SPAN, -1),
        segment.reshape(count, SPAN),
    )

    def advance(carry, block):
        state, before = carry
        values, sizes, rates, keys_in, reads_out, labels = block
        summed = jnp.cumsum(rates, axis=0)
        order = jnp.arange(SPAN, dtype=jnp.int32)
        same = (labels[:, None] == labels[None, :]) & (order[:, None] >= order[None, :])
        across = summed.T[:, :, None] - summed.T[:, None, :]
        decay_mask = jnp.where(same[None], jnp.exp(jnp.where(same[None], across, 0.0)), 0.0)
        intersection = jnp.dot(reads_out, keys_in.T, precision=highest_precision)
        layer_parameters = intersection[None] * decay_mask * sizes.T[:, None, :]
        inside = jnp.einsum("hts,shp->thp", layer_parameters, values, precision=highest_precision)
        carried = (labels == before).astype(summed.dtype)
        reach = jnp.exp(summed) * carried[:, None]
        outside = (
            jnp.einsum("tn,hpn->thp", reads_out, state, precision=highest_precision)
            * reach[:, :, None]
        )
        final = labels[SPAN - 1]
        tail = (labels == final).astype(summed.dtype)
        toward = jnp.exp(summed[SPAN - 1][None, :] - summed) * sizes * tail[:, None]
        kept_part = jnp.exp(summed[SPAN - 1]) * (final == before).astype(summed.dtype)
        weighted = values * toward[:, :, None]
        fresh = jnp.einsum("shp,sn->hpn", weighted, keys_in, precision=highest_precision)
        return ((kept_part[:, None, None] * state + fresh, final), inside + outside)

    begin = (jnp.zeros((heads, width, in_map.shape[1]), per_head.dtype), jnp.int32(-1))
    ended, outputs = lax.scan(jax.checkpoint(advance), begin, blocks)
    return outputs.reshape(length, heads, width)


def mixer_local(
    gate_in,
    value_in,
    shared_in,
    step_in,
    conv_value_w,
    conv_value_b,
    conv_shared_w,
    conv_shared_b,
    step_bias,
    decay_log,
    skip_gain,
    segment=None,
):
    state_size = shared_in.shape[1] // 2
    heads = step_in.shape[1]
    values = jax.nn.silu(causal_conv(value_in, conv_value_w, conv_value_b, segment))
    shared = jax.nn.silu(causal_conv(shared_in, conv_shared_w, conv_shared_b, segment))
    steps = jax.nn.softplus(step_in + step_bias)
    decays = -steps * jnp.exp(decay_log)
    per_head = values.reshape(values.shape[0], heads, -1)
    scanned = span_scan(
        per_head, steps, decays, shared[:, :state_size], shared[:, state_size:], segment
    )
    scanned = scanned + skip_gain[None, :, None] * per_head
    return scanned.reshape(values.shape) * jax.nn.silu(gate_in)


def rms_rows(resid, gain):
    return resid * lax.rsqrt(jnp.mean(resid * resid, axis=1, keepdims=True) + norm_eps) * gain


def fetch_layer(gate_value_weight, w_bc, w_dt, w_out, layer):
    return (
        lax.all_gather(gate_value_weight[layer], "dp", axis=0, tiled=True),
        lax.all_gather(w_bc[layer], "dp", axis=0, tiled=True),
        lax.all_gather(w_dt[layer], "dp", axis=0, tiled=True),
        lax.all_gather(w_out[layer], "dp", axis=0, tiled=True),
    )


def local(
    tokens,
    gate_value_weight,
    w_bc,
    w_dt,
    w_out,
    norm_gain,
    conv_value_w,
    conv_value_b,
    conv_shared_w,
    conv_shared_b,
    step_bias,
    decay_log,
    skip_gain,
    gate_gain,
    starts,
    cotangent,
):
    pieces = lax.axis_size("tensor")
    tok_rows = tokens.shape[0]
    length = pieces * tok_rows
    positions = lax.iota(jnp.int32, length)
    labels = jnp.sum(
        (positions[:, None] >= starts[0][None, :]).astype(jnp.int32), axis=1, dtype=jnp.int32
    ) - jnp.int32(1)
    resid = tokens.astype(jnp.float32)
    saved = []
    for layer in range(LAYERS):
        scaled, norm_pull = jax.vjp(rms_rows, resid, norm_gain[layer])
        normed_local = scaled.astype(jnp.bfloat16)
        normalized_rows = lax.all_gather(normed_local, "tensor", axis=0, tiled=True)
        loaded_weights = fetch_layer(gate_value_weight, w_bc, w_dt, w_out, layer)
        paired_pieces = jnp.einsum(
            "ql,lga->qga", normalized_rows, loaded_weights[0], preferred_element_type=jnp.float32
        )
        shared = jnp.dot(normalized_rows, loaded_weights[1], preferred_element_type=jnp.float32)
        step_in = jnp.dot(normalized_rows, loaded_weights[2], preferred_element_type=jnp.float32)
        gated, mixer_pull = jax.vjp(
            partial(mixer_local, segment=labels),
            paired_pieces[:, 0],
            paired_pieces[:, 1],
            shared,
            step_in,
            conv_value_w[layer],
            conv_value_b[layer],
            conv_shared_w[layer],
            conv_shared_b[layer],
            step_bias[layer],
            decay_log[layer],
            skip_gain[layer],
        )
        squares = lax.psum(jnp.sum(gated * gated, axis=1), "tensor")
        factor = lax.rsqrt(squares / INNER + norm_eps)
        mixed_in = (gated * factor[:, None] * gate_gain[layer]).astype(jnp.bfloat16)
        out_weight = loaded_weights[3]
        branch = lax.psum_scatter(
            jnp.einsum("ti,di->td", mixed_in, out_weight, preferred_element_type=jnp.float32),
            "tensor",
            scatter_dimension=0,
            tiled=True,
        )
        resid = resid + branch
        saved.append(
            (
                norm_pull,
                normed_local,
                normalized_rows,
                loaded_weights,
                mixer_pull,
                gated,
                factor,
                mixed_in,
            )
        )
    output = resid.astype(jnp.bfloat16)
    grad = cotangent.astype(jnp.float32)
    big_terms = [None] * LAYERS
    small_terms = [None] * LAYERS
    for layer in reversed(range(LAYERS)):
        (
            norm_pull,
            normed_local,
            normalized_rows,
            kept_weights,
            mixer_pull,
            gated,
            factor,
            mixed_in,
        ) = saved[layer]
        layer_parameters = fetch_layer(gate_value_weight, w_bc, w_dt, w_out, layer)
        grad_rows = lax.all_gather(grad.astype(jnp.bfloat16), "tensor", axis=0, tiled=True)
        grad_out = jnp.einsum("td,ti->di", grad_rows, mixed_in, preferred_element_type=jnp.float32)
        grad_mixed = jnp.einsum(
            "td,di->ti", grad_rows, layer_parameters[3], preferred_element_type=jnp.float32
        )
        weighted = grad_mixed * gate_gain[layer]
        grad_gate_gain = jnp.sum(grad_mixed * gated * factor[:, None], axis=0)
        dots = lax.psum(jnp.sum(weighted * gated, axis=1), "tensor")
        grad_gated = (
            factor[:, None] * weighted - gated * (factor * factor * factor * dots / INNER)[:, None]
        )
        (
            grad_gate,
            grad_value,
            grad_shared,
            grad_step,
            grad_cvw,
            grad_cvb,
            grad_csw,
            grad_csb,
            grad_bias,
            grad_decay,
            grad_skip,
        ) = mixer_pull(grad_gated)
        grad_paired_pieces = jnp.stack([grad_gate, grad_value], axis=1).astype(jnp.bfloat16)
        grad_step_low = grad_step.astype(jnp.bfloat16)
        grad_wzx = jnp.einsum(
            "lq,lan->qan", normalized_rows, grad_paired_pieces, preferred_element_type=jnp.float32
        )
        grad_wdt = jnp.einsum(
            "td,th->dh", normalized_rows, grad_step_low, preferred_element_type=jnp.float32
        )
        grad_normed_rows = jnp.einsum(
            "bxp,sxp->bs",
            grad_paired_pieces,
            layer_parameters[0],
            preferred_element_type=jnp.float32,
        )
        grad_normed_rows = grad_normed_rows + jnp.einsum(
            "th,dh->td", grad_step_low, layer_parameters[2], preferred_element_type=jnp.float32
        )
        grad_normed, grad_shared_local = (
            lax.psum_scatter(grad_normed_rows, "tensor", scatter_dimension=0, tiled=True),
            lax.psum_scatter(grad_shared, "tensor", scatter_dimension=0, tiled=True),
        )
        shared_low = grad_shared_local.astype(jnp.bfloat16)
        grad_wbc = jnp.einsum(
            "td,tn->dn", normed_local, shared_low, preferred_element_type=jnp.float32
        )
        grad_normed = grad_normed + jnp.einsum(
            "tn,dn->td", shared_low, layer_parameters[1], preferred_element_type=jnp.float32
        )
        grad_resid, grad_norm_gain = norm_pull(grad_normed)
        grad = grad + grad_resid
        terms = (grad_wzx, grad_wbc, grad_wdt, grad_out)
        terms = (
            lax.psum_scatter(grad_wzx, "dp", scatter_dimension=0, tiled=True),
            lax.psum_scatter(grad_wbc, "dp", scatter_dimension=0, tiled=True),
            lax.psum_scatter(grad_wdt, "dp", scatter_dimension=0, tiled=True),
            lax.psum_scatter(grad_out, "dp", scatter_dimension=0, tiled=True),
        )
        big_terms[layer] = terms
        small_terms[layer] = (
            grad_cvw,
            grad_cvb,
            grad_bias,
            grad_decay,
            grad_skip,
            grad_gate_gain,
            grad_norm_gain,
            grad_csw,
            grad_csb,
        )

    def stacked(group, member):
        return jnp.stack([group[layer][member] for layer in range(LAYERS)], axis=0)

    sum_zx = stacked(big_terms, 0)
    sum_bc = stacked(big_terms, 1)
    sum_dt = stacked(big_terms, 2)
    sum_out = stacked(big_terms, 3)
    sum_cvw, sum_cvb, sum_bias, sum_decay, sum_skip, sum_gate, sum_norm, sum_csw, sum_csb = (
        lax.psum(
            (
                stacked(small_terms, 0),
                stacked(small_terms, 1),
                stacked(small_terms, 2),
                stacked(small_terms, 3),
                stacked(small_terms, 4),
                stacked(small_terms, 5),
                stacked(small_terms, 6),
                stacked(small_terms, 7),
                stacked(small_terms, 8),
            ),
            "dp",
        )
    )
    sum_bc, sum_norm, sum_csw, sum_csb = (
        lax.psum(sum_bc.astype(jnp.bfloat16), "tensor").astype(jnp.float32),
        lax.psum(sum_norm.astype(jnp.bfloat16), "tensor").astype(jnp.float32),
        lax.psum(sum_csw.astype(jnp.bfloat16), "tensor").astype(jnp.float32),
        lax.psum(sum_csb.astype(jnp.bfloat16), "tensor").astype(jnp.float32),
    )
    return (
        output,
        grad,
        sum_zx,
        sum_bc,
        sum_dt,
        sum_out,
        sum_norm,
        sum_cvw,
        sum_cvb,
        sum_csw,
        sum_csb,
        sum_bias,
        sum_decay,
        sum_skip,
        sum_gate,
    )


def solution(mesh):
    in_specs = (
        P(("dp", "tensor"), None),
        P(None, "dp", None, "tensor"),
        P(None, "dp", None),
        P(None, "dp", "tensor"),
        P(None, "dp", "tensor"),
        P(),
        P(None, None, "tensor"),
        P(None, "tensor"),
        P(),
        P(),
        P(None, "tensor"),
        P(None, "tensor"),
        P(None, "tensor"),
        P(None, "tensor"),
        P("dp", None),
        P(("dp", "tensor"), None),
    )
    out_specs = (
        P(("dp", "tensor"), None),
        P(("dp", "tensor"), None),
        P(None, "dp", None, "tensor"),
        P(None, "dp", None),
        P(None, "dp", "tensor"),
        P(None, "dp", "tensor"),
        P(),
        P(None, None, "tensor"),
        P(None, "tensor"),
        P(),
        P(),
        P(None, "tensor"),
        P(None, "tensor"),
        P(None, "tensor"),
        P(None, "tensor"),
    )
    return jax.shard_map(local, mesh=mesh, in_specs=in_specs, out_specs=out_specs, check_vma=False)
```

profile of v0, /device:TPU:0, one launch (start us, length us, event | category | flops | bytes accessed | tf_op | source)
XLA Modules:
  0.0 2292.4 jit_solution(7530033760956396146)
XLA Ops:
  16.3 12.7 all-gather.2
  42.7 82.9 %all-gather.17.cloned.1.call-done = bf16[2048,1024]{1,0:T(8,128)(2,1)} async-done(((bf16[512,1024]{1,0:T(8,128)(2,1)}), bf16[2048,1024]{1,0:T(8,128)(2,1)}) %all-gather.17.cloned.1.call-update) | async-done | bytes 4194320 | tf_op jit(solution)/shard_map/all_gather | solution.py:141
  168.1 104.7 %while.92 = (s32[]{:T(128)}, f32[8,64,128]{2,1,0:T(8,128)S(1)}, s32[]{:T(128)}, f32[8,256,8,64]{1,3,2,0:T(8,128)}, f32[8,8,64,128]{3,2,1,0:T(8,128)S(1)}, /*inde...) while((s32[]{:T(128)}, f32[8,64,128]{2,1,0:T(8,128)S(1)}, ...), condition=%wide.region_5.7_spmd.clone, body=%wide.region_2.6_spmd.clone.sunk | while | flops 909782016 | bytes 5280227 | solution.py:66
  272.9 19.7 copy.164
  325.5 142.7 %reduce-scatter.15.cloned.1.call-done = f32[512,1024]{1,0:T(8,128)} async-done(((f32[2048,1024]{1,0:T(8,128)}), f32[512,1024]{1,0:T(8,128)}) %reduce-scatter.15.cloned.1.call-update) | async-done | bytes 2097168 | tf_op jit(solution)/shard_map/reduce_scatter | solution.py:166
  499.9 82.2 %all-gather.19.cloned.1.call-done = bf16[2048,1024]{1,0:T(8,128)(2,1)} async-done(((bf16[512,1024]{1,0:T(8,128)(2,1)}), bf16[2048,1024]{1,0:T(8,128)(2,1)}) %all-gather.19.cloned.1.call-update) | async-done | bytes 4194320 | tf_op jit(solution)/shard_map/all_gather | solution.py:141
  625.2 110.2 %while.93 = (s32[]{:T(128)}, f32[8,64,128]{2,1,0:T(8,128)S(1)}, s32[]{:T(128)}, f32[8,256,8,64]{1,3,2,0:T(8,128)}, f32[8,8,64,128]{3,2,1,0:T(8,128)}, /*index=5*...) while((s32[]{:T(128)}, f32[8,64,128]{2,1,0:T(8,128)S(1)}, ...), condition=%wide.region_13.15_spmd.clone, body=%wide.region_10.14_spmd.clone.sunk | while | flops 909782016 | bytes 5280735 | solution.py:66
  816.4 195.0 %while.94 = (s32[]{:T(128)}, f32[8,64,128]{2,1,0:T(8,128)S(1)}, f32[8,256,8,64]{1,3,2,0:T(8,128)}, f32[8,256,8]{1,2,0:T(8,128)S(1)}, f32[8,256,8]{1,2,0:T(8,128)...) while((s32[]{:T(128)}, f32[8,64,128]{2,1,0:T(8,128)S(1)}, ...), condition=%wide.region_32.34_spmd.clone, body=%wide.region_19.33_spmd.clone.sunk | while | flops 2126687232 | bytes 15382869 | solution.py:66
  1060.0 146.1 %reduce-scatter.19.cloned.1.call-done = f32[512,1024]{1,0:T(8,128)} async-done(((f32[2048,1024]{1,0:T(8,128)}), f32[512,1024]{1,0:T(8,128)}) %reduce-scatter.19.cloned.1.call-update) | async-done | bytes 2097168 | tf_op jit(solution)/shard_map/reduce_scatter | solution.py:243
  1212.4 81.6 %all-gather.23.cloned.1.call-done = bf16[2048,1024]{1,0:T(8,128)(2,1)} async-done(((bf16[512,1024]{1,0:T(8,128)(2,1)}), bf16[2048,1024]{1,0:T(8,128)(2,1)}) %all-gather.23.cloned.1.call-update) | async-done | bytes 4194320 | tf_op jit(solution)/shard_map/all_gather | solution.py:201
  1341.9 202.1 %while.95 = (s32[]{:T(128)}, f32[8,64,128]{2,1,0:T(8,128)S(1)}, f32[8,256,8,64]{1,3,2,0:T(8,128)}, f32[8,256,8]{1,2,0:T(8,128)S(1)}, f32[8,256,8]{1,2,0:T(8,128)...) while((s32[]{:T(128)}, f32[8,64,128]{2,1,0:T(8,128)S(1)}, ...), condition=%wide.region_51.53_spmd.clone, body=%wide.region_38.52_spmd.clone.sunk | while | flops 2126687232 | bytes 15382869 | solution.py:66
  1559.6 41.4 %reduce-scatter.25.cloned.1.call-done = f32[512,256]{1,0:T(8,128)} async-done(((f32[2048,256]{1,0:T(8,128)}), f32[512,256]{1,0:T(8,128)}) %reduce-scatter.25.cloned.1.call-update) | async-done | bytes 524304 | tf_op jit(solution)/shard_map/reduce_scatter | solution.py:244
  1626.1 14.2 reduce-scatter.33.cloned.1.call-done
  1641.1 38.7 %reduce-scatter.31.cloned.1.call-done = f32[128,256]{1,0:T(8,128)} async-done(((f32[1024,256]{1,0:T(8,128)}), f32[128,256]{1,0:T(8,128)}) %reduce-scatter.31.cloned.1.call-update) | async-done | bytes 131088 | tf_op jit(solution)/shard_map/reduce_scatter | solution.py:258
  1705.8 20.6 multiply_reduce_fusion.15
  1758.2 35.8 %reduce-scatter.41.cloned.1.call-done = f32[128,512]{1,0:T(8,128)} async-done(((f32[1024,512]{1,0:T(8,128)}), f32[128,512]{1,0:T(8,128)}) %reduce-scatter.41.cloned.1.call-update) | async-done | bytes 262160 | tf_op jit(solution)/shard_map/reduce_scatter | solution.py:260
  1794.0 44.7 %reduce-scatter.39.cloned.1.call-done = f32[128,512]{1,0:T(8,128)} async-done(((f32[1024,512]{1,0:T(8,128)}), f32[128,512]{1,0:T(8,128)}) %reduce-scatter.39.cloned.1.call-update) | async-done | bytes 262160 | tf_op jit(solution)/shard_map/reduce_scatter | solution.py:260
  1840.6 35.5 %all-reduce.55.cloned.1.call-done = bf16[2,128,256]{2,1,0:T(8,128)(2,1)} async-done(((bf16[2,128,256]{2,1,0:T(8,128)(2,1)}), bf16[2,128,256]{2,1,0:T(8,128)(2,1)}) %all-reduce.55.cloned.1.call-update) | async-done | bytes 131088 | tf_op jit(solution)/shard_map/psum | solution.py:299
  1877.7 52.9 %reduce-scatter.29.cloned.1.call-done = f32[128,2,512]{2,0,1:T(8,128)} async-done(((f32[1024,2,512]{2,0,1:T(8,128)}), f32[128,2,512]{2,0,1:T(8,128)}) %reduce-scatter.29.cloned.1.call-update) | async-done | bytes 524304 | tf_op jit(solution)/shard_map/reduce_scatter | solution.py:257
  1930.7 54.7 %reduce-scatter.27.cloned.1.call-done = f32[128,2,512]{2,0,1:T(8,128)} async-done(((f32[1024,2,512]{2,0,1:T(8,128)}), f32[128,2,512]{2,0,1:T(8,128)}) %reduce-scatter.27.cloned.1.call-update) | async-done | bytes 524304 | tf_op jit(solution)/shard_map/reduce_scatter | solution.py:257
  1988.5 143.8 %reduce-scatter.23.cloned.1.call-done = f32[512,1024]{1,0:T(8,128)} async-done(((f32[2048,1024]{1,0:T(8,128)}), f32[512,1024]{1,0:T(8,128)}) %reduce-scatter.23.cloned.1.call-update) | async-done | bytes 2097168 | tf_op jit(solution)/shard_map/reduce_scatter | solution.py:243
  2136.4 26.1 %all-reduce.51 = (bf16[2,1024]{1,0:T(2,128)(2,1)S(1)}, f32[2,4,512]{2,1,0:T(4,128)}, f32[2,512]{1,0:T(2,128)}, bf16[2,4,256]{2,1,0:T(4,128)(2,1)S(1)}, bf16[2,25...) all-reduce(f32[2,1024]{1,0:T(2,128)S(1)} %pad_maximum_fusion.11, ...), channel_id=1, replica_groups=mesh['dp'=8,'tensor'=4] {'dp'}, use_global_device_ids=true, to_apply=%region_66.68 | all-reduce | flops 10800 | bytes 77184 | tf_op jit(solution)/shard_map/psum | solution.py:283
  2162.5 13.3 all-reduce.52
  2177.7 103.2 %reduce-scatter.17.cloned.1.call-done = f32[512,1024]{1,0:T(8,128)} async-done(((f32[2048,1024]{1,0:T(8,128)}), f32[512,1024]{1,0:T(8,128)}) %reduce-scatter.17.cloned.1.call-update) | async-done | bytes 2097168 | tf_op jit(solution)/shard_map/reduce_scatter | solution.py:166
  (1398 shorter events, 1038.7 us)
Async XLA Ops:
  7.3 35.4 %all-gather.25.cloned.1.call-start = ((), (), s32[]{:S(2)}) async-start(), calls=%async_computation.33 | async-start | bytes 2359296 | tf_op jit(solution)/shard_map/all_gather | solution.py:104
  9.6 116.0 %all-gather.17.cloned.1.call-start = ((), (), s32[]{:S(2)}) async-start(), calls=%async_computation.14 | async-start | bytes 5242880 | tf_op jit(solution)/shard_map/all_gather | solution.py:141
  15.1 301.4 %all-gather.27.cloned.1.call-start = ((), (), s32[]{:S(2)}) async-start(), calls=%async_computation.34 | async-start | bytes 1179648 | tf_op jit(solution)/shard_map/all_gather | solution.py:107
  15.9 452.3 %reduce-scatter.15.cloned.1.call-start = ((), (), s32[]{:S(2)}) async-start(), calls=%async_computation.15 | async-start | bytes 10485760 | tf_op jit(solution)/shard_map/reduce_scatter | solution.py:166
  37.8 747.8 %copy-start.58 = (f32[1,512]{1,0:T(1,128)}, f32[1,512]{1,0:T(1,128)S(1)}, u32[]{:S(2)}) copy-start(f32[1,512]{1,0:T(1,128)S(1)} %get-tuple-element.1762) | copy-start | bytes 6148
  324.7 175.3 %all-gather.29.cloned.1.call-start = ((), (), s32[]{:S(2)}) async-start(), calls=%async_computation.35 | async-start | bytes 2359296 | tf_op jit(solution)/shard_map/all_gather | solution.py:104
  325.5 256.7 %all-gather.19.cloned.1.call-start = ((), (), s32[]{:S(2)}) async-start(), calls=%async_computation.16 | async-start | bytes 5242880 | tf_op jit(solution)/shard_map/all_gather | solution.py:141
  472.7 293.9 %all-gather.31.cloned.1.call-start = ((), (), s32[]{:S(2)}) async-start(), calls=%async_computation.36 | async-start | bytes 1179648 | tf_op jit(solution)/shard_map/all_gather | solution.py:107
  473.5 293.2 %all-gather.21.cloned.1.call-start = ((), (), s32[]{:S(2)}) async-start(), calls=%async_computation.18 | async-start | bytes 5242880 | tf_op jit(solution)/shard_map/all_gather | solution.py:201
  474.2 585.7 %reduce-scatter.21.cloned.1.call-start = ((), (), s32[]{:S(2)}) async-start(), calls=%async_computation.20 | async-start | bytes 2621440 | tf_op jit(solution)/shard_map/reduce_scatter | solution.py:244
  1017.4 188.7 %reduce-scatter.19.cloned.1.call-start = ((), (), s32[]{:S(2)}) async-start(), calls=%async_computation.19 | async-start | bytes 10485760 | tf_op jit(solution)/shard_map/reduce_scatter | solution.py:243
  1052.8 241.2 %all-gather.23.cloned.1.call-start = ((), (), s32[]{:S(2)}) async-start(), calls=%async_computation.21 | async-start | bytes 5242880 | tf_op jit(solution)/shard_map/all_gather | solution.py:201
  1212.4 388.7 %reduce-scatter.25.cloned.1.call-start = ((), (), s32[]{:S(2)}) async-start(), calls=%async_computation.23 | async-start | bytes 2621440 | tf_op jit(solution)/shard_map/reduce_scatter | solution.py:244
  1558.0 82.2 %reduce-scatter.33.cloned.1.call-start = ((), (), s32[]{:S(2)}) async-start(), calls=%async_computation.27 | async-start | bytes 1179648 | tf_op jit(solution)/shard_map/reduce_scatter | solution.py:258
  1559.6 120.3 %reduce-scatter.31.cloned.1.call-start = ((), (), s32[]{:S(2)}) async-start(), calls=%async_computation.26 | async-start | bytes 1179648 | tf_op jit(solution)/shard_map/reduce_scatter | solution.py:258
  1603.6 153.2 %reduce-scatter.37.cloned.1.call-start = ((), (), s32[]{:S(2)}) async-start(), calls=%async_computation.30 | async-start | bytes 36864 | tf_op jit(solution)/shard_map/reduce_scatter | solution.py:259
  1607.1 149.7 %reduce-scatter.35.cloned.1.call-start = ((), (), s32[]{:S(2)}) async-start(), calls=%async_computation.29 | async-start | bytes 36864 | tf_op jit(solution)/shard_map/reduce_scatter | solution.py:259
  1610.9 183.1 %reduce-scatter.41.cloned.1.call-start = ((), (), s32[]{:S(2)}) async-start(), calls=%async_computation.32 | async-start | bytes 2359296 | tf_op jit(solution)/shard_map/reduce_scatter | solution.py:260
  1618.6 220.1 %reduce-scatter.39.cloned.1.call-start = ((), (), s32[]{:S(2)}) async-start(), calls=%async_computation.31 | async-start | bytes 2359296 | tf_op jit(solution)/shard_map/reduce_scatter | solution.py:260
  1626.0 250.1 %all-reduce.55.cloned.1.call-start = ((), (), s32[]{:S(2)}) async-start(), calls=%async_computation.28 | async-start | bytes 262144 | tf_op jit(solution)/shard_map/psum | solution.py:299
  1681.5 249.2 %reduce-scatter.29.cloned.1.call-start = ((), (), s32[]{:S(2)}) async-start(), calls=%async_computation.25 | async-start | bytes 4718592 | tf_op jit(solution)/shard_map/reduce_scatter | solution.py:257
  1691.3 294.1 %reduce-scatter.27.cloned.1.call-start = ((), (), s32[]{:S(2)}) async-start(), calls=%async_computation.24 | async-start | bytes 4718592 | tf_op jit(solution)/shard_map/reduce_scatter | solution.py:257
  1736.8 395.6 %reduce-scatter.23.cloned.1.call-start = ((), (), s32[]{:S(2)}) async-start(), calls=%async_computation.22 | async-start | bytes 10485760 | tf_op jit(solution)/shard_map/reduce_scatter | solution.py:243
  1746.5 534.3 %reduce-scatter.17.cloned.1.call-start = ((), (), s32[]{:S(2)}) async-start(), calls=%async_computation.17 | async-start | bytes 10485760 | tf_op jit(solution)/shard_map/reduce_scatter | solution.py:166
  (105 other events, 7428.1 us)
Sparse Core Ops, SparseCore 0:
  10.6 32.0 all-gather.24
  44.8 80.7 all-gather.16
  128.1 22.0 all-gather.26
  324.8 143.3 reduce-scatter.14
  470.6 29.3 all-gather.28
  501.4 80.7 all-gather.18
  584.6 22.0 all-gather.30
  608.2 80.7 all-gather.20
  1017.6 42.3 reduce-scatter.20
  1062.3 143.7 reduce-scatter.18
  1212.5 81.4 all-gather.22
  1558.1 42.9 reduce-scatter.24
  1604.8 35.3 reduce-scatter.32
  1643.8 35.9 reduce-scatter.30
  1683.3 31.2 reduce-scatter.36
  1717.7 31.3 reduce-scatter.34
  1752.7 41.1 reduce-scatter.40
  1797.5 41.2 reduce-scatter.38
  1841.6 34.4 all-reduce.54
  1879.7 50.9 reduce-scatter.28
  1934.0 51.3 reduce-scatter.26
  1987.8 144.4 reduce-scatter.22
  2134.8 145.9 reduce-scatter.16
where the time goes:
time: 2300 us; the launch traced here: 2290 us
  waiting for transfers between devices  1120 us (49%)
  matrix products  470 us (20%)
  local copies, waits for them, and re-layouts  273 us (12%)
  other arithmetic  248 us (11%)
  blocking collectives  118 us (5%)
  loops' own time  44.8 us (2%)
    reduce_scatter x2, waiting for transfers between devices, local(): lax.psum_scatter(grad_normed_rows, 'tensor', scatter_dimension=0, tiled=T...  290 us
    reduce_scatter x2, waiting for transfers between devices, local(): lax.psum_scatter(jnp.einsum('ti,di->td', mixed_in, out_weight, preferred_...  246 us
    all_gather x2, waiting for transfers between devices, local(): normalized_rows = lax.all_gather(normed_local, 'tensor', axis=0, tiled=True)  165 us
    dot_general x48, matrix products, advance(): jnp.einsum('hts,shp->thp', layer_parameters, values, precision=highest_pr...  158 us
    reduce_scatter x2, waiting for transfers between devices, local(): lax.psum_scatter(grad_wzx, 'dp', scatter_dimension=0, tiled=True)  108 us
    all_gather x2, waiting for transfers between devices, local(): lax.all_gather(grad.astype(jnp.bfloat16), 'tensor', axis=0, tiled=True)  81.6 us
    reduce_scatter x2, waiting for transfers between devices, local(): lax.psum_scatter(grad_out, 'dp', scatter_dimension=0, tiled=True)  80.6 us
    dot_general x64, matrix products, advance(): jnp.einsum('tn,hpn->thp', reads_out, state, precision=highest_precision)  71.7 us
  transfers between devices with their start and end apart: 23, of which 18 were waited for; matrix products, arithmetic and copies ran while one was open for 21% of the time, Pallas kernels for 0%

commit v1 on v0

v1 whole, which is shorter than its diff:
```python
from functools import partial

import jax
import jax.numpy as jnp
from jax import lax
from jax.experimental import pallas as pl
from jax.experimental.pallas import tpu as pltpu
from jax.sharding import PartitionSpec as P

LAYERS = 2
EPS = 1e-05
HALO = 16
CH = 128
GC = 256
HD = 64
HG = GC // HD
LANES = 128
STATE = 128
NEG = -1e30
VMEM_LIMIT = 60 * 1024 * 1024
MESH = pl.DeviceIdType.MESH
HI = lax.Precision.HIGHEST
F32 = jnp.float32
BF = jnp.bfloat16


def dot_nn(a, b, precision=None):
    return lax.dot_general(a, b, (((1,), (0,)), ((), ())), precision=precision, preferred_element_type=F32)


def dot_nt(a, b):
    return lax.dot_general(a, b, (((1,), (1,)), ((), ())), preferred_element_type=F32)


def dot_tn(a, b):
    return lax.dot_general(a, b, (((0,), (0,)), ((), ())), preferred_element_type=F32)


def sigmoid(v):
    return 0.5 * jnp.tanh(0.5 * v) + 0.5


def twice(v):
    return jnp.concatenate([v, v], axis=1)


def split2(v):
    high = v.astype(BF)
    return jnp.concatenate([high, (v - high.astype(F32)).astype(BF)], axis=1)


def iota2(shape, dim):
    return lax.broadcasted_iota(jnp.int32, shape, dim)


def spread(group):
    row = iota2((2 * LANES, GC), 0) % LANES
    head = iota2((2 * LANES, GC), 1) // HD + group * HG
    return (row == head).astype(F32).astype(BF)


def collect(group):
    head = (iota2((2 * GC, LANES), 0) % GC) // HD + group * HG
    return (head == iota2((2 * GC, LANES), 1)).astype(F32).astype(BF)


def conv(load, keep_ref, weights, tokens):
    total = weights[4:5] + weights[0:1] * load(0)
    for k in range(1, 4):
        total = total + weights[k : k + 1] * (load(k) * twice(keep_ref[k - 1]))
    return total


def conv_back(grad, load, keep_ref, weights, tokens):
    rows = []
    total = None
    for k in range(4):
        part = grad if k == 0 else grad * twice(keep_ref[k - 1])
        rows.append(jnp.sum(part * load(k), axis=0, keepdims=True))
        wide = jnp.concatenate([jnp.zeros((HALO, grad.shape[1]), F32), weights[k : k + 1] * part], axis=0)
        if k:
            wide = pltpu.roll(wide, tokens + HALO - k, 0)
        total = wide if total is None else total + wide
    rows.append(jnp.sum(grad, axis=0, keepdims=True))
    return total, rows


def step_terms(step_in, heads_ref, carried_ref, tail_ref, kept_ref, tokens):
    chunks = tokens // CH
    raw = step_in + heads_ref[0:1]
    steps = jnp.maximum(raw, 0.0) + jnp.log1p(jnp.exp(-jnp.abs(raw)))
    rates = -steps * heads_ref[1:2]
    lower = (iota2((CH, CH), 0) >= iota2((CH, CH), 1)).astype(F32)
    sums, toward, kept = [], [], []
    for c in range(chunks):
        summed = dot_nn(lower, rates[c * CH : (c + 1) * CH], HI)
        last = summed[CH - 1 : CH]
        sums.append(summed)
        toward.append(jnp.exp(last - summed))
        kept.append(jnp.exp(last) * kept_ref[c : c + 1])
    kept.append(jnp.zeros((8 - chunks, LANES), F32))
    summed = jnp.concatenate(sums, axis=0)
    toward = jnp.concatenate(toward, axis=0) * tail_ref[...]
    reach = jnp.exp(summed) * carried_ref[...]
    return raw, steps, rates, summed, toward, reach, jnp.concatenate(kept, axis=0)


def put_sums(summed, col_ref, row_ref, groups, tokens):
    for c in range(tokens // CH):
        turned = summed[c * CH : (c + 1) * CH].T
        for group in range(groups):
            row_ref[group, 0:HG, c * CH : (c + 1) * CH] = turned[group * HG : (group + 1) * HG]
    for group in range(groups):
        shift = (LANES - group * HG) % LANES
        col_ref[group] = pltpu.roll(summed, shift, 1) if shift else summed


def halves(v):
    first = iota2(v.shape, 1) < HD
    return jnp.concatenate([jnp.where(first, v, 0.0), jnp.where(first, 0.0, v)], axis=0).astype(BF)


def forward_kernel(
    dims,
    x_ref, gain_ref, w_ref, wo_ref, wbc_ref, wdt_ref, gp_ref, gpb_ref, csw_ref, heads_ref,
    keep_ref, bias_ref, carried_ref, tail_ref, kept_ref,
    next_ref, normed_ref, gate_ref, val_ref, y_ref, state_ref, shared_ref, step_ref, r_ref,
    nx, inb, inbt, outb, cross, col, row, terms, ke, intra, xs, gs, fresh, fold, incoming, outgoing, branch, squares,
    halo_send, halo_recv, send, recv,
):
    pieces, groups, tokens, skew = dims
    chunks = tokens // CH
    i = pl.program_id(0)
    z = lax.axis_index("tensor")
    right, left = jnp.minimum(z + 1, pieces - 1), jnp.maximum(z - 1, 0)

    def halo_copy():
        return pltpu.make_async_remote_copy(
            src_ref=nx.at[pl.ds(tokens, HALO)], dst_ref=nx.at[pl.ds(0, HALO)],
            send_sem=halo_send, recv_sem=halo_recv, device_id={"tensor": right}, device_id_type=MESH,
        )

    def state_copy(group):
        return pltpu.make_async_remote_copy(
            src_ref=outgoing.at[group], dst_ref=incoming.at[group],
            send_sem=send.at[group], recv_sem=recv.at[group], device_id={"tensor": right}, device_id_type=MESH,
        )

    @pl.when(i == 0)
    def _():
        barrier = pltpu.get_barrier_semaphore()

        @pl.when(z > 0)
        def _():
            pl.semaphore_signal(barrier, inc=1, device_id={"tensor": left}, device_id_type=MESH)

        x = x_ref[...]
        scale = lax.rsqrt(jnp.mean(x * x, axis=1, keepdims=True) + EPS)
        nx[pl.ds(HALO, tokens), :] = (x * scale * gain_ref[...]).astype(BF)

        @pl.when(z < pieces - 1)
        def _():
            pl.semaphore_wait(barrier, 1)
            halo_copy().start()

        @pl.when(z == 0)
        def _():
            nx[pl.ds(0, HALO), :] = jnp.zeros((HALO, nx.shape[1]), BF)
            incoming[...] = jnp.zeros(incoming.shape, BF)

        step_in = dot_nn(nx[pl.ds(HALO, tokens), :], wdt_ref[...])
        step_ref[...] = step_in
        _, steps, _, summed, toward, reach, kept = step_terms(
            step_in, heads_ref, carried_ref, tail_ref, kept_ref, tokens
        )
        put_sums(summed, col, row, groups, tokens)
        terms[0] = split2(steps)
        terms[1] = split2(toward)
        terms[2] = split2(reach)
        kept2 = split2(kept)
        for group in range(groups):
            ke[group] = dot_nn(kept2, spread(group))

        @pl.when(z > 0)
        def _():
            halo_copy().wait_recv()

        shared_ref[...] = dot_nn(nx[...], wbc_ref[...])
        mixed = conv(lambda k: shared_ref[pl.ds(HALO - k, tokens), :], keep_ref, csw_ref[...], tokens)
        maps = mixed * sigmoid(mixed)
        for c in range(chunks):
            part = maps[c * CH : (c + 1) * CH]
            into, out = part[:, :STATE], part[:, STATE:].astype(BF)
            inb[c], outb[c], inbt[c] = into.astype(BF), out, into.T.astype(BF)
            cross[c] = dot_nt(out, into.astype(BF))
        branch[...] = jnp.zeros(branch.shape, F32)
        squares[...] = jnp.zeros(squares.shape, F32)

    @pl.when(i < groups)
    def _():
        depth = nx.shape[1]
        group = i
        slot = lax.rem(group, skew + 1)
        gate_ref[0] = dot_nn(nx[pl.ds(HALO, tokens), :], w_ref[:, 0, 0].reshape(depth, GC))
        val_ref[0] = dot_nn(nx[...], w_ref[:, 0, 1].reshape(depth, GC))
        mixed = conv(lambda k: val_ref[0, pl.ds(HALO - k, tokens), :], keep_ref, gp_ref[0], tokens)
        xs[slot] = mixed * sigmoid(mixed)
        gate = gate_ref[0]
        gs[slot] = gate * sigmoid(gate)
        spreader = spread(group)
        state = jnp.zeros((STATE, GC), F32)
        for c in range(chunks):
            rows = pl.ds(c * CH, CH)
            sized = xs[slot, rows, :] * dot_nn(terms[0, rows, :], spreader)
            weighted = (sized * dot_nn(terms[1, rows, :], spreader)).astype(BF)
            new = dot_nn(inbt[c], weighted)
            fresh[slot, c] = new
            state = ke[group, c : c + 1] * state + new
            for pair in range(HG // 2):
                lanes = pl.ds(pair * LANES, LANES)
                decayed = []
                for j in (2 * pair, 2 * pair + 1):
                    across = col[group, rows, j : j + 1] - row[group, j : j + 1, rows]
                    decayed.append((cross[c] * jnp.exp(jnp.minimum(across, bias_ref[c]))).astype(BF))
                blocks = halves(sized[:, pair * LANES : (pair + 1) * LANES])
                intra[slot, rows, lanes] = dot_nn(jnp.concatenate(decayed, axis=1), blocks)
        fold[slot] = state

    j = i - z

    @pl.when(jnp.logical_and(j >= 0, j < groups))
    def _():
        @pl.when(z > 0)
        def _():
            state_copy(j).wait_recv()

        @pl.when(z < pieces - 1)
        def _():
            total = ke[j, 0:1]
            for c in range(1, chunks):
                total = total * ke[j, c : c + 1]
            outgoing[j] = (total * incoming[j].astype(F32) + fold[lax.rem(j, skew + 1)]).astype(BF)
            state_copy(j).start()

    @pl.when(i >= skew)
    def _():
        group = i - skew
        slot = lax.rem(group, skew + 1)
        depth = nx.shape[1]
        spreader = spread(group)
        gp = gpb_ref[0]
        state = incoming[group].astype(F32)
        for c in range(chunks):
            rows = pl.ds(c * CH, CH)
            low = state.astype(BF)
            state_ref[0, c] = low
            y = intra[slot, rows, :] + dot_nn(outb[c], low) * dot_nn(terms[2, rows, :], spreader)
            y_ref[0, rows, :] = y
            gated = (y + gp[6:7] * xs[slot, rows, :]) * gs[slot, rows, :]
            squares[rows, :] += jnp.sum(gated * gated, axis=1, keepdims=True)
            intra[slot, rows, :] = gated * gp[5:6]
            if c < chunks - 1:
                state = ke[group, c : c + 1] * state + fresh[slot, c]
        branch[...] += dot_nt(intra[slot].astype(BF), wo_ref[:, 0].reshape(depth, GC))

    @pl.when(i == groups + skew - 1)
    def _():
        inner = groups * GC
        factor = lax.rsqrt(squares[...] * (1.0 / inner) + EPS)
        r_ref[...] = factor
        next_ref[...] = x_ref[...] + branch[...] * factor[:, 0:1]
        normed_ref[...] = nx[...]

        @pl.when(z < pieces - 1)
        def _():
            halo_copy().wait_send()
            for group in range(groups):
                state_copy(group).wait_send()


def backward_kernel(
    dims,
    g_ref, x_ref, next_ref, gain_ref, normed_ref, r_ref, w_ref, wo_ref, wbc_ref, wdt_ref, gp_ref, gpb_ref, csw_ref,
    heads_ref, keep_ref, biast_ref, carried_ref, tail_ref, kept_ref,
    gate_ref, val_ref, y_ref, valb_ref, yb_ref, state_ref, shared_ref, step_ref,
    gx_ref, gw_ref, gwo_ref, gbc_ref, gdt_ref, ggp_ref, ggate_ref, gcs_ref, gheads_ref, ggain_ref,
    gb, gbt, nxt, nht, r2, inb, outb, outbt, crosst, col, row, terms, ke,
    dys, xs, fs, dgs, us, fold, incoming, outgoing, gnorm, dct, dbt, dgt, sd, sp, sq, se, dxd, hrecv,
    halo_send, halo_recv, send, recv,
):
    pieces, groups, tokens, skew = dims
    chunks = tokens // CH
    i = pl.program_id(0)
    z = lax.axis_index("tensor")
    right, left = jnp.minimum(z + 1, pieces - 1), jnp.maximum(z - 1, 0)
    back = pieces - 1 - z
    depth = x_ref.shape[1]
    inner = groups * GC

    def halo_copy():
        return pltpu.make_async_remote_copy(
            src_ref=gnorm.at[pl.ds(0, HALO)], dst_ref=hrecv,
            send_sem=halo_send, recv_sem=halo_recv, device_id={"tensor": left}, device_id_type=MESH,
        )

    def state_copy(group):
        return pltpu.make_async_remote_copy(
            src_ref=outgoing.at[group], dst_ref=incoming.at[group],
            send_sem=send.at[group], recv_sem=recv.at[group], device_id={"tensor": left}, device_id_type=MESH,
        )

    def shared_conv():
        return conv(lambda k: shared_ref[pl.ds(HALO - k, tokens), :], keep_ref, csw_ref[...], tokens)

    @pl.when(i == 0)
    def _():
        barrier = pltpu.get_barrier_semaphore()

        @pl.when(z < pieces - 1)
        def _():
            pl.semaphore_signal(barrier, inc=1, device_id={"tensor": right}, device_id_type=MESH)

        @pl.when(z > 0)
        def _():
            pl.semaphore_wait(barrier, 1)

        @pl.when(z == pieces - 1)
        def _():
            incoming[...] = jnp.zeros(incoming.shape, BF)

        low = g_ref[...].astype(BF)
        gb[...] = low
        gbt[...] = low.T
        dots = jnp.sum(low.astype(F32) * (next_ref[...] - x_ref[...]), axis=1, keepdims=True)
        r = r_ref[...]
        r2[...] = r * r * dots * (1.0 / inner)
        nxt[...] = normed_ref[pl.ds(HALO, tokens), :].T
        nht[...] = normed_ref[pl.ds(0, HALO), :].T
        _, steps, _, summed, toward, reach, kept = step_terms(
            step_ref[...], heads_ref, carried_ref, tail_ref, kept_ref, tokens
        )
        put_sums(summed, col, row, groups, tokens)
        terms[0] = split2(steps)
        terms[1] = split2(toward)
        terms[2] = split2(reach)
        kept2 = split2(kept)
        for group in range(groups):
            ke[group] = dot_nn(kept2, spread(group))
        mixed = shared_conv()
        maps = mixed * sigmoid(mixed)
        for c in range(chunks):
            part = maps[c * CH : (c + 1) * CH]
            into, out = part[:, :STATE].astype(BF), part[:, STATE:]
            inb[c], outb[c], outbt[c] = into, out.astype(BF), out.T.astype(BF)
            crosst[c] = dot_nt(into, out.astype(BF))
        for ref in (gnorm, dct, dbt, dgt, sd, sp, sq, se):
            ref[...] = jnp.zeros(ref.shape, F32)

    @pl.when(i < groups)
    def _():
        group = i
        slot = lax.rem(group, skew + 1)
        gp = gp_ref[0]
        mixed = conv(lambda k: val_ref[0, pl.ds(HALO - k, tokens), :], keep_ref, gp, tokens)
        part = sigmoid(mixed)
        x = mixed * part
        xs[slot] = x
        fs[slot] = part + x * (1.0 - part)
        r = twice(r_ref[...])
        gm = dot_nn(gb[...], wo_ref[:, 0].reshape(depth, GC))
        scan = y_ref[0] + gp[6:7] * x
        gate = gate_ref[0]
        part = sigmoid(gate)
        silu = gate * part
        gated = scan * silu
        normal = gated * r
        gwo_ref[:, 0] = dot_nn(gbt[...], (normal * gp[5:6]).astype(BF)).astype(BF).reshape(gwo_ref.shape[0], -1, GC)
        ggated = r * gp[5:6] * gm - gated * twice(r2[...])
        dy = ggated * silu
        dys[slot] = dy
        dgs[slot] = (ggated * scan * (part + silu * (1.0 - part))).astype(BF)
        ggate_ref[0] = jnp.concatenate(
            [
                jnp.sum(gm * normal, axis=0, keepdims=True),
                jnp.sum(dy * x, axis=0, keepdims=True),
                jnp.zeros((6, GC), F32),
            ],
            axis=0,
        )
        spreader = spread(group)
        state = jnp.zeros((STATE, GC), F32)
        for c in reversed(range(chunks)):
            rows = pl.ds(c * CH, CH)
            reached = (dys[slot, rows, :] * dot_nn(terms[2, rows, :], spreader)).astype(BF)
            new = dot_nn(outbt[c], reached)
            us[slot, c] = new
            state = ke[group, c : c + 1] * state + new
        fold[slot] = state

    j = i - back

    @pl.when(jnp.logical_and(j >= 0, j < groups))
    def _():
        @pl.when(z < pieces - 1)
        def _():
            state_copy(j).wait_recv()

        @pl.when(z > 0)
        def _():
            total = ke[j, 0:1]
            for c in range(1, chunks):
                total = total * ke[j, c : c + 1]
            outgoing[j] = (total * incoming[j].astype(F32) + fold[lax.rem(j, skew + 1)]).astype(BF)
            state_copy(j).start()

    @pl.when(i >= skew)
    def _():
        group = i - skew
        slot = lax.rem(group, skew + 1)
        gp = gpb_ref[0]
        spreader, collector = spread(group), collect(group)
        grad = incoming[group].astype(F32)
        ends = [None] * chunks
        for c in reversed(range(chunks)):
            rows = pl.ds(c * CH, CH)
            low = grad.astype(BF)
            state = state_ref[0, c]
            ends[c] = jnp.sum(low.astype(F32) * state.astype(F32), axis=0, keepdims=True) * ke[group, c : c + 1]
            grad = ke[group, c : c + 1] * grad + us[slot, c]
            x = xs[slot, rows, :]
            dy = dys[slot, rows, :]
            steps = dot_nn(terms[0, rows, :], spreader)
            toward = dot_nn(terms[1, rows, :], spreader)
            reached = (dy * dot_nn(terms[2, rows, :], spreader)).astype(BF)
            sized = x * steps
            weighted = (sized * toward).astype(BF)
            later = dot_nn(inb[c], low) * toward
            dbt[c] += dot_nt(weighted, low)
            dct[c] += dot_nt(reached, state)
            parts = []
            cross = crosst[c]
            pairs_total = jnp.zeros((CH, CH), F32)
            for pair in range(HG // 2):
                at = slice(pair * LANES, (pair + 1) * LANES)
                dyp = dy[:, at]
                products = dot_nt(halves(sized[:, at]), dyp.astype(BF))
                decayed = []
                for n in range(2):
                    h = 2 * pair + n
                    across = row[group, h : h + 1, rows] - col[group, rows, h : h + 1]
                    decay = jnp.exp(jnp.minimum(across, biast_ref[c]))
                    decayed.append((cross * decay).astype(BF))
                    pairs_total = pairs_total + products[n * CH : (n + 1) * CH] * decay
                parts.append(dot_nn(jnp.concatenate(decayed, axis=1), halves(dyp)))
            dgt[c] += pairs_total
            within = jnp.concatenate(parts, axis=1)
            whole = within + later
            lowered = dy.astype(BF).astype(F32) * yb_ref[0, rows, :] - sized.astype(BF).astype(F32) * within
            sd[rows, :] += dot_nn(split2(whole * x), collector)
            sp[rows, :] += dot_nn(split2(lowered), collector)
            sq[rows, :] += dot_nn(split2(sized * later), collector)
            dxd[rows, :] = (whole * steps + gp[6:7] * dy) * fs[slot, rows, :]
        ends.append(jnp.zeros((8 - chunks, GC), F32))
        se[...] += dot_nn(split2(jnp.concatenate(ends, axis=0)), collector)
        wide, sums = conv_back(
            dxd[...], lambda k: valb_ref[0, pl.ds(HALO - k, tokens), :], keep_ref, gp, tokens
        )
        ggp_ref[0] = jnp.concatenate(sums + [jnp.zeros((3, GC), F32)], axis=0)
        wide = wide.astype(BF)
        dgate = dgs[slot]
        shape = (gw_ref.shape[0], -1, GC)
        gw_ref[:, 0, 0] = dot_nn(nxt[...], dgate).astype(BF).reshape(shape)
        gw_ref[:, 0, 1] = (dot_nn(nxt[...], wide[HALO:]) + dot_nn(nht[...], wide[:HALO])).astype(BF).reshape(shape)
        gnorm[...] += dot_nt(wide, w_ref[:, 0, 1].reshape(depth, GC))
        gnorm[pl.ds(HALO, tokens), :] += dot_nt(dgate, w_ref[:, 0, 0].reshape(depth, GC))

    @pl.when(i == groups + skew - 1)
    def _():
        upper = (iota2((CH, CH), 0) <= iota2((CH, CH), 1)).astype(F32)
        before = (iota2((CH, CH), 0) > iota2((CH, CH), 1)).astype(F32)
        raw, steps, rates, _, _, _, _ = step_terms(step_ref[...], heads_ref, carried_ref, tail_ref, kept_ref, tokens)
        drates, dmaps = [], []
        for c in range(chunks):
            rows = slice(c * CH, (c + 1) * CH)
            drates.append(dot_nn(upper, sp[rows, :], HI) + dot_nn(before, sq[rows, :], HI) + se[c : c + 1])
            low = dgt[c].astype(BF)
            into = dbt[c] + dot_nn(low, outb[c])
            out = dct[c] + dot_tn(low, inb[c])
            dmaps.append(jnp.concatenate([into, out], axis=1))
        drate = jnp.concatenate(drates, axis=0)
        dstep = (sd[...] - drate * heads_ref[1:2]) * sigmoid(raw)
        gheads_ref[...] = jnp.concatenate(
            [
                jnp.sum(dstep, axis=0, keepdims=True),
                jnp.sum(drate * rates, axis=0, keepdims=True),
                jnp.zeros((6, LANES), F32),
            ],
            axis=0,
        )
        mixed = shared_conv()
        part = sigmoid(mixed)
        dmixed = jnp.concatenate(dmaps, axis=0) * (part + mixed * part * (1.0 - part))
        wide, sums = conv_back(
            dmixed, lambda k: shared_ref[pl.ds(HALO - k, tokens), :], keep_ref, csw_ref[...], tokens
        )
        gcs_ref[...] = jnp.concatenate(sums + [jnp.zeros((3, 2 * STATE), F32)], axis=0)
        wide = wide.astype(BF)
        dstep = dstep.astype(BF)
        gnorm[...] += dot_nt(wide, wbc_ref[...])
        gnorm[pl.ds(HALO, tokens), :] += dot_nt(dstep, wdt_ref[...])

        @pl.when(z > 0)
        def _():
            halo_copy().start()

        gbc_ref[...] = (dot_nn(nxt[...], wide[HALO:]) + dot_nn(nht[...], wide[:HALO])).astype(BF)
        gdt_ref[...] = dot_nn(nxt[...], dstep).astype(BF)

        @pl.when(z < pieces - 1)
        def _():
            halo_copy().wait_recv()
            gnorm[pl.ds(tokens, HALO), :] += hrecv[...]

        x = x_ref[...]
        gn = gnorm[pl.ds(HALO, tokens), :]
        q = lax.rsqrt(jnp.mean(x * x, axis=1, keepdims=True) + EPS)
        gained = gn * gain_ref[...]
        inside = jnp.sum(gained * x, axis=1, keepdims=True) * (1.0 / depth)
        gx_ref[...] = g_ref[...] + q * gained - x * (q * q * q * inside)
        ggain_ref[...] = jnp.concatenate(
            [jnp.sum(gn * x * q, axis=0, keepdims=True), jnp.zeros((7, depth), F32)], axis=0
        )

        @pl.when(z > 0)
        def _():
            halo_copy().wait_send()
            for group in range(groups):
                state_copy(group).wait_send()


def whole(shape):
    return pl.BlockSpec(shape, lambda i: (0,) * len(shape))


def layer_forward(dims, x, gain, w, wo, wbc, wdt, gp, csw, heads, masks):
    pieces, groups, tokens, skew = dims
    keep, bias, _, carried, tail, kept = masks
    chunks = tokens // CH
    depth = x.shape[1]
    dp, _, _, share, wide = w.shape
    per = wide // GC
    ext = tokens + HALO
    last = groups - 1
    slots = skew + 1

    def early(i):
        return jnp.minimum(i, last)

    def late(i):
        return jnp.maximum(i - skew, 0)

    def block(rows, at):
        return pl.BlockSpec((1, rows, GC), lambda i: (at(i), 0, 0))

    return pl.pallas_call(
        partial(forward_kernel, dims),
        grid=(groups + skew,),
        in_specs=[
            whole((tokens, depth)), whole((1, depth)),
            pl.BlockSpec((dp, 1, 2, share, GC), lambda i: (0, early(i) // per, 0, 0, early(i) % per)),
            pl.BlockSpec((dp, 1, share, GC), lambda i: (0, late(i) // per, 0, late(i) % per)),
            whole(wbc.shape), whole(wdt.shape), block(8, early), block(8, late), whole(csw.shape), whole(heads.shape),
            whole(keep.shape), whole(bias.shape), whole(carried.shape), whole(tail.shape), whole(kept.shape),
        ],
        out_specs=[
            whole((tokens, depth)), whole((ext, depth)), block(tokens, early), block(ext, early), block(tokens, late),
            pl.BlockSpec((1, chunks, STATE, GC), lambda i: (late(i), 0, 0, 0)),
            whole((ext, 2 * STATE)), whole((tokens, LANES)), whole((tokens, LANES)),
        ],
        out_shape=[
            jax.ShapeDtypeStruct((tokens, depth), F32),
            jax.ShapeDtypeStruct((ext, depth), BF),
            jax.ShapeDtypeStruct((groups, tokens, GC), F32),
            jax.ShapeDtypeStruct((groups, ext, GC), F32),
            jax.ShapeDtypeStruct((groups, tokens, GC), F32),
            jax.ShapeDtypeStruct((groups, chunks, STATE, GC), BF),
            jax.ShapeDtypeStruct((ext, 2 * STATE), F32),
            jax.ShapeDtypeStruct((tokens, LANES), F32),
            jax.ShapeDtypeStruct((tokens, LANES), F32),
        ],
        scratch_shapes=[
            pltpu.VMEM((ext, depth), BF),
            pltpu.VMEM((chunks, CH, STATE), BF),
            pltpu.VMEM((chunks, STATE, CH), BF),
            pltpu.VMEM((chunks, CH, STATE), BF),
            pltpu.VMEM((chunks, CH, CH), F32),
            pltpu.VMEM((groups, tokens, LANES), F32),
            pltpu.VMEM((groups, 8, tokens), F32),
            pltpu.VMEM((3, tokens, 2 * LANES), BF),
            pltpu.VMEM((groups, 8, GC), F32),
            pltpu.VMEM((slots, tokens, GC), F32),
            pltpu.VMEM((slots, tokens, GC), F32),
            pltpu.VMEM((slots, tokens, GC), F32),
            pltpu.VMEM((slots, chunks, STATE, GC), F32),
            pltpu.VMEM((slots, STATE, GC), F32),
            pltpu.VMEM((groups, STATE, GC), BF),
            pltpu.VMEM((groups, STATE, GC), BF),
            pltpu.VMEM((tokens, depth), F32),
            pltpu.VMEM((tokens, LANES), F32),
            pltpu.SemaphoreType.DMA,
            pltpu.SemaphoreType.DMA,
            pltpu.SemaphoreType.DMA((groups,)),
            pltpu.SemaphoreType.DMA((groups,)),
        ],
        compiler_params=pltpu.CompilerParams(
            collective_id=0, has_side_effects=True, vmem_limit_bytes=VMEM_LIMIT, dimension_semantics=("arbitrary",)
        ),
        name="layer_forward",
    )(x, gain, w, wo, wbc, wdt, gp, gp, csw, heads, keep, bias, carried, tail, kept)


def layer_backward(dims, g, x, after, gain, saved, w, wo, wbc, wdt, gp, csw, heads, masks):
    pieces, groups, tokens, skew = dims
    keep, _, biast, carried, tail, kept = masks
    normed, gate, val, y, states, shared, step_in, r = saved
    chunks = tokens // CH
    depth = x.shape[1]
    dp, pieces_w, _, share, wide = w.shape
    per = wide // GC
    ext = tokens + HALO
    last = groups - 1
    slots = skew + 1

    def early(i):
        return jnp.minimum(i, last)

    def late(i):
        return jnp.maximum(i - skew, 0)

    def block(rows, at):
        return pl.BlockSpec((1, rows, GC), lambda i: (at(i), 0, 0))

    def pair_block(at):
        return pl.BlockSpec((dp, 1, 2, share, GC), lambda i: (0, at(i) // per, 0, 0, at(i) % per))

    def single_block(at):
        return pl.BlockSpec((dp, 1, share, GC), lambda i: (0, at(i) // per, 0, at(i) % per))

    return pl.pallas_call(
        partial(backward_kernel, dims),
        grid=(groups + skew,),
        in_specs=[
            whole((tokens, depth)), whole((tokens, depth)), whole((tokens, depth)), whole((1, depth)),
            whole((ext, depth)), whole((tokens, LANES)), pair_block(late), single_block(early),
            whole(wbc.shape), whole(wdt.shape), block(8, early), block(8, late), whole(csw.shape), whole(heads.shape),
            whole(keep.shape), whole(biast.shape), whole(carried.shape), whole(tail.shape), whole(kept.shape),
            block(tokens, early), block(ext, early), block(tokens, early), block(ext, late), block(tokens, late),
            pl.BlockSpec((1, chunks, STATE, GC), lambda i: (late(i), 0, 0, 0)),
            whole((ext, 2 * STATE)), whole((tokens, LANES)),
        ],
        out_specs=[
            whole((tokens, depth)), pair_block(late), single_block(early),
            whole((depth, 2 * STATE)), whole((depth, LANES)), block(8, late), block(8, early),
            whole((8, 2 * STATE)), whole((8, LANES)), whole((8, depth)),
        ],
        out_shape=[
            jax.ShapeDtypeStruct((tokens, depth), F32),
            jax.ShapeDtypeStruct(w.shape, BF),
            jax.ShapeDtypeStruct(wo.shape, BF),
            jax.ShapeDtypeStruct((depth, 2 * STATE), BF),
            jax.ShapeDtypeStruct((depth, LANES), BF),
            jax.ShapeDtypeStruct((groups, 8, GC), F32),
            jax.ShapeDtypeStruct((groups, 8, GC), F32),
            jax.ShapeDtypeStruct((8, 2 * STATE), F32),
            jax.ShapeDtypeStruct((8, LANES), F32),
            jax.ShapeDtypeStruct((8, depth), F32),
        ],
        scratch_shapes=[
            pltpu.VMEM((tokens, depth), BF),
            pltpu.VMEM((depth, tokens), BF),
            pltpu.VMEM((depth, tokens), BF),
            pltpu.VMEM((depth, HALO), BF),
            pltpu.VMEM((tokens, LANES), F32),
            pltpu.VMEM((chunks, CH, STATE), BF),
            pltpu.VMEM((chunks, CH, STATE), BF),
            pltpu.VMEM((chunks, STATE, CH), BF),
            pltpu.VMEM((chunks, CH, CH), F32),
            pltpu.VMEM((groups, tokens, LANES), F32),
            pltpu.VMEM((groups, 8, tokens), F32),
            pltpu.VMEM((3, tokens, 2 * LANES), BF),
            pltpu.VMEM((groups, 8, GC), F32),
            pltpu.VMEM((slots, tokens, GC), F32),
            pltpu.VMEM((slots, tokens, GC), F32),
            pltpu.VMEM((slots, tokens, GC), F32),
            pltpu.VMEM((slots, tokens, GC), BF),
            pltpu.VMEM((slots, chunks, STATE, GC), F32),
            pltpu.VMEM((slots, STATE, GC), F32),
            pltpu.VMEM((groups, STATE, GC), BF),
            pltpu.VMEM((groups, STATE, GC), BF),
            pltpu.VMEM((ext, depth), F32),
            pltpu.VMEM((chunks, CH, STATE), F32),
            pltpu.VMEM((chunks, CH, STATE), F32),
            pltpu.VMEM((chunks, CH, CH), F32),
            pltpu.VMEM((tokens, LANES), F32),
            pltpu.VMEM((tokens, LANES), F32),
            pltpu.VMEM((tokens, LANES), F32),
            pltpu.VMEM((8, LANES), F32),
            pltpu.VMEM((tokens, GC), F32),
            pltpu.VMEM((HALO, depth), F32),
            pltpu.SemaphoreType.DMA,
            pltpu.SemaphoreType.DMA,
            pltpu.SemaphoreType.DMA((groups,)),
            pltpu.SemaphoreType.DMA((groups,)),
        ],
        compiler_params=pltpu.CompilerParams(
            collective_id=1, has_side_effects=True, vmem_limit_bytes=VMEM_LIMIT, dimension_semantics=("arbitrary",)
        ),
        name="layer_backward",
    )(
        g, x, after, gain, normed, r, w, wo, wbc, wdt, gp, gp, csw, heads, keep, biast, carried, tail, kept,
        gate, val, y, val, y, states, shared, step_in,
    )


def build_masks(starts, tokens, z):
    chunks = tokens // CH
    positions = z * tokens - HALO + lax.iota(jnp.int32, tokens + HALO)
    labels = jnp.sum((positions[:, None] >= starts[None, :]).astype(jnp.int32), axis=1) - 1
    own = labels[HALO:]
    keep = jnp.stack([(labels[HALO - k : HALO - k + tokens] == own).astype(F32) for k in range(1, 4)])
    keep = jnp.broadcast_to(keep[:, :, None], (3, tokens, LANES))
    cut = own.reshape(chunks, CH)
    order = lax.iota(jnp.int32, CH)
    seen = (cut[:, :, None] == cut[:, None, :]) & (order[:, None] >= order[None, :])[None]
    bias = jnp.where(seen, 0.0, NEG).astype(F32)
    before = labels[HALO - 1 :: CH][:chunks]
    final = cut[:, CH - 1]
    carried = (cut == before[:, None]).astype(F32).reshape(tokens, 1)
    tail = (cut == final[:, None]).astype(F32).reshape(tokens, 1)
    kept = jnp.pad((final == before).astype(F32), (0, 8 - chunks))[:, None]
    lanes = lambda v: jnp.broadcast_to(v, (v.shape[0], LANES))
    return keep, bias, jnp.swapaxes(bias, 1, 2), lanes(carried), lanes(tail), lanes(kept)


def local(
    tokens, gate_value_weight, w_bc, w_dt, w_out, norm_gain, conv_value_w, conv_value_b, conv_shared_w, conv_shared_b,
    step_bias, decay_log, skip_gain, gate_gain, starts, cotangent,
):
    pieces, dp = lax.axis_size("tensor"), lax.axis_size("dp")
    z = lax.axis_index("tensor")
    count, depth = tokens.shape
    inner = pieces * conv_value_b.shape[1]
    heads = pieces * step_bias.shape[1]
    groups = inner // GC
    dims = (pieces, groups, count, pieces - 1)
    both = ("dp", "tensor")
    masks = build_masks(starts[0], count, z)

    own = conv_value_b.shape[1]
    few = step_bias.shape[1]
    extra = jnp.concatenate([step_bias, decay_log, jnp.zeros((LAYERS, own - 2 * few), F32)], axis=1)
    pack = jnp.concatenate(
        [
            conv_value_w, conv_value_b[:, None], gate_gain[:, None],
            jnp.repeat(skip_gain, HD, axis=1)[:, None], extra[:, None],
        ],
        axis=1,
    )
    pack = lax.all_gather(pack, "tensor", axis=0)
    extra = pack[:, :, 7]
    heads_in = jnp.stack(
        [
            jnp.swapaxes(extra[:, :, :few], 0, 1).reshape(LAYERS, heads),
            jnp.exp(jnp.swapaxes(extra[:, :, few : 2 * few], 0, 1).reshape(LAYERS, heads)),
        ],
        axis=1,
    )
    heads_in = jnp.pad(heads_in, ((0, 0), (0, 6), (0, LANES - heads)))
    gp = pack.reshape(pieces, LAYERS, 8, own // GC, GC).transpose(1, 0, 3, 2, 4).reshape(LAYERS, groups, 8, GC)
    csw = jnp.pad(jnp.concatenate([conv_shared_w, conv_shared_b[:, None]], axis=1), ((0, 0), (0, 3), (0, 0)))

    params = []
    for layer in range(LAYERS):
        pair = jnp.swapaxes(gate_value_weight[layer], 0, 1)
        pair = lax.all_gather(pair, both, axis=0).reshape((dp, pieces) + pair.shape)
        out = lax.all_gather(w_out[layer], both, axis=0).reshape((dp, pieces) + w_out.shape[1:])
        wbc = lax.all_gather(w_bc[layer], "dp", axis=0, tiled=True)
        wdt = lax.all_gather(w_dt[layer], both, axis=0).reshape((dp, pieces) + w_dt.shape[1:])
        wdt = jnp.pad(wdt.transpose(0, 2, 1, 3).reshape(depth, heads), ((0, 0), (0, LANES - heads)))
        params.append((pair, out, wbc, wdt, gp[layer], csw[layer], heads_in[layer]))

    x = tokens.astype(F32)
    line = [x]
    saved = []
    for layer in range(LAYERS):
        x, *kept = layer_forward(dims, x, norm_gain[layer][None], *params[layer], masks)
        line.append(x)
        saved.append(kept)
    grad = cotangent.astype(F32)
    big, small = [None] * LAYERS, [None] * LAYERS
    for layer in reversed(range(LAYERS)):
        grad, gw, gwo, gbc, gdt, ggp, ggate, gcs, gheads, ggain = layer_backward(
            dims, grad, line[layer], line[layer + 1], norm_gain[layer][None], saved[layer], *params[layer], masks
        )
        gdt = gdt[:, :heads].reshape(dp, depth // dp, pieces, few).transpose(0, 2, 1, 3)

        def scatter(v):
            v = lax.psum_scatter(v, "dp", scatter_dimension=0, tiled=True)
            return lax.psum_scatter(v, "tensor", scatter_dimension=1, tiled=True)[0, 0].astype(F32)

        gbc = lax.psum(lax.psum_scatter(gbc, "dp", scatter_dimension=0, tiled=True), "tensor").astype(F32)
        big[layer] = (jnp.swapaxes(scatter(gw), 0, 1), gbc, scatter(gdt), scatter(gwo))
        rows = jnp.concatenate([ggp[:, :5], ggate[:, :2]], axis=1)
        rows = rows.reshape(pieces, own // GC, 7, GC).transpose(0, 2, 1, 3).reshape(pieces, 7, own)
        small[layer] = (rows, gcs[:5], gheads[:2, :heads], ggain[0])
    small = lax.psum(small, both)

    def stacked(group, member):
        return jnp.stack([group[layer][member] for layer in range(LAYERS)], axis=0)

    rows = lax.dynamic_index_in_dim(stacked(small, 0), z, axis=1, keepdims=False)
    gcs = stacked(small, 1)
    gheads = lax.dynamic_slice_in_dim(stacked(small, 2), z * few, few, axis=2)
    return (
        x.astype(BF), grad, stacked(big, 0), stacked(big, 1), stacked(big, 2), stacked(big, 3), stacked(small, 3),
        rows[:, :4], rows[:, 4], gcs[:, :4], gcs[:, 4], gheads[:, 0], gheads[:, 1],
        jnp.sum(rows[:, 6].reshape(LAYERS, few, HD), axis=2), rows[:, 5],
    )


def solution(mesh):
    in_specs = (
        P(("dp", "tensor"), None),
        P(None, "dp", None, "tensor"),
        P(None, "dp", None),
        P(None, "dp", "tensor"),
        P(None, "dp", "tensor"),
        P(),
        P(None, None, "tensor"),
        P(None, "tensor"),
        P(),
        P(),
        P(None, "tensor"),
        P(None, "tensor"),
        P(None, "tensor"),
        P(None, "tensor"),
        P("dp", None),
        P(("dp", "tensor"), None),
    )
    out_specs = (
        P(("dp", "tensor"), None),
        P(("dp", "tensor"), None),
        P(None, "dp", None, "tensor"),
        P(None, "dp", None),
        P(None, "dp", "tensor"),
        P(None, "dp", "tensor"),
        P(),
        P(None, None, "tensor"),
        P(None, "tensor"),
        P(),
        P(),
        P(None, "tensor"),
        P(None, "tensor"),
        P(None, "tensor"),
        P(None, "tensor"),
    )
    return jax.shard_map(local, mesh=mesh, in_specs=in_specs, out_specs=out_specs, check_vma=False)
```

time: 2300 us -> 1160 us (0.50)
  matrix products: 470 us -> 0 us
  waiting for transfers between devices: 1120 us -> 698 us
  local copies, waits for them, and re-layouts: 273 us -> 37.7 us
  other arithmetic: 248 us -> 15.6 us
  Pallas kernels: 0 us -> 205 us
  blocking collectives: 118 us -> 188 us
  loops' own time: 44.8 us -> 0 us
    dot_general x248 -> x0, matrix products: 470 us -> none  [the longest x48 158 us: advance(): jnp.einsum('hts,shp->thp', layer_parameters, values, precision=highest_pr...]
    reduce_scatter x14 -> x12, waiting for transfers between devices: 826 us -> 480 us  [the longest x6 328 us: scatter(): v = lax.psum_scatter(v, 'dp', scatter_dimension=0, tiled=True)]
    pallas_call x0 -> x4, Pallas kernels: none -> 205 us  [the longest x2 138 us: layer_backward(): pl.pallas_call(partial(backward_kernel, dims), grid=(groups + skew,), in_...]
    all_gather x8 -> x4, waiting for transfers between devices: 257 us -> 69.8 us  [the longest x2 69.7 us: local(): pair = lax.all_gather(pair, both, axis=0).reshape((dp, pieces) + pair.shape)]
    all_gather x4 -> x5, blocking collectives: 41.2 us -> 168 us  [the longest x2 131 us: local(): lax.all_gather(w_dt[layer], both, axis=0)]
    psum x1 -> x2, waiting for transfers between devices: 35.5 us -> 144 us  [the longest x1 129 us: local(): small = lax.psum(small, both)]
    reshape x28 -> x7, local copies, waits for them, and re-layouts: 101 us -> 0.47 us  [the longest x2 0.34 us: local(): wdt.transpose(0, 2, 1, 3).reshape(depth, heads)]
    reduce_sum x45 -> x2, other arithmetic: 79.9 us -> 1.39 us  [the longest x1 0.74 us: build_masks(): jnp.sum((positions[:, None] >= starts[None, :]).astype(jnp.int32), axis=1)]
  transfers between devices with their start and end apart: 23 -> 18, of which waited for: 18 -> 15; matrix products, arithmetic and copies ran while one was open for 21% -> 4% of each run, Pallas kernels for 0% -> 3%
where the time goes in v1:
time: 1160 us
  waiting for transfers between devices  698 us (60%)
  Pallas kernels  205 us (18%)
  blocking collectives  188 us (16%)
  local copies, waits for them, and re-layouts  37.7 us (3%)
  other arithmetic  15.6 us (1%)
  between operations  15 us (1%)
    reduce_scatter x6, waiting for transfers between devices, scatter(): v = lax.psum_scatter(v, 'dp', scatter_dimension=0, tiled=True)  328 us
    pallas_call x2, Pallas kernels, layer_backward(): pl.pallas_call(partial(backward_kernel, dims), grid=(groups + skew,), in_...  138 us
    all_gather x2, blocking collectives, local(): lax.all_gather(w_dt[layer], both, axis=0)  131 us
    psum x1, waiting for transfers between devices, local(): small = lax.psum(small, both)  129 us
    reduce_scatter x4, waiting for transfers between devices, scatter(): lax.psum_scatter(v, 'tensor', scatter_dimension=1, tiled=True)[0, 0]  98.2 us
    all_gather x2, waiting for transfers between devices, local(): pair = lax.all_gather(pair, both, axis=0).reshape((dp, pieces) + pair.shape)  69.7 us
    pallas_call x2, Pallas kernels, layer_forward(): pl.pallas_call(partial(forward_kernel, dims), grid=(groups + skew,), in_s...  67.5 us
    reduce_scatter x2, waiting for transfers between devices, local(): lax.psum_scatter(gbc, 'dp', scatter_dimension=0, tiled=True)  53.9 us
  transfers between devices with their start and end apart: 18, of which 15 were waited for; matrix products, arithmetic and copies ran while one was open for 4% of the time, Pallas kernels for 3%

profile of v1, /device:TPU:0, one launch (start us, length us, event | category | flops | bytes accessed | tf_op | source)
XLA Modules:
  0.0 1160.2 jit_solution(14924673341942654081)
XLA Ops:
  17.9 15.3 %all-gather.2 = f32[8,8,512]{2,1,0:T(8,128)S(1)} all-gather(f32[2,8,512]{2,1,0:T(8,128)S(1)} %concatenate.16), channel_id=4, replica_groups=mesh['dp'=8,'tensor'=4] {'tensor'}, dimensions={0}, use_global_device_ids=true | all-gather | bytes 163840 | tf_op jit(solution)/shard_map/all_gather | solution.py:769
  34.2 66.3 %all_gather.40 = bf16[32,128,8]{1,2,0:T(8,128)(2,1)S(1)} all-gather(bf16[1,128,8]{1,2,0:T(8,128)(2,1)S(1)} %get-tuple-element.213), channel_id=1, replica_groups=mesh['dp'=8,'tensor'=4] {'dp','tensor'}, dimensions={0}, use_global_device_ids=true | all-gather | bytes 67584 | tf_op jit(solution)/shard_map/all_gather | solution.py:788
  102.3 65.1 %all_gather.47 = bf16[32,128,8]{1,2,0:T(8,128)(2,1)S(1)} all-gather(bf16[1,128,8]{1,2,0:T(8,128)(2,1)S(1)} %get-tuple-element.212), channel_id=1, replica_groups=mesh['dp'=8,'tensor'=4] {'dp','tensor'}, dimensions={0}, use_global_device_ids=true | all-gather | bytes 67584 | tf_op jit(solution)/shard_map/all_gather | solution.py:788
  170.9 11.0 all-gather.1
  199.6 33.9 %layer_forward.2 = (f32[512,1024]{1,0:T(8,128)}, bf16[528,1024]{1,0:T(8,128)(2,1)}, f32[8,512,256]{2,1,0:T(8,128)}, f32[8,528,256]{2,1,0:T(8,128)}, f32[8,512,25...) custom-call(f32[512,1024]{1,0:T(8,128)} %convert_element_type.89.x_r, ...), custom_call_target="tpu_custom_call" | custom-call | tf_op jit(solution)/shard_map/layer_forward/pallas_call | solution.py:565
  233.6 69.7 %all-gather.16.cloned.1.call-done = bf16[64,128,512]{2,1,0:T(8,128)(2,1)} async-done(((bf16[2,128,512]{2,1,0:T(8,128)(2,1)}), bf16[64,128,512]{2,1,0:T(8,128)(2,1)}) %all-gather.16.cloned.1.call-update) | async-done | bytes 8388624 | tf_op jit(solution)/shard_map/all_gather | solution.py:785
  303.3 33.6 %layer_forward.3 = (f32[512,1024]{1,0:T(8,128)}, bf16[528,1024]{1,0:T(8,128)(2,1)}, f32[8,512,256]{2,1,0:T(8,128)}, f32[8,528,256]{2,1,0:T(8,128)}, f32[8,512,25...) custom-call(f32[512,1024]{1,0:T(8,128)} %get-tuple-element.53.x_ref., ...), custom_call_target="tpu_custom_call" | custom-call | tf_op jit(solution)/shard_map/layer_forward/pallas_call | solution.py:565
  336.9 72.7 %layer_backward.2 = (f32[512,1024]{1,0:T(8,128)}, bf16[8,4,2,128,512]{4,3,2,1,0:T(8,128)(2,1)}, bf16[8,4,128,512]{3,2,1,0:T(8,128)(2,1)}, bf16[1024,256]{1,0:T(8...) custom-call(f32[512,1024]{1,0:T(8,128)} %convert_element_type.94.g_r, ...), custom_call_target="tpu_custom_call" | custom-call | tf_op jit(solution)/shard_map/layer_backward/pallas_call | solution.py:649
  409.7 64.9 %layer_backward.3 = (f32[512,1024]{1,0:T(8,128)}, bf16[8,4,2,128,512]{4,3,2,1,0:T(8,128)(2,1)}, bf16[8,4,128,512]{3,2,1,0:T(8,128)(2,1)}, bf16[1024,256]{1,0:T(8...) custom-call(f32[512,1024]{1,0:T(8,128)} %get-tuple-element.63.g_ref,, ...), custom_call_target="tpu_custom_call" | custom-call | tf_op jit(solution)/shard_map/layer_backward/pallas_call | solution.py:649
  489.6 16.5 %reduce-scatter.22.cloned.1.call-done = bf16[128,256]{1,0:T(8,128)(2,1)} async-done(((bf16[1024,256]{1,0:T(8,128)(2,1)}), bf16[128,256]{1,0:T(8,128)(2,1)}) %reduce-scatter.22.cloned.1.call-update) | async-done | bytes 65552 | tf_op jit(solution)/shard_map/reduce_scatter | solution.py:811
  506.1 37.4 %reduce-scatter.24.cloned.1.call-done = bf16[128,256]{1,0:T(8,128)(2,1)} async-done(((bf16[1024,256]{1,0:T(8,128)(2,1)}), bf16[128,256]{1,0:T(8,128)(2,1)}) %reduce-scatter.24.cloned.1.call-update) | async-done | bytes 65552 | tf_op jit(solution)/shard_map/reduce_scatter | solution.py:811
  543.6 54.6 %reduce-scatter.30.cloned.1.call-done = bf16[1,4,128,512]{3,2,1,0:T(8,128)(2,1)} async-done(((bf16[8,4,128,512]{3,2,1,0:T(8,128)(2,1)}), bf16[1,4,128,512]{3,2,1,0:T(8,128)(2,1)}) %reduce-scatter.30.cloned.1.call-update) | async-done | bytes 524304 | tf_op jit(solution)/shard_map/reduce_scatter | solution.py:808
  598.3 55.0 %reduce-scatter.34.cloned.1.call-done = bf16[1,4,128,512]{3,2,1,0:T(8,128)(2,1)} async-done(((bf16[8,4,128,512]{3,2,1,0:T(8,128)(2,1)}), bf16[1,4,128,512]{3,2,1,0:T(8,128)(2,1)}) %reduce-scatter.34.cloned.1.call-update) | async-done | bytes 524304 | tf_op jit(solution)/shard_map/reduce_scatter | solution.py:808
  653.4 74.7 %reduce-scatter.14.cloned.1.call-done = bf16[1,4,2,128,512]{4,3,2,1,0:T(8,128)(2,1)} async-done(((bf16[8,4,2,128,512]{4,3,2,1,0:T(8,128)(2,1)}), bf16[1,4,2,128,512]{4,3,2,1,0:T(8,128)(2,1)}) %reduce-scatter.14.cloned.1.call-update) | async-done | bytes 1048592 | tf_op jit(solution)/shard_map/reduce_scatter | solution.py:808
  728.2 75.0 %reduce-scatter.18.cloned.1.call-done = bf16[1,4,2,128,512]{4,3,2,1,0:T(8,128)(2,1)} async-done(((bf16[8,4,2,128,512]{4,3,2,1,0:T(8,128)(2,1)}), bf16[1,4,2,128,512]{4,3,2,1,0:T(8,128)(2,1)}) %reduce-scatter.18.cloned.1.call-update) | async-done | bytes 1048592 | tf_op jit(solution)/shard_map/reduce_scatter | solution.py:808
  804.9 128.8 %all-reduce.13.cloned.1.call-done = (f32[1,1024]{1,0:T(1,128)}, f32[1,1024]{1,0:T(1,128)}, f32[1,4,7,512]{3,1,2,0:T(4,128)}, f32[1,4,7,512]{3,1,2,0:T(4,128)}, f...) async-done(((f32[1,1024]{1,0:T(1,128)}, f32[1,1024]{1,0:T(1,128)}, f32[1,4,7,512]{3,1,2,0:T(4,128)}, ...) | async-done | bytes 133648 | tf_op jit(solution)/shard_map/psum | solution.py:816
  941.8 31.7 %reduce-scatter.26.cloned.1.call-done = bf16[1,4,128,8]{2,3,1,0:T(8,128)(2,1)} async-done(((bf16[8,4,128,8]{2,3,1,0:T(8,128)(2,1)}), bf16[1,4,128,8]{2,3,1,0:T(8,128)(2,1)}) %reduce-scatter.26.cloned.1.call-update) | async-done | bytes 8208 | tf_op jit(solution)/shard_map/reduce_scatter | solution.py:808
  973.4 37.1 %reduce-scatter.28.cloned.1.call-done = bf16[1,4,128,8]{2,3,1,0:T(8,128)(2,1)} async-done(((bf16[8,4,128,8]{2,3,1,0:T(8,128)(2,1)}), bf16[1,4,128,8]{2,3,1,0:T(8,128)(2,1)}) %reduce-scatter.28.cloned.1.call-update) | async-done | bytes 8208 | tf_op jit(solution)/shard_map/reduce_scatter | solution.py:808
  1010.5 19.4 %all-reduce.8 = (bf16[1,4,128,8]{2,3,1,0:T(8,128)(2,1)S(1)}, bf16[1,4,128,8]{2,3,0,1:T(8,128)(2,1)S(1)}) all-reduce(bf16[1,4,128,8]{2,3,1,0:T(8,128)(2,1)} %reduce-scatter.28.cloned.1.call-done, bf16[1,4,128,8]{2,3,0,1:T(8,128)(2,1)} %bitcast.210), channel_id=16, replica_groups=mesh['dp'=8,'tensor'=4] {'tensor'}, use_global_device_ids=true, to_apply=%region_12.13.clone | all-reduce | flops 8192 | bytes 32768
  1031.9 15.5 %all-reduce.15.cloned.1.call-done = (bf16[1,128,256]{2,1,0:T(8,128)(2,1)}, bf16[1,128,256]{2,1,0:T(8,128)(2,1)}) async-done(((bf16[1,128,256]{2,1,0:T(8,128)(2,1)}, bf16[1,128,256]{2,1,0:T(8,128)(2,1)}), (bf16[1,128,256]{2,1,0:T(8,128)(2,1)}, bf16[1,128,256]{2,1,0:T(8,128)(2,1)})) %all-reduce.15.cloned.1.call-update) | async-done | bytes 131088 | tf_op jit(solution)/shard_map/psum | solution.py:811
  1049.0 22.0 %reduce-scatter.32.cloned.1.call-done = bf16[1,1,128,512]{3,2,1,0:T(8,128)(2,1)} async-done(((bf16[1,4,128,512]{3,2,1,0:T(8,128)(2,1)}), bf16[1,1,128,512]{3,2,1,0:T(8,128)(2,1)}) %reduce-scatter.32.cloned.1.call-update) | async-done | bytes 131088 | tf_op jit(solution)/shard_map/reduce_scatter | solution.py:809
  1071.0 22.2 %reduce-scatter.36.cloned.1.call-done = bf16[1,1,128,512]{3,2,1,0:T(8,128)(2,1)} async-done(((bf16[1,4,128,512]{3,2,1,0:T(8,128)(2,1)}), bf16[1,1,128,512]{3,2,1,0:T(8,128)(2,1)}) %reduce-scatter.36.cloned.1.call-update) | async-done | bytes 131088 | tf_op jit(solution)/shard_map/reduce_scatter | solution.py:809
  1095.0 26.0 %reduce-scatter.16.cloned.1.call-done = bf16[1,1,2,128,512]{4,3,2,1,0:T(8,128)(2,1)} async-done(((bf16[1,4,2,128,512]{4,3,2,1,0:T(8,128)(2,1)}), bf16[1,1,2,128,512]{4,3,2,1,0:T(8,128)(2,1)}) %reduce-scatter.16.cloned.1.call-update) | async-done | bytes 262160 | tf_op jit(solution)/shard_map/reduce_scatter | solution.py:809
  1121.0 28.0 %reduce-scatter.20.cloned.1.call-done = bf16[1,1,2,128,512]{4,3,2,1,0:T(8,128)(2,1)} async-done(((bf16[1,4,2,128,512]{4,3,2,1,0:T(8,128)(2,1)}), bf16[1,1,2,128,512]{4,3,2,1,0:T(8,128)(2,1)}) %reduce-scatter.20.cloned.1.call-update) | async-done | bytes 262160 | tf_op jit(solution)/shard_map/reduce_scatter | solution.py:809
  (172 shorter events, 68.7 us)
Async XLA Ops:
  7.2 93.5 %copy-start.13 = (f32[2,256]{1,0:T(2,128)S(1)}, f32[2,256]{1,0:T(2,128)}, u32[]{:S(2)}) copy-start(f32[2,256]{1,0:T(2,128)} %param.25) | copy-start | bytes 6148
  7.2 93.5 %copy-start.2 = (bf16[512,1024]{1,0:T(8,128)(2,1)S(1)}, bf16[512,1024]{1,0:T(8,128)(2,1)}, u32[]{:S(2)}) copy-start(bf16[512,1024]{1,0:T(8,128)(2,1)} %param.16) | copy-start | bytes 3145732
  7.2 189.0 %all-gather.10.cloned.1.call-start = ((), (), s32[]{:S(2)}) async-start(), calls=%async_computation.12 | async-start | bytes 4325376 | tf_op jit(solution)/shard_map/all_gather | solution.py:786
  9.0 187.1 %all-gather.14.cloned.1.call-start = ((), (), s32[]{:S(2)}) async-start(), calls=%async_computation.26 | async-start | bytes 8650752 | tf_op jit(solution)/shard_map/all_gather | solution.py:785
  10.5 158.7 %copy-start.3 = (bf16[512,1024]{1,0:T(8,128)(2,1)S(1)}, bf16[512,1024]{1,0:T(8,128)(2,1)}, u32[]{:S(2)}) copy-start(bf16[512,1024]{1,0:T(8,128)(2,1)} %param.31) | copy-start | bytes 3145732
  11.3 222.3 %all-gather.12.cloned.1.call-start = ((), (), s32[]{:S(2)}) async-start(), calls=%async_computation.13 | async-start | bytes 4325376 | tf_op jit(solution)/shard_map/all_gather | solution.py:786
  12.0 291.3 %all-gather.16.cloned.1.call-start = ((), (), s32[]{:S(2)}) async-start(), calls=%async_computation.27 | async-start | bytes 8650752 | tf_op jit(solution)/shard_map/all_gather | solution.py:785
  12.8 493.3 %reduce-scatter.22.cloned.1.call-start = ((), (), s32[]{:S(2)}) async-start(), calls=%async_computation.18 | async-start | bytes 589824 | tf_op jit(solution)/shard_map/reduce_scatter | solution.py:811
  474.6 68.9 %reduce-scatter.24.cloned.1.call-start = ((), (), s32[]{:S(2)}) async-start(), calls=%async_computation.19 | async-start | bytes 589824 | tf_op jit(solution)/shard_map/reduce_scatter | solution.py:811
  475.2 123.0 %reduce-scatter.30.cloned.1.call-start = ((), (), s32[]{:S(2)}) async-start(), calls=%async_computation.22 | async-start | bytes 4718592 | tf_op jit(solution)/shard_map/reduce_scatter | solution.py:808
  476.0 177.4 %reduce-scatter.34.cloned.1.call-start = ((), (), s32[]{:S(2)}) async-start(), calls=%async_computation.24 | async-start | bytes 4718592 | tf_op jit(solution)/shard_map/reduce_scatter | solution.py:808
  476.7 251.4 %reduce-scatter.14.cloned.1.call-start = ((), (), s32[]{:S(2)}) async-start(), calls=%async_computation.14 | async-start | bytes 9437184 | tf_op jit(solution)/shard_map/reduce_scatter | solution.py:808
  477.4 325.7 %reduce-scatter.18.cloned.1.call-start = ((), (), s32[]{:S(2)}) async-start(), calls=%async_computation.16 | async-start | bytes 9437184 | tf_op jit(solution)/shard_map/reduce_scatter | solution.py:808
  478.0 325.1 %copy-start.14 = (u32[32]{0:T(128)S(1)}, u32[32]{0:T(128)}, u32[]{:S(2)}) copy-start(u32[32]{0:T(128)} %constant.46) | copy-start | bytes 388
  478.0 325.7 %copy-start = (f32[512,1024]{1,0:T(8,128)S(1)}, f32[512,1024]{1,0:T(8,128)}, u32[]{:S(2)}) copy-start(f32[512,1024]{1,0:T(8,128)} %get-tuple-element.54.next_ref) | copy-start | bytes 6291460
  478.1 455.7 %all-reduce.13.cloned.1.call-start = ((), (), s32[]{:S(2)}) async-start(), calls=%async_computation.28 | async-start | bytes 282624 | tf_op jit(solution)/shard_map/psum | solution.py:816
  487.8 485.6 %reduce-scatter.26.cloned.1.call-start = ((), (), s32[]{:S(2)}) async-start(), calls=%async_computation.20 | async-start | bytes 73728 | tf_op jit(solution)/shard_map/reduce_scatter | solution.py:808
  488.7 521.8 %reduce-scatter.28.cloned.1.call-start = ((), (), s32[]{:S(2)}) async-start(), calls=%async_computation.21 | async-start | bytes 73728 | tf_op jit(solution)/shard_map/reduce_scatter | solution.py:808
  489.6 557.9 %all-reduce.15.cloned.1.call-start = ((), (), s32[]{:S(2)}) async-start(), calls=%async_computation.29 | async-start | bytes 262144 | tf_op jit(solution)/shard_map/psum | solution.py:811
  543.6 527.5 %reduce-scatter.32.cloned.1.call-start = ((), (), s32[]{:S(2)}) async-start(), calls=%async_computation.23 | async-start | bytes 655360 | tf_op jit(solution)/shard_map/reduce_scatter | solution.py:809
  598.3 495.0 %reduce-scatter.36.cloned.1.call-start = ((), (), s32[]{:S(2)}) async-start(), calls=%async_computation.25 | async-start | bytes 655360 | tf_op jit(solution)/shard_map/reduce_scatter | solution.py:809
  653.4 467.6 %reduce-scatter.16.cloned.1.call-start = ((), (), s32[]{:S(2)}) async-start(), calls=%async_computation.15 | async-start | bytes 1310720 | tf_op jit(solution)/shard_map/reduce_scatter | solution.py:809
  728.1 420.9 %reduce-scatter.20.cloned.1.call-start = ((), (), s32[]{:S(2)}) async-start(), calls=%async_computation.17 | async-start | bytes 1310720 | tf_op jit(solution)/shard_map/reduce_scatter | solution.py:809
  804.9 347.0 %copy-start.1 = (f32[512,1024]{1,0:T(8,128)S(1)}, f32[512,1024]{1,0:T(8,128)}, u32[]{:S(2)}) copy-start(f32[512,1024]{1,0:T(8,128)} %get-tuple-element.241) | copy-start | bytes 6291460
  (9 other events, 278.5 us)
Sparse Core Ops, SparseCore 0:
  11.6 65.1 all-gather.9
  80.3 76.0 all-gather.13
  159.5 61.8 all-gather.11
  224.1 79.1 all-gather.15
  474.8 31.3 reduce-scatter.21
  509.4 34.1 reduce-scatter.23
  546.9 51.3 reduce-scatter.29
  602.0 51.3 reduce-scatter.33
  656.8 71.2 reduce-scatter.13
  731.8 71.2 reduce-scatter.17
  810.7 122.9 all-reduce.12
  937.1 36.2 reduce-scatter.25
  977.3 33.2 reduce-scatter.27
  1012.8 34.6 all-reduce.14
  1049.6 21.3 reduce-scatter.31
  1073.2 19.9 reduce-scatter.35
  1095.5 25.4 reduce-scatter.15
  1123.1 25.7 reduce-scatter.19

commit v2 on v1

v2 whole, which is shorter than its diff:
```python
from functools import partial

import jax
import jax.numpy as jnp
from jax import lax
from jax.experimental import pallas as pl
from jax.experimental.pallas import tpu as pltpu
from jax.sharding import PartitionSpec as P

LAYERS = 2
EPS = 1e-05
HALO = 16
CH = 128
GC = 256
HD = 64
HG = GC // HD
LANES = 128
STATE = 128
NEG = -1e30
SLOTS = 2
VMEM_LIMIT = 58 * 1024 * 1024
VMEM_LIMIT_FORWARD = 62 * 1024 * 1024
STEP_US = 3.2
TICK = 1.3
MESH = pl.DeviceIdType.MESH
HI = lax.Precision.HIGHEST
F32 = jnp.float32
BF = jnp.bfloat16


def dot_nn(a, b, precision=None):
    return lax.dot_general(a, b, (((1,), (0,)), ((), ())), precision=precision, preferred_element_type=F32)


def dot_nt(a, b):
    return lax.dot_general(a, b, (((1,), (1,)), ((), ())), preferred_element_type=F32)


def dot_tn(a, b):
    return lax.dot_general(a, b, (((0,), (0,)), ((), ())), preferred_element_type=F32)


def sigmoid(v):
    return 0.5 * jnp.tanh(0.5 * v) + 0.5


def twice(v):
    return jnp.concatenate([v, v], axis=1)


def split2(v):
    high = v.astype(BF)
    return jnp.concatenate([high, (v - high.astype(F32)).astype(BF)], axis=1)


def iota2(shape, dim):
    return lax.broadcasted_iota(jnp.int32, shape, dim)


def spread(group):
    row = iota2((2 * LANES, GC), 0) % LANES
    head = iota2((2 * LANES, GC), 1) // HD + group * HG
    return (row == head).astype(F32).astype(BF)


def collect(group):
    head = (iota2((2 * GC, LANES), 0) % GC) // HD + group * HG
    return (head == iota2((2 * GC, LANES), 1)).astype(F32).astype(BF)


def conv(load, keep_ref, weights, tokens):
    total = weights[4:5] + weights[0:1] * load(0)
    for k in range(1, 4):
        total = total + weights[k : k + 1] * (load(k) * twice(keep_ref[k - 1]))
    return total


def conv_back(grad, load, keep_ref, weights, tokens):
    rows = []
    total = None
    for k in range(4):
        part = grad if k == 0 else grad * twice(keep_ref[k - 1])
        rows.append(jnp.sum(part * load(k), axis=0, keepdims=True))
        wide = jnp.concatenate([jnp.zeros((HALO, grad.shape[1]), F32), weights[k : k + 1] * part], axis=0)
        if k:
            wide = pltpu.roll(wide, tokens + HALO - k, 0)
        total = wide if total is None else total + wide
    rows.append(jnp.sum(grad, axis=0, keepdims=True))
    return total, rows


def step_terms(step_in, heads_ref, carried_ref, tail_ref, kept_ref, tokens):
    chunks = tokens // CH
    raw = step_in + heads_ref[0:1]
    steps = jnp.maximum(raw, 0.0) + jnp.log1p(jnp.exp(-jnp.abs(raw)))
    rates = -steps * heads_ref[1:2]
    lower = (iota2((CH, CH), 0) >= iota2((CH, CH), 1)).astype(F32)
    sums, toward, kept = [], [], []
    for c in range(chunks):
        summed = dot_nn(lower, rates[c * CH : (c + 1) * CH], HI)
        last = summed[CH - 1 : CH]
        sums.append(summed)
        toward.append(jnp.exp(last - summed))
        kept.append(jnp.exp(last) * kept_ref[c : c + 1])
    kept.append(jnp.zeros((8 - chunks, LANES), F32))
    summed = jnp.concatenate(sums, axis=0)
    toward = jnp.concatenate(toward, axis=0) * tail_ref[...]
    reach = jnp.exp(summed) * carried_ref[...]
    return raw, steps, rates, summed, toward, reach, jnp.concatenate(kept, axis=0)


def put_sums(summed, col_ref, row_ref, groups, tokens):
    for c in range(tokens // CH):
        turned = summed[c * CH : (c + 1) * CH].T
        for group in range(groups):
            row_ref[group, 0:HG, c * CH : (c + 1) * CH] = turned[group * HG : (group + 1) * HG]
    col_ref[0] = summed


def turn_sums(col_ref, group):
    col_ref[1] = pltpu.roll(col_ref[0], lax.rem(LANES - group * HG, LANES), 1)


def put_heads(rows_ref, heads_ref):
    total = rows_ref[0, 0, 7:8, :]
    for k in range(1, rows_ref.shape[0]):
        total = total + rows_ref[k, 0, 7:8, :]
    heads_ref[...] = jnp.concatenate(
        [total[:, :LANES], jnp.exp(total[:, LANES:]), jnp.zeros((6, LANES), F32)], axis=0
    )


def shared_taps(csw_ref, csb_ref, layer):
    return jnp.concatenate([csw_ref[layer], csb_ref[layer : layer + 1]], axis=0)


def halves(v):
    first = iota2(v.shape, 1) < HD
    return jnp.concatenate([jnp.where(first, v, 0.0), jnp.where(first, 0.0, v)], axis=0).astype(BF)


def forward_kernel(
    dims,
    x_ref, gain_ref, wa, wb, oa, ob, few_ref, pa, pb, qa, qb, rows_ref, csw_ref, csb_ref,
    keep_ref, bias_ref, carried_ref, tail_ref, kept_ref, *rest,
):
    pieces, groups, tokens, skew, bits, layer, gathers = dims
    if gathers:
        few_mine, mine_ref, *rest = rest
    next_ref, nxt_ref, nht_ref, gate_ref, val_ref, y_ref, state_ref, shared_ref, step_ref, r_ref, *rest = rest
    if gathers:
        few_out, wall_ref, *rest = rest
    nx, inb, inbt, outb, cross, col, row, terms, ke, intra, xs, gs, fresh, fold, *rest = rest
    incoming, outgoing, branch, squares, heads_ref, halo_send, halo_recv, send, recv, *rest = rest
    if gathers:
        few_z, few_all, *rest = rest
    place = Place(bits)
    chunks = tokens // CH
    i = pl.program_id(0)
    z = lax.axis_index("tensor")
    right, left = jnp.minimum(z + 1, pieces - 1), jnp.maximum(z - 1, 0)

    def halo_copy():
        return pltpu.make_async_remote_copy(
            src_ref=nx.at[pl.ds(tokens, HALO)], dst_ref=nx.at[pl.ds(0, HALO)],
            send_sem=halo_send, recv_sem=halo_recv, device_id={"tensor": right}, device_id_type=MESH,
        )

    def state_copy(group):
        return pltpu.make_async_remote_copy(
            src_ref=outgoing.at[group], dst_ref=incoming.at[group],
            send_sem=send.at[group], recv_sem=recv.at[group], device_id={"tensor": right}, device_id_type=MESH,
        )

    gather = Gather(place, z, pieces, mine_ref, wall_ref, few_mine, few_z, few_all, *rest) if gathers else None
    steps_all = groups + skew
    plan = [[] for _ in range(steps_all)]
    if gathers:
        for when, act in gather.events():
            plan[min(int((when * TICK + 3.0) / STEP_US), steps_all - 1)].append(act)

    @pl.when(i == 0)
    def _():
        greet(place, z, pieces)
        x = x_ref[...]
        scale = lax.rsqrt(jnp.mean(x * x, axis=1, keepdims=True) + EPS)
        nx[pl.ds(HALO, tokens), :] = (x * scale * gain_ref[layer : layer + 1]).astype(BF)
        put_heads(rows_ref, heads_ref)

        @pl.when(z < pieces - 1)
        def _():
            halo_copy().start()

        if gathers:
            gather.start()

        @pl.when(z == 0)
        def _():
            nx[pl.ds(0, HALO), :] = jnp.zeros((HALO, nx.shape[1]), BF)
            incoming[...] = jnp.zeros(incoming.shape, BF)

        depth = nx.shape[1]
        step_in = dot_nn(nx[pl.ds(HALO, tokens), :], few_ref[:, :, 2 * STATE :].reshape(depth, LANES))
        step_ref[...] = step_in
        _, steps, _, summed, toward, reach, kept = step_terms(
            step_in, heads_ref, carried_ref, tail_ref, kept_ref, tokens
        )
        put_sums(summed, col, row, groups, tokens)
        terms[0] = split2(steps)
        terms[1] = split2(toward)
        terms[2] = split2(reach)
        kept2 = split2(kept)
        for group in range(groups):
            ke[group] = dot_nn(kept2, spread(group))

        @pl.when(z > 0)
        def _():
            halo_copy().wait_recv()

        shared_ref[...] = dot_nn(nx[...], few_ref[:, :, : 2 * STATE].reshape(depth, 2 * STATE))
        taps = shared_taps(csw_ref, csb_ref, layer)
        mixed = conv(lambda k: shared_ref[pl.ds(HALO - k, tokens), :], keep_ref, taps, tokens)
        maps = mixed * sigmoid(mixed)
        for c in range(chunks):
            part = maps[c * CH : (c + 1) * CH]
            into, out = part[:, :STATE], part[:, STATE:].astype(BF)
            inb[c], outb[c], inbt[c] = into.astype(BF), out, into.T.astype(BF)
            cross[c] = dot_nt(out, into.astype(BF))
        branch[...] = jnp.zeros(branch.shape, F32)
        squares[...] = jnp.zeros(squares.shape, F32)

    @pl.when(i < groups)
    def _():
        depth = nx.shape[1]
        group = i
        slot = lax.rem(group, skew + 1)
        gate_ref[0] = dot_nn(nx[pl.ds(HALO, tokens), :], side((wa, wb), 0))
        val_ref[0] = dot_nn(nx[...], side((wa, wb), 1))
        mixed = conv(lambda k: val_ref[0, pl.ds(HALO - k, tokens), :], keep_ref, side_params((pa, pb)), tokens)
        xs[slot] = mixed * sigmoid(mixed)
        gate = gate_ref[0]
        gs[slot] = gate * sigmoid(gate)
        turn_sums(col, group)
        spreader = spread(group)
        state = jnp.zeros((STATE, GC), F32)
        for c in range(chunks):
            rows = pl.ds(c * CH, CH)
            sized = xs[slot, rows, :] * dot_nn(terms[0, rows, :], spreader)
            weighted = (sized * dot_nn(terms[1, rows, :], spreader)).astype(BF)
            new = dot_nn(inbt[c], weighted)
            fresh[slot, c] = new
            state = ke[group, c : c + 1] * state + new
            for pair in range(HG // 2):
                lanes = pl.ds(pair * LANES, LANES)
                decayed = []
                for j in (2 * pair, 2 * pair + 1):
                    across = col[1, rows, j : j + 1] - row[group, j : j + 1, rows]
                    decayed.append((cross[c] * jnp.exp(jnp.minimum(across, bias_ref[c]))).astype(BF))
                blocks = halves(sized[:, pair * LANES : (pair + 1) * LANES])
                intra[slot, rows, lanes] = dot_nn(jnp.concatenate(decayed, axis=1), blocks)
        fold[slot] = state

    j = i - z

    @pl.when(jnp.logical_and(j >= 0, j < groups))
    def _():
        @pl.when(z > 0)
        def _():
            state_copy(j).wait_recv()

        @pl.when(z < pieces - 1)
        def _():
            total = ke[j, 0:1]
            for c in range(1, chunks):
                total = total * ke[j, c : c + 1]
            outgoing[j] = (total * incoming[j].astype(F32) + fold[lax.rem(j, skew + 1)]).astype(BF)
            state_copy(j).start()

    @pl.when(i >= skew)
    def _():
        group = i - skew
        slot = lax.rem(group, skew + 1)
        depth = nx.shape[1]
        spreader = spread(group)
        gp = side_params((qa, qb))
        state = incoming[group].astype(F32)
        for c in range(chunks):
            rows = pl.ds(c * CH, CH)
            low = state.astype(BF)
            state_ref[0, c] = low
            y = intra[slot, rows, :] + dot_nn(outb[c], low) * dot_nn(terms[2, rows, :], spreader)
            y_ref[0, rows, :] = y
            gated = (y + gp[6:7] * xs[slot, rows, :]) * gs[slot, rows, :]
            squares[rows, :] += jnp.sum(gated * gated, axis=1, keepdims=True)
            intra[slot, rows, :] = gated * gp[5:6]
            if c < chunks - 1:
                state = ke[group, c : c + 1] * state + fresh[slot, c]
        branch[...] += dot_nt(intra[slot].astype(BF), side((oa, ob), 0))

    for step, acts in enumerate(plan):
        if acts:

            @pl.when(i == step)
            def _(acts=acts):
                for act in acts:
                    act()

    @pl.when(i == groups + skew - 1)
    def _():
        inner = groups * GC
        factor = lax.rsqrt(squares[...] * (1.0 / inner) + EPS)
        r_ref[...] = factor
        next_ref[...] = x_ref[...] + branch[...] * factor[:, 0:1]
        nxt_ref[...] = nx[pl.ds(HALO, tokens), :].T
        nht_ref[...] = nx[pl.ds(0, HALO), :].T
        if gathers:
            gather.finish()
            few_out[...] = few_all[...]

        @pl.when(z < pieces - 1)
        def _():
            halo_copy().wait_send()
            for group in range(groups):
                state_copy(group).wait_send()


class Place:
    def __init__(self, bits):
        self.bits = bits
        self.index = lax.axis_index("dp")
        self.bit = [lax.rem(self.index // (1 << b), 2) for b in range(bits)]
        self.dims = (2,) * bits
        self.all = (slice(None),) * bits

    def flip(self, b):
        return self.index + (1 << b) * (1 - 2 * self.bit[b])

    def along(self, done):
        return tuple(slice(None) if b in done else self.bit[b] for b in reversed(range(self.bits)))

    def order(self, odd):
        rest = list(range(1, self.bits))
        return [0] + (rest[::-1] if odd else rest)

    def partner(self, odd, step):
        return self.flip(self.order(odd)[step])

    def region(self, odd, step, keep):
        order = self.order(odd)
        at = []
        for b in reversed(range(self.bits)):
            if b in order[:step]:
                at.append(self.bit[b])
            elif b == order[step]:
                at.append(self.bit[b] if keep else 1 - self.bit[b])
            else:
                at.append(slice(None))
        return tuple(at)

    def mine(self):
        return tuple(self.bit[b] for b in reversed(range(self.bits)))


def backward_kernel(
    dims,
    g_ref, x_ref, next_ref, gain_ref, nxt, nht, r_ref, wa, wb, oa, ob, few_ref, pa, pb, qa, qb, rows_ref,
    csw_ref, csb_ref, keep_ref, biast_ref, carried_ref, tail_ref, kept_ref,
    gate_ref, val_ref, y_ref, valb_ref, yb_ref, state_ref, shared_ref, step_ref,
    gx_ref, gw_ref, gm_ref, small_ref,
    gb, gbt, r2, inb, outb, outbt, crosst, col, row, terms, ke,
    dys, xs, fs, dgs, fold, incoming, outgoing, gnorm, dct, dbt, dgt, sd, sp, sq, se, dxd, hrecv,
    own, own_m, got_z, got_m, halo_send, halo_recv, send, recv, sum_send, sum_recv, z_send, z_recv,
    msum_send, msum_recv, mz_send, mz_recv, next_sem, load_sem, heads_ref,
    few_total, few_got, few_z, few_send, few_recv, fz_send, fz_recv, *got,
):
    pieces, groups, tokens, skew, bits, layer = dims
    chunks = tokens // CH
    i = pl.program_id(0)
    z = lax.axis_index("tensor")
    right, left = jnp.minimum(z + 1, pieces - 1), jnp.maximum(z - 1, 0)
    back = pieces - 1 - z
    depth = gb.shape[1]
    inner = groups * GC

    def halo_copy():
        return pltpu.make_async_remote_copy(
            src_ref=gnorm, dst_ref=hrecv,
            send_sem=halo_send, recv_sem=halo_recv, device_id={"tensor": left}, device_id_type=MESH,
        )

    def state_copy(group):
        return pltpu.make_async_remote_copy(
            src_ref=outgoing.at[group], dst_ref=incoming.at[group],
            send_sem=send.at[group], recv_sem=recv.at[group], device_id={"tensor": left}, device_id_type=MESH,
        )

    place = Place(bits)
    parts, parts_m = got[:bits], got[bits:]

    def part(step, group, half):
        left = (slice(None),) * (bits - 1 - step + 2)
        return (lax.rem(group, SLOTS),) + left + (pl.ds(half * LANES, LANES),)

    def held(step, group, half, keep):
        return (group,) + place.region(half, step, keep) + (slice(None), slice(None), pl.ds(half * LANES, LANES))

    def sum_copy(group, step, half):
        return pltpu.make_async_remote_copy(
            src_ref=own.at[held(step, group, half, False)], dst_ref=parts[step].at[part(step, group, half)],
            send_sem=sum_send.at[group, step, half], recv_sem=sum_recv.at[group, step, half],
            device_id={"dp": place.partner(half, step)}, device_id_type=MESH,
        )

    def z_copy(group, half):
        column = group // (pieces // 2)
        return pltpu.make_async_remote_copy(
            src_ref=own.at[(group,) + place.mine() + (slice(None), slice(None), pl.ds(half * LANES, LANES))],
            dst_ref=got_z.at[z, column], send_sem=z_send.at[group, half], recv_sem=z_recv.at[z, column],
            device_id={"tensor": quarter(group, half, pieces)}, device_id_type=MESH,
        )

    def advance(group, step):
        @pl.when(jnp.logical_and(group >= 0, group < groups))
        def _():
            for half in range(2):
                if step:
                    sum_copy(group, step - 1, half).wait_recv()
                    at = held(step - 1, group, half, True)
                    own[at] = own[at] + parts[step - 1][part(step - 1, group, half)]
                if step < bits:
                    sum_copy(group, step, half).start()
                if step == bits:

                    @pl.when(quarter(group, half, pieces) != z)
                    def _(half=half):
                        z_copy(group, half).start()

    def misc_copy(step):
        return pltpu.make_async_remote_copy(
            src_ref=own_m.at[place.region(False, step, False)], dst_ref=parts_m[step],
            send_sem=msum_send.at[step], recv_sem=msum_recv.at[step],
            device_id={"dp": place.partner(False, step)}, device_id_type=MESH,
        )

    def misc_z(k):
        return pltpu.make_async_remote_copy(
            src_ref=own_m.at[place.mine()], dst_ref=got_m.at[z], send_sem=mz_send.at[k], recv_sem=mz_recv.at[z],
            device_id={"tensor": lax.rem(z + k, pieces)}, device_id_type=MESH,
        )

    def misc_advance(step):
        if step:
            misc_copy(step - 1).wait_recv()
            at = place.region(False, step - 1, True)
            own_m[at] = own_m[at] + parts_m[step - 1][...]
        if step < bits:
            misc_copy(step).start()
        else:
            for k in range(1, pieces):
                misc_z(k).start()
            got_m[z] = own_m[place.mine()]

    def drain(late):
        for step in reversed(range(1, bits + 1)):
            if late <= step:
                advance(groups - 1 + late - step, step)

    def few_copy(step):
        return pltpu.make_async_remote_copy(
            src_ref=few_total.at[step], dst_ref=few_got.at[step], send_sem=few_send.at[step],
            recv_sem=few_recv.at[step], device_id={"dp": place.partner(False, step)}, device_id_type=MESH,
        )

    def few_line(k, source):
        return pltpu.make_async_remote_copy(
            src_ref=few_total.at[bits], dst_ref=few_z.at[source], send_sem=fz_send.at[k], recv_sem=fz_recv.at[source],
            device_id={"tensor": lax.rem(z + k, pieces)}, device_id_type=MESH,
        )

    def few_advance(step):
        if step:
            few_copy(step - 1).wait_recv()
            few_total[step] = few_total[step - 1] + few_got[step - 1]
        if step < bits:
            few_copy(step).start()
        else:
            for k in range(1, pieces):
                few_line(k, z).start()
            few_z[z] = few_total[bits]

    def load_blocks():
        found = []
        for k in range(depth // GC):
            cols = pl.ds(k * GC, GC)
            found.append(pltpu.make_async_copy(x_ref.at[:, cols], xs.at[k], load_sem.at[0, k]))
            found.append(pltpu.make_async_copy(g_ref.at[:, cols], fs.at[k], load_sem.at[1, k]))
        return found

    def taps():
        return shared_taps(csw_ref, csb_ref, layer)

    def shared_conv():
        return conv(lambda k: shared_ref[pl.ds(HALO - k, tokens), :], keep_ref, taps(), tokens)

    @pl.when(i == 0)
    def _():
        greet(place, z, pieces)
        put_heads(rows_ref, heads_ref)

        @pl.when(z == pieces - 1)
        def _():
            incoming[...] = jnp.zeros(incoming.shape, BF)

        copies = [pltpu.make_async_copy(next_ref, gx_ref, next_sem)] + load_blocks()
        for copy in copies:
            copy.start()
        for copy in copies:
            copy.wait()
        dots = jnp.zeros((tokens, 1), F32)
        for k in range(depth // GC):
            cols = slice(k * GC, (k + 1) * GC)
            low = fs[k].astype(BF)
            gb[:, cols] = low
            gbt[cols, :] = low.T
            dots = dots + jnp.sum(low.astype(F32) * (gx_ref[:, cols] - xs[k]), axis=1, keepdims=True)
        r = r_ref[...]
        r2[...] = r * r * dots * (1.0 / inner)
        _, steps, _, summed, toward, reach, kept = step_terms(
            step_ref[...], heads_ref, carried_ref, tail_ref, kept_ref, tokens
        )
        put_sums(summed, col, row, groups, tokens)
        terms[0] = split2(steps)
        terms[1] = split2(toward)
        terms[2] = split2(reach)
        kept2 = split2(kept)
        for group in range(groups):
            ke[group] = dot_nn(kept2, spread(group))
        mixed = shared_conv()
        maps = mixed * sigmoid(mixed)
        for c in range(chunks):
            part = maps[c * CH : (c + 1) * CH]
            into, out = part[:, :STATE].astype(BF), part[:, STATE:]
            inb[c], outb[c], outbt[c] = into, out.astype(BF), out.T.astype(BF)
            crosst[c] = dot_nt(into, out.astype(BF))
        for ref in (gx_ref, gnorm, dct, dbt, dgt, sd, sp, sq, se):
            ref[...] = jnp.zeros(ref.shape, F32)

    @pl.when(i < groups)
    def _():
        group = i
        slot = lax.rem(group, skew + 1)
        gp = side_params((pa, pb))
        mixed = conv(lambda k: val_ref[0, pl.ds(HALO - k, tokens), :], keep_ref, gp, tokens)
        part = sigmoid(mixed)
        x = mixed * part
        xs[slot] = x
        fs[slot] = part + x * (1.0 - part)
        r = twice(r_ref[...])
        gm = dot_nn(gb[...], side((oa, ob), 0))
        scan = y_ref[0] + gp[6:7] * x
        gate = gate_ref[0]
        part = sigmoid(gate)
        silu = gate * part
        gated = scan * silu
        normal = gated * r
        own[(group,) + place.all + (2,)] = (
            dot_nn(gbt[...], (normal * gp[5:6]).astype(BF)).astype(BF).reshape(place.dims + (-1, GC))
        )
        ggated = r * gp[5:6] * gm - gated * twice(r2[...])
        dy = ggated * silu
        dys[slot] = dy.astype(BF)
        dgs[slot] = (ggated * scan * (part + silu * (1.0 - part))).astype(BF)
        small_ref[pl.ds(group * 8, 8), :] = jnp.concatenate(
            [
                jnp.zeros((5, GC), F32),
                jnp.sum(gm * normal, axis=0, keepdims=True),
                jnp.sum(dy * x, axis=0, keepdims=True),
                jnp.zeros((1, GC), F32),
            ],
            axis=0,
        )
        spreader = spread(group)
        state = jnp.zeros((STATE, GC), F32)
        for c in reversed(range(chunks)):
            rows = pl.ds(c * CH, CH)
            reached = (dys[slot, rows, :].astype(F32) * dot_nn(terms[2, rows, :], spreader)).astype(BF)
            new = dot_nn(outbt[c], reached)
            state = ke[group, c : c + 1] * state + new
        fold[slot] = state

    j = i - back

    @pl.when(jnp.logical_and(j >= 0, j < groups))
    def _():
        @pl.when(z < pieces - 1)
        def _():
            state_copy(j).wait_recv()

        @pl.when(z > 0)
        def _():
            total = ke[j, 0:1]
            for c in range(1, chunks):
                total = total * ke[j, c : c + 1]
            outgoing[j] = (total * incoming[j].astype(F32) + fold[lax.rem(j, skew + 1)]).astype(BF)
            state_copy(j).start()

    @pl.when(i >= skew)
    def _():
        group = i - skew
        slot = lax.rem(group, skew + 1)
        gp = side_params((qa, qb))
        spreader, collector = spread(group), collect(group)
        turn_sums(col, group)
        grad = incoming[group].astype(F32)
        ends = [None] * chunks
        for c in reversed(range(chunks)):
            rows = pl.ds(c * CH, CH)
            low = grad.astype(BF)
            state = state_ref[0, c]
            ends[c] = jnp.sum(low.astype(F32) * state.astype(F32), axis=0, keepdims=True) * ke[group, c : c + 1]
            x = xs[slot, rows, :]
            dy = dys[slot, rows, :].astype(F32)
            steps = dot_nn(terms[0, rows, :], spreader)
            toward = dot_nn(terms[1, rows, :], spreader)
            reached = (dy * dot_nn(terms[2, rows, :], spreader)).astype(BF)
            grad = ke[group, c : c + 1] * grad + dot_nn(outbt[c], reached)
            sized = x * steps
            weighted = (sized * toward).astype(BF)
            later = dot_nn(inb[c], low) * toward
            dbt[c] += dot_nt(weighted, low)
            dct[c] += dot_nt(reached, state)
            parts = []
            cross = crosst[c]
            pairs_total = jnp.zeros((CH, CH), F32)
            for pair in range(HG // 2):
                at = slice(pair * LANES, (pair + 1) * LANES)
                dyp = dy[:, at]
                products = dot_nt(halves(sized[:, at]), dyp.astype(BF))
                decayed = []
                for n in range(2):
                    h = 2 * pair + n
                    across = row[group, h : h + 1, rows] - col[1, rows, h : h + 1]
                    decay = jnp.exp(jnp.minimum(across, biast_ref[c]))
                    decayed.append((cross * decay).astype(BF))
                    pairs_total = pairs_total + products[n * CH : (n + 1) * CH] * decay
                parts.append(dot_nn(jnp.concatenate(decayed, axis=1), halves(dyp)))
            dgt[c] += pairs_total
            within = jnp.concatenate(parts, axis=1)
            whole = within + later
            lowered = dy * yb_ref[0, rows, :] - sized.astype(BF).astype(F32) * within
            sd[rows, :] += dot_nn(split2(whole * x), collector)
            sp[rows, :] += dot_nn(split2(lowered), collector)
            sq[rows, :] += dot_nn(split2(sized * later), collector)
            dxd[rows, :] = (whole * steps + gp[6:7] * dy) * fs[slot, rows, :]
        for step in reversed(range(1, bits + 1)):
            advance(group - step, step)
        ends.append(jnp.zeros((8 - chunks, GC), F32))
        se[...] += dot_nn(split2(jnp.concatenate(ends, axis=0)), collector)
        wide, sums = conv_back(
            dxd[...], lambda k: valb_ref[0, pl.ds(HALO - k, tokens), :], keep_ref, gp, tokens
        )
        small_ref[pl.ds(group * 8, 8), :] += jnp.concatenate(sums + [jnp.zeros((3, GC), F32)], axis=0)
        wide = wide.astype(BF)
        dgate = dgs[slot]
        shape = place.dims + (-1, GC)
        own[(group,) + place.all + (0,)] = dot_nn(nxt[...], dgate).astype(BF).reshape(shape)
        own[(group,) + place.all + (1,)] = (
            (dot_nn(nxt[...], wide[HALO:]) + dot_nn(nht[...], wide[:HALO])).astype(BF).reshape(shape)
        )
        advance(group, 0)
        back_wide = dot_nt(wide, side((wa, wb), 1))
        gnorm[...] += back_wide[:HALO]
        gx_ref[...] += back_wide[HALO:] + dot_nt(dgate, side((wa, wb), 0))

    @pl.when(i == groups + skew - 1)
    def _():
        for copy in load_blocks():
            copy.start()
        upper = (iota2((CH, CH), 0) <= iota2((CH, CH), 1)).astype(F32)
        before = (iota2((CH, CH), 0) > iota2((CH, CH), 1)).astype(F32)
        raw, steps, rates, _, _, _, _ = step_terms(step_ref[...], heads_ref, carried_ref, tail_ref, kept_ref, tokens)
        drates, dmaps = [], []
        for c in range(chunks):
            rows = slice(c * CH, (c + 1) * CH)
            drates.append(dot_nn(upper, sp[rows, :], HI) + dot_nn(before, sq[rows, :], HI) + se[c : c + 1])
            low = dgt[c].astype(BF)
            into = dbt[c] + dot_nn(low, outb[c])
            out = dct[c] + dot_tn(low, inb[c])
            dmaps.append(jnp.concatenate([into, out], axis=1))
        drate = jnp.concatenate(drates, axis=0)
        dstep = (sd[...] - drate * heads_ref[1:2]) * sigmoid(raw)
        head_sums = jnp.concatenate(
            [jnp.sum(dstep, axis=0, keepdims=True), jnp.sum(drate * rates, axis=0, keepdims=True)], axis=1
        )
        mixed = shared_conv()
        part = sigmoid(mixed)
        dmixed = jnp.concatenate(dmaps, axis=0) * (part + mixed * part * (1.0 - part))
        wide, sums = conv_back(dmixed, lambda k: shared_ref[pl.ds(HALO - k, tokens), :], keep_ref, taps(), tokens)
        small_ref[pl.ds(groups * 8, 8), :] = jnp.concatenate(sums + [jnp.zeros((3, 2 * STATE), F32)], axis=0)
        wide = wide.astype(BF)
        dstep = dstep.astype(BF)
        back_wide = dot_nt(wide, few_ref[:, :, : 2 * STATE].reshape(depth, 2 * STATE))
        gnorm[...] += back_wide[:HALO]

        @pl.when(z > 0)
        def _():
            halo_copy().start()

        gx_ref[...] += back_wide[HALO:] + dot_nt(dstep, few_ref[:, :, 2 * STATE :].reshape(depth, LANES))
        drain(1)
        misc = jnp.concatenate(
            [dot_nn(nxt[...], wide[HALO:]) + dot_nn(nht[...], wide[:HALO]), dot_nn(nxt[...], dstep)], axis=1
        )
        own_m[...] = misc.astype(BF).reshape(own_m.shape)
        misc_advance(0)

        @pl.when(z < pieces - 1)
        def _():
            halo_copy().wait_recv()
            gx_ref[pl.ds(tokens - HALO, HALO), :] += hrecv[...]

        for copy in load_blocks():
            copy.wait()
        blocks = [(k, slice(k * GC, (k + 1) * GC)) for k in range(depth // GC)]
        power = inside = jnp.zeros((tokens, 1), F32)
        for k, cols in blocks:
            power = power + jnp.sum(xs[k] * xs[k], axis=1, keepdims=True)
            gained = gx_ref[:, cols] * gain_ref[layer : layer + 1, cols]
            inside = inside + jnp.sum(gained * xs[k], axis=1, keepdims=True)
        q = lax.rsqrt(power * (1.0 / depth) + EPS)
        inside = inside * (q * q * q) * (1.0 / depth)
        cuts = [jnp.sum(gx_ref[:, cols] * xs[k] * q, axis=0, keepdims=True) for k, cols in blocks]
        few_total[0, pl.ds(0, groups * 8 + 8), :] = small_ref[pl.ds(0, groups * 8 + 8), :]
        few_total[0, pl.ds(groups * 8 + 8, 8), :] = jnp.concatenate(
            cuts + [head_sums, jnp.zeros((7 - len(cuts), GC), F32)], axis=0
        )
        few_advance(0)
        misc_advance(1)
        for k, cols in blocks:
            gx_ref[:, cols] = fs[k] + q * (gx_ref[:, cols] * gain_ref[layer : layer + 1, cols]) - xs[k] * inside
        for step in range(2, bits + 1):
            drain(step)
            few_advance(step - 1)
            misc_advance(step)
        few_advance(bits)
        for k in range(1, pieces):
            few_line(k, lax.rem(z + k, pieces)).wait_recv()
        total = few_z[0]
        for source in range(1, pieces):
            total = total + few_z[source]
        small_ref[...] = total
        for k in range(1, pieces):
            source = lax.rem(z + k, pieces)
            pltpu.make_async_remote_copy(
                src_ref=own_m.at[place.mine()], dst_ref=got_m.at[source], send_sem=mz_send.at[k],
                recv_sem=mz_recv.at[source], device_id={"tensor": source}, device_id_type=MESH,
            ).wait_recv()
        total = got_m[0].astype(F32)
        for source in range(1, pieces):
            total = total + got_m[source].astype(F32)
        gm_ref[...] = total
        upper_half = z >= pieces // 2
        first = jnp.where(upper_half, pieces - 1 - z, z)
        for column in range(groups // (pieces // 2)):
            group = first + column * (pieces // 2)
            for k in range(1, pieces):
                source = lax.rem(z + k, pieces)
                pltpu.make_async_remote_copy(
                    src_ref=got_z.at[source, column], dst_ref=got_z.at[source, column],
                    send_sem=z_send.at[0, 0], recv_sem=z_recv.at[source, column],
                    device_id={"tensor": source}, device_id_type=MESH,
                ).wait_recv()
            for half in range(2):

                @pl.when(upper_half if half else jnp.logical_not(upper_half))
                def _(half=half, group=group, column=column):
                    total = own[(group,) + place.mine() + (slice(None), slice(None), pl.ds(half * LANES, LANES))]
                    total = total.astype(F32)
                    for k in range(1, pieces):
                        total = total + got_z[lax.rem(z + k, pieces), column].astype(F32)
                    gw_ref[:, :, column * LANES : (column + 1) * LANES] = total

        for group in range(groups):
            for step in range(bits):
                for half in range(2):
                    sum_copy(group, step, half).wait_send()

            for half in range(2):

                @pl.when(quarter(group, half, pieces) != z)
                def _(group=group, half=half):
                    z_copy(group, half).wait_send()

        for step in range(bits):
            misc_copy(step).wait_send()
            few_copy(step).wait_send()
        for k in range(1, pieces):
            misc_z(k).wait_send()
            few_line(k, z).wait_send()

        @pl.when(z > 0)
        def _():
            halo_copy().wait_send()
            for group in range(groups):
                state_copy(group).wait_send()


def whole(shape):
    return pl.BlockSpec(shape, lambda i: (0,) * len(shape), pipeline_mode=pl.Buffered(1))


def quarter(group, half, pieces):
    at = group % (pieces // 2)
    return pieces - 1 - at if half else at


def group_specs(dims, wall):
    pieces, groups, _, skew = dims
    dp, _, _, share, _ = wall
    last = groups - 1

    def early(i):
        return jnp.minimum(i, last)

    def late(i):
        return jnp.maximum(i - skew, 0)

    def block(rows, at):
        return pl.BlockSpec((1, rows, GC), lambda i: (at(i), 0, 0))

    def both(make):
        return [make(0), make(1)]

    def column(i, at):
        return at(i) // (pieces // 2)

    def pair(at):
        return both(
            lambda half: pl.BlockSpec(
                (dp, 1, 2, share, LANES), lambda i: (0, quarter(at(i), half, pieces), 0, 0, column(i, at))
            )
        )

    def single(at):
        return both(
            lambda half: pl.BlockSpec(
                (dp, 1, 1, share, LANES), lambda i: (0, quarter(at(i), half, pieces), 2, 0, column(i, at))
            )
        )

    def params(layer, at):
        return both(
            lambda half: pl.BlockSpec(
                (1, 1, 8, LANES), lambda i: (quarter(at(i), half, pieces), layer, 0, column(i, at))
            )
        )

    return early, late, block, pair, single, params


def side(refs, n):
    rows = refs[0].shape[0] * refs[0].shape[3]
    return jnp.concatenate([ref[:, 0, n].reshape(rows, LANES) for ref in refs], axis=1)


def side_params(refs):
    return jnp.concatenate([ref[0, 0] for ref in refs], axis=1)


def fixed(shape, place):
    return pl.BlockSpec(shape, lambda i: place, pipeline_mode=pl.Buffered(1))


def layer_forward(dims, bits, layer, x, gain, w, few, pack, csw, csb, masks, later):
    pieces, groups, tokens, skew = dims
    keep, bias, _, carried, tail, kept = masks
    chunks = tokens // CH
    depth = x.shape[1]
    ext = tokens + HALO
    slots = skew + 1
    early, late, block, pair, single, params = group_specs(dims, w.shape)
    anywhere = pl.BlockSpec(memory_space=pl.ANY)
    near = pl.BlockSpec(memory_space=pltpu.VMEM)
    gathers = later is not None
    cut = (2,) * bits
    buffers, sems = gather_scratch(pieces, bits, w.shape[3])
    if gathers:
        later_few, later = later
    return pl.pallas_call(
        partial(forward_kernel, dims + (bits, layer, gathers)),
        grid=(groups + skew,),
        in_specs=[
            whole((tokens, depth)), whole(gain.shape), *pair(early), *single(late),
            whole(few.shape), *params(layer, early), *params(layer, late), fixed((pieces, 1, 8, 2 * LANES), (0, layer, 0, 0)),
            whole(csw.shape), whole(csb.shape),
            whole(keep.shape), whole(bias.shape), whole(carried.shape), whole(tail.shape), whole(kept.shape),
        ] + [near, anywhere] * gathers,
        out_specs=[
            whole((tokens, depth)), whole((depth, tokens)), whole((depth, HALO)),
            block(tokens, early), block(ext, early), block(tokens, late),
            pl.BlockSpec((1, chunks, STATE, GC), lambda i: (late(i), 0, 0, 0)),
            whole((ext, 2 * STATE)), whole((tokens, LANES)), whole((tokens, LANES)),
        ] + [near, anywhere] * gathers,
        out_shape=[
            jax.ShapeDtypeStruct((tokens, depth), F32),
            jax.ShapeDtypeStruct((depth, tokens), BF),
            jax.ShapeDtypeStruct((depth, HALO), BF),
            jax.ShapeDtypeStruct((groups, tokens, GC), F32),
            jax.ShapeDtypeStruct((groups, ext, GC), F32),
            jax.ShapeDtypeStruct((groups, tokens, GC), F32),
            jax.ShapeDtypeStruct((groups, chunks, STATE, GC), BF),
            jax.ShapeDtypeStruct((ext, 2 * STATE), F32),
            jax.ShapeDtypeStruct((tokens, LANES), F32),
            jax.ShapeDtypeStruct((tokens, LANES), F32),
        ] + (
            [jax.ShapeDtypeStruct(cut + later_few.shape, BF), jax.ShapeDtypeStruct(cut + (pieces,) + later.shape, BF)]
            if gathers
            else []
        ),
        scratch_shapes=[
            pltpu.VMEM((ext, depth), BF),
            pltpu.VMEM((chunks, CH, STATE), BF),
            pltpu.VMEM((chunks, STATE, CH), BF),
            pltpu.VMEM((chunks, CH, STATE), BF),
            pltpu.VMEM((chunks, CH, CH), F32),
            pltpu.VMEM((2, tokens, LANES), F32),
            pltpu.VMEM((groups, 8, tokens), F32),
            pltpu.VMEM((3, tokens, 2 * LANES), BF),
            pltpu.VMEM((groups, 8, GC), F32),
            pltpu.VMEM((slots, tokens, GC), F32),
            pltpu.VMEM((slots, tokens, GC), F32),
            pltpu.VMEM((slots, tokens, GC), F32),
            pltpu.VMEM((slots, chunks, STATE, GC), F32),
            pltpu.VMEM((slots, STATE, GC), F32),
            pltpu.VMEM((groups, STATE, GC), BF),
            pltpu.VMEM((groups, STATE, GC), BF),
            pltpu.VMEM((tokens, depth), F32),
            pltpu.VMEM((tokens, LANES), F32),
            pltpu.VMEM((8, LANES), F32),
            pltpu.SemaphoreType.DMA,
            pltpu.SemaphoreType.DMA,
            pltpu.SemaphoreType.DMA((groups,)),
            pltpu.SemaphoreType.DMA((groups,)),
        ] + (buffers + sems if gathers else []),
        compiler_params=pltpu.CompilerParams(
            collective_id=layer, has_side_effects=True, vmem_limit_bytes=VMEM_LIMIT_FORWARD,
            dimension_semantics=("arbitrary",),
        ),
        name="layer_forward",
    )(
        x, gain, w, w, w, w, few, pack, pack, pack, pack, pack, csw, csb, keep, bias, carried, tail, kept,
        *([later_few, later] if gathers else []),
    )


def layer_backward(dims, bits, layer, g, x, after, gain, saved, w, few, pack, csw, csb, masks):
    pieces, groups, tokens, skew = dims
    keep, _, biast, carried, tail, kept = masks
    nxt, nht, gate, val, y, states, shared, step_in, r = saved
    anywhere = pl.BlockSpec(memory_space=pl.ANY)
    chunks = tokens // CH
    depth = x.shape[1]
    _, _, _, share, wide = w.shape
    ext = tokens + HALO
    slots = max(skew + 1, depth // GC)
    few_shape = (groups * 8 + 16, GC)
    halves_of = [(2,) * (bits - 1 - step) for step in range(bits)]
    early, late, block, pair, single, params = group_specs(dims, w.shape)
    return pl.pallas_call(
        partial(backward_kernel, dims + (bits, layer)),
        grid=(groups + skew,),
        in_specs=[
            anywhere, anywhere, anywhere, whole(gain.shape),
            whole(nxt.shape), whole(nht.shape), whole((tokens, LANES)), *pair(late), *single(early),
            whole(few.shape), *params(layer, early), *params(layer, late), fixed((pieces, 1, 8, 2 * LANES), (0, layer, 0, 0)),
            whole(csw.shape), whole(csb.shape),
            whole(keep.shape), whole(biast.shape), whole(carried.shape), whole(tail.shape), whole(kept.shape),
            block(tokens, early), block(ext, early), block(tokens, early), block(ext, late), block(tokens, late),
            pl.BlockSpec((1, chunks, STATE, GC), lambda i: (late(i), 0, 0, 0)),
            whole((ext, 2 * STATE)), whole((tokens, LANES)),
        ],
        out_specs=[
            whole((tokens, depth)), whole((3, share, wide)), whole((share, 2 * STATE + LANES)),
            whole((groups * 8 + 16, GC)),
        ],
        out_shape=[
            jax.ShapeDtypeStruct((tokens, depth), F32),
            jax.ShapeDtypeStruct((3, share, wide), F32),
            jax.ShapeDtypeStruct((share, 2 * STATE + LANES), F32),
            jax.ShapeDtypeStruct((groups * 8 + 16, GC), F32),
        ],
        scratch_shapes=[
            pltpu.VMEM((tokens, depth), BF),
            pltpu.VMEM((depth, tokens), BF),
            pltpu.VMEM((tokens, LANES), F32),
            pltpu.VMEM((chunks, CH, STATE), BF),
            pltpu.VMEM((chunks, CH, STATE), BF),
            pltpu.VMEM((chunks, STATE, CH), BF),
            pltpu.VMEM((chunks, CH, CH), F32),
            pltpu.VMEM((2, tokens, LANES), F32),
            pltpu.VMEM((groups, 8, tokens), F32),
            pltpu.VMEM((3, tokens, 2 * LANES), BF),
            pltpu.VMEM((groups, 8, GC), F32),
            pltpu.VMEM((slots, tokens, GC), BF),
            pltpu.VMEM((slots, tokens, GC), F32),
            pltpu.VMEM((slots, tokens, GC), F32),
            pltpu.VMEM((slots, tokens, GC), BF),
            pltpu.VMEM((slots, STATE, GC), F32),
            pltpu.VMEM((groups, STATE, GC), BF),
            pltpu.VMEM((groups, STATE, GC), BF),
            pltpu.VMEM((HALO, depth), F32),
            pltpu.VMEM((chunks, CH, STATE), F32),
            pltpu.VMEM((chunks, CH, STATE), F32),
            pltpu.VMEM((chunks, CH, CH), F32),
            pltpu.VMEM((tokens, LANES), F32),
            pltpu.VMEM((tokens, LANES), F32),
            pltpu.VMEM((tokens, LANES), F32),
            pltpu.VMEM((8, LANES), F32),
            pltpu.VMEM((tokens, GC), F32),
            pltpu.VMEM((HALO, depth), F32),
            pltpu.VMEM((groups,) + (2,) * bits + (3, share, GC), BF),
            pltpu.VMEM((2,) * bits + (share, 2 * STATE + LANES), BF),
            pltpu.VMEM((pieces, 2 * groups // pieces, 3, share, LANES), BF),
            pltpu.VMEM((pieces, share, 2 * STATE + LANES), BF),
            pltpu.SemaphoreType.DMA,
            pltpu.SemaphoreType.DMA,
            pltpu.SemaphoreType.DMA((groups,)),
            pltpu.SemaphoreType.DMA((groups,)),
            pltpu.SemaphoreType.DMA((groups, bits, 2)),
            pltpu.SemaphoreType.DMA((groups, bits, 2)),
            pltpu.SemaphoreType.DMA((groups, 2)),
            pltpu.SemaphoreType.DMA((pieces, 2 * groups // pieces)),
            pltpu.SemaphoreType.DMA((bits,)),
            pltpu.SemaphoreType.DMA((bits,)),
            pltpu.SemaphoreType.DMA((pieces,)),
            pltpu.SemaphoreType.DMA((pieces,)),
            pltpu.SemaphoreType.DMA,
            pltpu.SemaphoreType.DMA((2, depth // GC)),
            pltpu.VMEM((8, LANES), F32),
            pltpu.VMEM((bits + 1,) + few_shape, F32),
            pltpu.VMEM((bits,) + few_shape, F32),
            pltpu.VMEM((pieces,) + few_shape, F32),
            pltpu.SemaphoreType.DMA((bits,)),
            pltpu.SemaphoreType.DMA((bits,)),
            pltpu.SemaphoreType.DMA((pieces,)),
            pltpu.SemaphoreType.DMA((pieces,)),
            *[pltpu.VMEM((SLOTS,) + dims_left + (3, share, GC), BF) for dims_left in halves_of],
            *[pltpu.VMEM(dims_left + (share, 2 * STATE + LANES), BF) for dims_left in halves_of],
        ],
        compiler_params=pltpu.CompilerParams(
            collective_id=3 + layer, has_side_effects=True, vmem_limit_bytes=VMEM_LIMIT, dimension_semantics=("arbitrary",)
        ),
        name="layer_backward",
    )(
        g, x, after, gain, nxt, nht, r, w, w, w, w, few, pack, pack, pack, pack, pack, csw, csb, keep, biast, carried, tail, kept,
        gate, val, y, val, y, states, shared, step_in,
    )


def near_first(z, pieces):
    table = [sorted(range(pieces), key=lambda k: (abs(k - at), k > at)) for at in range(pieces)]
    return [sum(jnp.where(z == at, table[at][p], 0) for at in range(pieces)) for p in range(pieces)]


class Gather:
    def __init__(self, place, z, pieces, mine, wall, few, few_z, few_all, *sems):
        self.place, self.z, self.pieces, self.bits = place, z, pieces, place.bits
        self.mine, self.wall, self.few, self.few_z, self.few_all = mine, wall, few, few_z, few_all
        self.own_sem, self.z_send, self.z_recv, self.d_send, self.d_recv, *sems = sems
        self.t_send, self.t_recv, self.f_send, self.f_recv = sems
        wide = mine.shape[-1]
        self.cols = [pl.ds(0, wide // 2), pl.ds(wide // 2, wide // 2)]
        self.few_cols = [pl.ds(0, 2 * STATE), pl.ds(2 * STATE, LANES)]
        self.order = near_first(z, pieces)
        rest = list(range(1, self.bits))
        self.paths = [rest + [0], rest[::-1] + [0]]
        self.own = pltpu.make_async_copy(mine, wall.at[place.mine() + (z,)], self.own_sem)

    def z_copy(self, zi, up):
        src = self.mine if zi is self.z else self.wall.at[self.place.mine() + (zi,)]
        return pltpu.make_async_remote_copy(
            src_ref=src, dst_ref=self.wall.at[self.place.mine() + (zi,)], send_sem=self.z_send.at[int(up), zi],
            recv_sem=self.z_recv.at[zi], device_id={"tensor": self.z + (1 if up else -1)}, device_id_type=MESH,
        )

    def d_copy(self, p, half, step):
        path = self.paths[half]
        cols = (slice(None), slice(None), self.cols[half])
        ref = self.wall.at[self.place.along(path[:step]) + (self.order[p],) + cols]
        return pltpu.make_async_remote_copy(
            src_ref=ref if p or step else self.mine.at[cols], dst_ref=ref, send_sem=self.d_send.at[p, half, step], recv_sem=self.d_recv.at[p, half, step],
            device_id={"dp": self.place.flip(path[step])}, device_id_type=MESH,
        )

    def pass_on(self, zi, act):
        z, last = self.z, self.pieces - 1

        @pl.when(jnp.logical_and(zi <= z, z < last))
        def _():
            act(self.z_copy(zi, True))

        @pl.when(jnp.logical_and(zi >= z, z > 0))
        def _():
            act(self.z_copy(zi, False))

    def line_copy(self, k):
        return pltpu.make_async_remote_copy(
            src_ref=self.few.at[:, self.few_cols[1]], dst_ref=self.few_z.at[self.z], send_sem=self.t_send.at[k],
            recv_sem=self.t_recv.at[k], device_id={"tensor": lax.rem(self.z + k, self.pieces)}, device_id_type=MESH,
        )

    def few_copy(self, half, step):
        path = self.paths[half]
        ref = self.few_all.at[self.place.along(path[:step]) + (slice(None), self.few_cols[half])]
        return pltpu.make_async_remote_copy(
            src_ref=ref, dst_ref=ref, send_sem=self.f_send.at[half, step], recv_sem=self.f_recv.at[half, step],
            device_id={"dp": self.place.flip(path[step])}, device_id_type=MESH,
        )

    def few_event(self, step):
        if step == 0:
            total = self.few[:, self.few_cols[1]]
            for k in range(1, self.pieces):
                self.line_copy(k).wait_recv()
                total = total + self.few_z[lax.rem(self.z + self.pieces - k, self.pieces)]
            self.few_all[self.place.mine()] = jnp.concatenate([self.few[:, self.few_cols[0]], total], axis=1)
        for half in range(2):
            if step:
                self.few_copy(half, step - 1).wait_recv()
            if step < self.bits:
                self.few_copy(half, step).start()

    def start(self):
        for half in range(2):
            self.d_copy(0, half, 0).start()
        self.pass_on(self.z, lambda copy: copy.start())
        self.own.start()
        for k in range(1, self.pieces):
            self.line_copy(k).start()

    def arrive(self, p):
        zi = self.order[p]
        pltpu.make_async_remote_copy(
            src_ref=self.mine, dst_ref=self.wall.at[self.place.mine() + (zi,)], send_sem=self.z_send.at[0, zi],
            recv_sem=self.z_recv.at[zi], device_id={"tensor": zi}, device_id_type=MESH,
        ).wait_recv()
        self.pass_on(zi, lambda copy: copy.start())
        for half in range(2):
            self.d_copy(p, half, 0).start()

    def double(self, p, step):
        if p == 0 and step == 1:
            self.own.wait()
        for half in range(2):
            self.d_copy(p, half, step - 1).wait_recv()
            if step < self.bits:
                self.d_copy(p, half, step).start()

    def events(self):
        found = []
        for p in range(self.pieces):
            if p:
                found.append((10.0 * p, partial(self.arrive, p)))
            for step in range(1, self.bits + 1):
                late = 0.0 if step < self.bits - 1 else 0.8
                found.append((10.0 * p + 9.5 * step + late, partial(self.double, p, step)))
        for step in range(self.bits + 1):
            found.append((5.0 + 8.0 * step, partial(self.few_event, step)))
        return sorted(found, key=lambda event: event[0])

    def finish(self):
        for p in range(self.pieces):
            self.pass_on(self.order[p], lambda copy: copy.wait_send())
            for half in range(2):
                for step in range(self.bits):
                    self.d_copy(p, half, step).wait_send()
        for k in range(1, self.pieces):
            self.line_copy(k).wait_send()
        for half in range(2):
            for step in range(self.bits):
                self.few_copy(half, step).wait_send()


def greet(place, z, pieces):
    barrier = pltpu.get_barrier_semaphore()
    for b in range(place.bits):
        pl.semaphore_signal(barrier, inc=1, device_id={"dp": place.flip(b)}, device_id_type=MESH)
    for k in range(1, pieces):
        pl.semaphore_signal(barrier, inc=1, device_id={"tensor": lax.rem(z + k, pieces)}, device_id_type=MESH)
    pl.semaphore_wait(barrier, place.bits + pieces - 1)


def write_masks(z, tokens, starts_ref, keep_ref, bias_ref, biast_ref, carried_ref, tail_ref, kept_ref):
    first = z * tokens

    def label(position):
        total = None
        for k in range(starts_ref.shape[1]):
            term = jnp.where(position >= starts_ref[0, k], 1.0, 0.0)
            total = term if total is None else total + term
        return total

    def same(a, b):
        return jnp.where(a == b, 1.0, 0.0)

    for c in range(tokens // CH):
        begin = first + c * CH
        down = iota2((CH, LANES), 0) + begin
        across = iota2((CH, LANES), 1) + begin
        own, other = label(down), label(across)
        rows = pl.ds(c * CH, CH)
        for k in range(1, 4):
            keep_ref[k - 1, rows, :] = same(label(down - k), own)
        equal = own == other
        bias_ref[c] = jnp.where(equal, jnp.where(down >= across, 0.0, NEG), NEG)
        biast_ref[c] = jnp.where(equal, jnp.where(down <= across, 0.0, NEG), NEG)
        flat = jnp.zeros((CH, LANES), jnp.int32) + begin
        before, final = label(flat - 1), label(flat + (CH - 1))
        carried_ref[rows, :] = same(own, before)
        tail_ref[rows, :] = same(own, final)
        kept_ref[pl.ds(c, 1), :] = same(final, before)[:1]
    kept_ref[pl.ds(tokens // CH, 8 - tokens // CH), :] = jnp.zeros((8 - tokens // CH, LANES), F32)


def gather_kernel(
    dims, starts, tokens_ref, cotangent_ref, cvw, cvb, gate_gain, skip, bias_in, decay, bc, dt, mine, wall, x_all, g_all,
    few_out, few_later, pack_out, keep, bias, biast, carried, tail, kept,
    x_wide, g_wide, pack, pack_all, few, few_z, few_all, wide_sem, pk_send, pk_recv, *sems,
):
    pieces, tokens, bits = dims
    place = Place(bits)
    z = lax.axis_index("tensor")
    greet(place, z, pieces)
    gather = Gather(place, z, pieces, mine, wall, few, few_z, few_all, *sems)

    heads = skip.shape[1]
    upper_half = z >= pieces // 2
    first = HG * jnp.where(upper_half, pieces - 1 - z, z) + jnp.where(upper_half, HG // 2, 0)

    def lane_of(head):
        return first + HG * (pieces // 2) * (head // 2) + head % 2

    def spot(ref, layer):
        lane = iota2((1, LANES), 1)
        total = jnp.zeros((1, LANES), F32)
        for head in range(heads):
            total = jnp.where(lane == lane_of(head), ref[layer : layer + 1, head : head + 1], total)
        return total

    low, high = iota2((heads, LANES), 0), iota2((heads, LANES), 1)
    chosen = (lane_of(0) + HG * (pieces // 2) * (low // 2) + low % 2 == high).astype(F32).astype(BF)
    for layer in range(LAYERS):
        wide = jnp.concatenate([bc[layer], dot_nn(dt[layer], chosen).astype(BF)], axis=1)
        if layer == 0:
            few[...] = wide
        else:
            few_later[...] = wide
    gather.start()
    channel = iota2((1, cvb.shape[1]), 1) // HD
    for layer in range(LAYERS):
        skips = jnp.zeros(channel.shape, F32)
        for head in range(heads):
            skips = jnp.where(channel == head, skip[layer : layer + 1, head : head + 1], skips)
        own = slice(layer, layer + 1)
        rest = jnp.zeros((1, cvb.shape[1] - 2 * LANES), F32)
        tail_row = jnp.concatenate([spot(bias_in, layer), spot(decay, layer), rest], axis=1)
        pack[layer] = jnp.concatenate([cvw[layer], cvb[own], gate_gain[own], skips, tail_row], axis=0)

    def pack_copy(k):
        return pltpu.make_async_remote_copy(
            src_ref=pack, dst_ref=pack_all.at[z], send_sem=pk_send.at[k], recv_sem=pk_recv.at[k],
            device_id={"tensor": lax.rem(z + k, pieces)}, device_id_type=MESH,
        )

    for k in range(1, pieces):
        pack_copy(k).start()
    pack_all[z] = pack[...]
    wides = []
    for k, (narrow, wide, out) in enumerate(((tokens_ref, x_wide, x_all), (cotangent_ref, g_wide, g_all))):
        wide[...] = narrow[...].astype(F32)
        wides.append(pltpu.make_async_copy(wide, out, wide_sem.at[k]))
        wides[k].start()
    write_masks(z, tokens, starts, keep, bias, biast, carried, tail, kept)
    for _, act in gather.events():
        act()
    gather.finish()
    for copy in wides:
        copy.wait()
    for k in range(1, pieces):
        pack_copy(k).wait()
    few_out[...] = few_all[...]
    pack_out[...] = pack_all[...]


def gather_scratch(pieces, bits, share):
    dma = pltpu.SemaphoreType.DMA
    return [pltpu.VMEM((pieces, share, LANES), BF), pltpu.VMEM((2,) * bits + (share, 2 * STATE + LANES), BF)], [
        dma, dma((2, pieces)), dma((pieces,)), dma((pieces, 2, bits)), dma((pieces, 2, bits)),
        dma((pieces,)), dma((pieces,)), dma((2, bits)), dma((2, bits)),
    ]


def gather_first(dims, starts, x, g, params, bc, dt, share):
    pieces, tokens, bits = dims
    cut = (2,) * bits
    chunks = tokens // CH
    dma = pltpu.SemaphoreType.DMA
    anywhere = pl.BlockSpec(memory_space=pl.ANY)
    near = pl.BlockSpec(memory_space=pltpu.VMEM)
    buffers, sems = gather_scratch(pieces, bits, share.shape[1])
    pack = (LAYERS, 8, params[1].shape[1])
    few = (share.shape[1], 2 * STATE + LANES)
    return pl.pallas_call(
        partial(gather_kernel, dims),
        in_specs=[pl.BlockSpec(memory_space=pltpu.SMEM)] + [near] * 10 + [anywhere],
        out_specs=[anywhere] * 3 + [near] * 9,
        out_shape=[
            jax.ShapeDtypeStruct(cut + (pieces,) + share.shape, BF),
            jax.ShapeDtypeStruct(x.shape, F32),
            jax.ShapeDtypeStruct(g.shape, F32),
            jax.ShapeDtypeStruct(cut + few, BF),
            jax.ShapeDtypeStruct(few, BF),
            jax.ShapeDtypeStruct((pieces,) + pack, F32),
            jax.ShapeDtypeStruct((3, tokens, LANES), F32),
            jax.ShapeDtypeStruct((chunks, CH, CH), F32),
            jax.ShapeDtypeStruct((chunks, CH, CH), F32),
            jax.ShapeDtypeStruct((tokens, LANES), F32),
            jax.ShapeDtypeStruct((tokens, LANES), F32),
            jax.ShapeDtypeStruct((8, LANES), F32),
        ],
        scratch_shapes=[
            pltpu.VMEM(x.shape, F32), pltpu.VMEM(g.shape, F32), pltpu.VMEM(pack, F32), pltpu.VMEM((pieces,) + pack, F32),
            pltpu.VMEM(few, BF),
        ] + buffers + [dma((2,)), dma((pieces,)), dma((pieces,))] + sems,
        compiler_params=pltpu.CompilerParams(collective_id=2, has_side_effects=True, vmem_limit_bytes=VMEM_LIMIT),
        name="gather_first",
    )(starts, x, g, *params, bc, dt, share)


def local(
    tokens, gate_value_weight, w_bc, w_dt, w_out, norm_gain, conv_value_w, conv_value_b, conv_shared_w, conv_shared_b,
    step_bias, decay_log, skip_gain, gate_gain, starts, cotangent,
):
    pieces, dp = lax.axis_size("tensor"), lax.axis_size("dp")
    z = lax.axis_index("tensor")
    bits = (dp - 1).bit_length()
    count, depth = tokens.shape
    own = conv_value_b.shape[1]
    few = step_bias.shape[1]
    groups = pieces * own // GC
    dims = (pieces, groups, count, pieces - 1)

    shares = [
        jnp.concatenate([jnp.swapaxes(gate_value_weight[layer], 0, 1), w_out[layer][None]], axis=0)
        for layer in range(LAYERS)
    ]
    wall, x, grad, few_all, few_later, pack, *masks = gather_first(
        (pieces, count, bits), starts, tokens, cotangent,
        (conv_value_w, conv_value_b, gate_gain, skip_gain, step_bias, decay_log), w_bc, w_dt, shares[0],
    )
    line, saved, weights = [x], [], []
    for layer in range(LAYERS):
        weights.append((wall.reshape((dp,) + wall.shape[bits:]), few_all.reshape((dp,) + few_all.shape[bits:])))
        later = (few_later, shares[layer + 1]) if layer + 1 < LAYERS else None
        x, *kept = layer_forward(
            dims, bits, layer, x, norm_gain, *weights[-1], pack, conv_shared_w, conv_shared_b, masks, later
        )
        if later is not None:
            *kept, few_all, wall = kept
        line.append(x)
        saved.append(kept)
    upper_half = z >= pieces // 2
    at = jnp.where(upper_half, pieces - 1 - z, z)

    def own_heads(v):
        v = v[..., : pieces * few].reshape(v.shape[:-1] + (few // 2, pieces // 2, 2, 2))
        v = lax.dynamic_index_in_dim(v, at, axis=v.ndim - 3, keepdims=False)
        v = lax.dynamic_index_in_dim(v, upper_half.astype(jnp.int32), axis=v.ndim - 2, keepdims=False)
        return v.reshape(v.shape[:-2] + (few,))

    big, small = [None] * LAYERS, [None] * LAYERS
    for layer in reversed(range(LAYERS)):
        grad, gw, gm, small[layer] = layer_backward(
            dims, bits, layer, grad, line[layer], line[layer + 1], norm_gain, saved[layer], *weights[layer], pack,
            conv_shared_w, conv_shared_b, masks,
        )
        gdt = own_heads(gm[:, 2 * STATE :])
        big[layer] = (jnp.swapaxes(gw[:2], 0, 1), gm[:, : 2 * STATE], gdt, gw[2])
    small = jnp.stack(small)

    def stacked(member):
        return jnp.stack([big[layer][member] for layer in range(LAYERS)], axis=0)

    rows = small[:, : groups * 8].reshape(LAYERS, 2 * groups // pieces, pieces // 2, 8, 2, LANES)
    rows = lax.dynamic_index_in_dim(rows, at, axis=2, keepdims=False)
    rows = lax.dynamic_index_in_dim(rows, upper_half.astype(jnp.int32), axis=3, keepdims=False)
    rows = jnp.swapaxes(rows, 1, 2).reshape(LAYERS, 8, own)
    gcs = small[:, groups * 8 : groups * 8 + 8]
    ends = small[:, groups * 8 + 8 :]
    cuts = depth // GC
    gheads = own_heads(ends[:, cuts].reshape(LAYERS, 2, LANES))
    return (
        x.astype(BF), grad, stacked(0), stacked(1), stacked(2), stacked(3), ends[:, :cuts].reshape(LAYERS, depth),
        rows[:, :4], rows[:, 4], gcs[:, :4], gcs[:, 4], gheads[:, 0], gheads[:, 1],
        jnp.sum(rows[:, 6].reshape(LAYERS, few, HD), axis=2), rows[:, 5],
    )


def solution(mesh):
    in_specs = (
        P(("dp", "tensor"), None),
        P(None, "dp", None, "tensor"),
        P(None, "dp", None),
        P(None, "dp", "tensor"),
        P(None, "dp", "tensor"),
        P(),
        P(None, None, "tensor"),
        P(None, "tensor"),
        P(),
        P(),
        P(None, "tensor"),
        P(None, "tensor"),
        P(None, "tensor"),
        P(None, "tensor"),
        P("dp", None),
        P(("dp", "tensor"), None),
    )
    out_specs = (
        P(("dp", "tensor"), None),
        P(("dp", "tensor"), None),
        P(None, "dp", None, "tensor"),
        P(None, "dp", None),
        P(None, "dp", "tensor"),
        P(None, "dp", "tensor"),
        P(),
        P(None, None, "tensor"),
        P(None, "tensor"),
        P(),
        P(),
        P(None, "tensor"),
        P(None, "tensor"),
        P(None, "tensor"),
        P(None, "tensor"),
    )
    return jax.shard_map(local, mesh=mesh, in_specs=in_specs, out_specs=out_specs, check_vma=False)
```

time: 1160 us -> 473 us (0.41)
  waiting for transfers between devices: 698 us -> 0 us
  Pallas kernels: 205 us -> 444 us
  blocking collectives: 188 us -> 0 us
  local copies, waits for them, and re-layouts: 37.7 us -> 11.3 us
  between operations: 15 us -> 1.1 us
    reduce_scatter x12 -> x0, waiting for transfers between devices: 480 us -> none  [the longest x6 328 us: scatter(): v = lax.psum_scatter(v, 'dp', scatter_dimension=0, tiled=True)]
    pallas_call x4 -> x5, Pallas kernels: 205 us -> 444 us  [the longest x2 237 us: layer_backward(): pl.pallas_call(partial(backward_kernel, dims + (bits, layer)), grid=(grou...]
    all_gather x5 -> x0, blocking collectives: 168 us -> none  [the longest x2 131 us: local(): lax.all_gather(w_dt[layer], both, axis=0)]
    psum x2 -> x0, waiting for transfers between devices: 144 us -> none  [the longest x1 129 us: local(): small = lax.psum(small, both)]
    all_gather x4 -> x0, waiting for transfers between devices: 69.8 us -> none  [the longest x2 69.7 us: local(): pair = lax.all_gather(pair, both, axis=0).reshape((dp, pieces) + pair.shape)]
    unnamed x1 -> x0, blocking collectives: 19.4 us -> none
  transfers between devices with their start and end apart: 18 -> 0, of which waited for: 15 -> 0; matrix products, arithmetic and copies ran while one was open for 4% -> 0% of each run, Pallas kernels for 3% -> 0%
where the time goes in v2:
time: 473 us; the launch traced here: 464 us
  Pallas kernels  444 us (94%)
  local copies, waits for them, and re-layouts  11.3 us (2%)
  other arithmetic  8 us (2%)
    pallas_call x2, Pallas kernels, layer_backward(): pl.pallas_call(partial(backward_kernel, dims + (bits, layer)), grid=(grou...  237 us
    pallas_call x2, Pallas kernels, layer_forward(): pl.pallas_call(partial(forward_kernel, dims + (bits, layer, gathers)), gr...  127 us
    pallas_call x1, Pallas kernels, gather_first(): pl.pallas_call(partial(gather_kernel, dims), in_specs=[pl.BlockSpec(memor...  79.8 us

profile of v2, /device:TPU:0, one launch (start us, length us, event | category | flops | bytes accessed | tf_op | source)
XLA Modules:
  0.0 464.0 jit_solution(15398441544697352350)
XLA Ops:
  0.7 1.4 fusion.3
  2.2 0.9 pad_maximum_fusion.2
  3.2 0.7 copy.47.dt
  3.9 79.8 %gather_first.1 = (bf16[2,2,2,4,3,128,512]{6,5,4,3,2,1,0:T(8,128)(2,1)}, f32[512,1024]{1,0:T(8,128)}, f32[512,1024]{1,0:T(8,128)}, bf16[2,2,2,128,384]{4,3,2,1,0...) custom-call(s32[1,4]{1,0:T(1,128)} %starts.1, ...), custom_call_target="tpu_custom_call" | custom-call | tf_op jit(solution)/shard_map/gather_first/pallas_call | solution.py:1313
  83.7 88.5 %layer_forward.2 = (f32[512,1024]{1,0:T(8,128)}, bf16[1024,512]{1,0:T(8,128)(2,1)}, bf16[1024,16]{1,0:T(8,128)(2,1)}, f32[8,512,256]{2,1,0:T(8,128)}, f32[8,528,...) custom-call(f32[512,1024]{1,0:T(8,128)} %get-tuple-element.57.x_ref,, ...), custom_call_target="tpu_custom_call" | custom-call | tf_op jit(solution)/shard_map/layer_forward/pallas_call | solution.py:889
  172.2 38.2 %layer_forward.3 = (f32[512,1024]{1,0:T(8,128)}, bf16[1024,512]{1,0:T(8,128)(2,1)}, bf16[1024,16]{1,0:T(8,128)(2,1)}, f32[8,512,256]{2,1,0:T(8,128)}, f32[8,528,...) custom-call(f32[512,1024]{1,0:T(8,128)} %get-tuple-element.67.x_ref., ...), custom_call_target="tpu_custom_call" | custom-call | tf_op jit(solution)/shard_map/layer_forward/pallas_call | solution.py:889
  210.4 120.0 %layer_backward.2 = (f32[512,1024]{1,0:T(8,128)}, f32[3,128,512]{2,1,0:T(8,128)}, f32[128,384]{1,0:T(8,128)}, f32[80,256]{1,0:T(8,128)}) custom-call(f32[512,1024]{1,0:T(8,128)} %get-tuple-element.71.g_ref, f32[512,1024]{1,0:T(8,128)} %get-tuple-element.67.x_ref.next_ref, f32[512,1024]{1,0:T(8,128)} %get-tuple-element.70.next_ref, f32[2,1024]{1,0:T(2,128)} %gain_ref.7, ...), custom_call_target="tpu_custom_call" | custom-call | tf_op jit(solution)/shard_map/layer_backward/pallas_call | solution.py:969
  330.4 117.2 %layer_backward.3 = (f32[512,1024]{1,0:T(8,128)}, f32[3,128,512]{2,1,0:T(8,128)}, f32[128,384]{1,0:T(8,128)}, f32[80,256]{1,0:T(8,128)}) custom-call(f32[512,1024]{1,0:T(8,128)} %get-tuple-element.82.g_ref, f32[512,1024]{1,0:T(8,128)} %get-tuple-element.57.x_ref, f32[512,1024]{1,0:T(8,128)} %get-tuple-element.67.x_ref.next_ref, f32[2,1024]{1,0:T(2,128)} %gain_ref.7, ...), custom_call_target="tpu_custom_call" | custom-call | tf_op jit(solution)/shard_map/layer_backward/pallas_call | solution.py:969
  447.6 0.8 pad_maximum_fusion.6
  449.8 0.9 fusion
  450.8 0.7 reduce_sum.9
  451.5 0.6 copy.67
  452.1 0.6 copy.68
  452.7 0.6 slice.108
  453.3 1.3 fusion.1
  454.6 0.6 copy.59
  455.2 1.0 slice.92
  456.2 0.8 pad_maximum_fusion.1
  457.2 0.6 pad_maximum_fusion.5
  457.9 0.7 pad_maximum_fusion.4
  458.8 1.8 copy.52
  460.6 1.1 convert_element_type.4
  461.7 0.8 copy-done.1
  462.5 1.3 copy.71
  (40 shorter events, 2.0 us)
Async XLA Ops:
  0.6 1.5 copy-start.5
  0.7 2.5 copy-start.8
  330.4 117.2 %copy-start.4 = (f32[80,256]{1,0:T(8,128)S(1)}, f32[80,256]{1,0:T(8,128)}, u32[]{:S(2)}) copy-start(f32[80,256]{1,0:T(8,128)} %get-tuple-element.98) | copy-start | bytes 245764
  330.4 125.8 %copy-start.2 = (f32[3,128,512]{2,1,0:T(8,128)S(1)}, f32[3,128,512]{2,1,0:T(8,128)}, u32[]{:S(2)}) copy-start(f32[3,128,512]{2,1,0:T(8,128)} %get-tuple-element.94) | copy-start | bytes 2359300
  447.6 9.5 %copy-start.7 = (f32[128,384]{1,0:T(8,128)S(1)}, f32[128,384]{1,0:T(8,128)}, u32[]{:S(2)}) copy-start(f32[128,384]{1,0:T(8,128)} %get-tuple-element.95) | copy-start | bytes 589828
  447.6 9.5 %copy-start.6 = (f32[128,384]{1,0:T(8,128)S(1)}, f32[128,384]{1,0:T(8,128)}, u32[]{:S(2)}) copy-start(f32[128,384]{1,0:T(8,128)} %get-tuple-element.96) | copy-start | bytes 589828
  449.8 8.8 %copy-start.3 = (f32[3,128,512]{2,1,0:T(8,128)S(1)}, f32[3,128,512]{2,1,0:T(8,128)}, u32[]{:S(2)}) copy-start(f32[3,128,512]{2,1,0:T(8,128)} %get-tuple-element.93) | copy-start | bytes 2359300
  458.7 1.9 copy-start
  460.6 2.0 copy-start.1

commit v3 on v2

--- a/solution.py
+++ b/solution.py
@@ -18,10 +18,8 @@
 STATE = 128
 NEG = -1e30
 SLOTS = 2
-VMEM_LIMIT = 58 * 1024 * 1024
+VMEM_LIMIT = 60 * 1024 * 1024
 VMEM_LIMIT_FORWARD = 62 * 1024 * 1024
-STEP_US = 3.2
-TICK = 1.3
 MESH = pl.DeviceIdType.MESH
 HI = lax.Precision.HIGHEST
 F32 = jnp.float32
@@ -146,7 +144,9 @@
 ):
     pieces, groups, tokens, skew, bits, layer, gathers = dims
     if gathers:
-        few_mine, mine_ref, *rest = rest
+        few_mine, _, *rest = rest
+    if layer:
+        rest = rest[9:]
     next_ref, nxt_ref, nht_ref, gate_ref, val_ref, y_ref, state_ref, shared_ref, step_ref, r_ref, *rest = rest
     if gathers:
         few_out, wall_ref, *rest = rest
@@ -172,12 +172,14 @@
             send_sem=send.at[group], recv_sem=recv.at[group], device_id={"tensor": right}, device_id_type=MESH,
         )
 
-    gather = Gather(place, z, pieces, mine_ref, wall_ref, few_mine, few_z, few_all, *rest) if gathers else None
-    steps_all = groups + skew
-    plan = [[] for _ in range(steps_all)]
+    plan = [[] for _ in range(groups + skew)]
     if gathers:
-        for when, act in gather.events():
-            plan[min(int((when * TICK + 3.0) / STEP_US), steps_all - 1)].append(act)
+        plane = Plane(place, z, pieces, None, wall_ref, few_mine, few_z, few_all, *rest)
+        for step in range(1, bits + 1):
+            for p in range(pieces):
+                plan[min(4 * step + p - 2, groups + skew - 1)].append(partial(plane.double, p, step))
+        for step in range(bits + 1):
+            plan[min(2 * step + 1, groups + skew - 1)].append(partial(plane.few_event, step))
 
     @pl.when(i == 0)
     def _():
@@ -192,7 +194,9 @@
             halo_copy().start()
 
         if gathers:
-            gather.start()
+            for p in range(pieces):
+                plane.start(p)
+            plane.start_few()
 
         @pl.when(z == 0)
         def _():
@@ -200,7 +204,7 @@
             incoming[...] = jnp.zeros(incoming.shape, BF)
 
         depth = nx.shape[1]
-        step_in = dot_nn(nx[pl.ds(HALO, tokens), :], few_ref[:, :, 2 * STATE :].reshape(depth, LANES))
+        step_in = dot_nn(nx[pl.ds(HALO, tokens), :], few_ref[..., 2 * STATE :].reshape(depth, LANES))
         step_ref[...] = step_in
         _, steps, _, summed, toward, reach, kept = step_terms(
             step_in, heads_ref, carried_ref, tail_ref, kept_ref, tokens
@@ -217,7 +221,7 @@
         def _():
             halo_copy().wait_recv()
 
-        shared_ref[...] = dot_nn(nx[...], few_ref[:, :, : 2 * STATE].reshape(depth, 2 * STATE))
+        shared_ref[...] = dot_nn(nx[...], few_ref[..., : 2 * STATE].reshape(depth, 2 * STATE))
         taps = shared_taps(csw_ref, csb_ref, layer)
         mixed = conv(lambda k: shared_ref[pl.ds(HALO - k, tokens), :], keep_ref, taps, tokens)
         maps = mixed * sigmoid(mixed)
@@ -314,7 +318,7 @@
         nxt_ref[...] = nx[pl.ds(HALO, tokens), :].T
         nht_ref[...] = nx[pl.ds(0, HALO), :].T
         if gathers:
-            gather.finish()
+            plane.finish()
             few_out[...] = few_all[...]
 
         @pl.when(z < pieces - 1)
@@ -363,19 +367,23 @@
 
 def backward_kernel(
     dims,
-    g_ref, x_ref, next_ref, gain_ref, nxt, nht, r_ref, wa, wb, oa, ob, few_ref, pa, pb, qa, qb, rows_ref,
-    csw_ref, csb_ref, keep_ref, biast_ref, carried_ref, tail_ref, kept_ref,
-    gate_ref, val_ref, y_ref, valb_ref, yb_ref, state_ref, shared_ref, step_ref,
-    gx_ref, gw_ref, gm_ref, small_ref,
-    gb, gbt, r2, inb, outb, outbt, crosst, col, row, terms, ke,
-    dys, xs, fs, dgs, fold, incoming, outgoing, gnorm, dct, dbt, dgt, sd, sp, sq, se, dxd, hrecv,
-    own, own_m, got_z, got_m, halo_send, halo_recv, send, recv, sum_send, sum_recv, z_send, z_recv,
-    msum_send, msum_recv, mz_send, mz_recv, next_sem, load_sem, heads_ref,
-    few_total, few_got, few_z, few_send, few_recv, fz_send, fz_recv, *got,
+    g_ref, *refs,
 ):
-    pieces, groups, tokens, skew, bits, layer = dims
+    pieces, groups, tokens, skew, bits = dims
+    line_refs, refs = refs[: LAYERS + 1], refs[LAYERS + 1 :]
+    weights, refs = [refs[5 * n : 5 * n + 5] for n in range(LAYERS)], refs[5 * LAYERS :]
+    gain_ref, nxt, nht, r_ref, pa, pb, qa, qb, rows_ref, *refs = refs
+    csw_ref, csb_ref, keep_ref, biast_ref, carried_ref, tail_ref, kept_ref, *refs = refs
+    gate_ref, val_ref, y_ref, valb_ref, state_ref, shared_ref, step_ref, *refs = refs
+    gx_ref, gw_ref, gm_ref, small_ref, mid_ref, *refs = refs
+    gb, gbt, r2, inb, outb, outbt, crosst, col, row, terms, ke, *refs = refs
+    dys, xs, fs, dgs, fold, incoming, outgoing, gnorm, dct, dbt, dgt, sd, sp, sq, se, dxd, hrecv, *refs = refs
+    own, own_m, got_z, got_m, halo_send, halo_recv, send, recv, sum_send, sum_recv, z_send, z_recv, *refs = refs
+    msum_send, msum_recv, mz_send, mz_recv, next_sem, load_sem, heads_ref, *refs = refs
+    few_total, few_got, few_z, few_send, few_recv, fz_send, fz_recv, *got = refs
     chunks = tokens // CH
-    i = pl.program_id(0)
+    phase, i = pl.program_id(0), pl.program_id(1)
+    layer = LAYERS - 1 - phase
     z = lax.axis_index("tensor")
     right, left = jnp.minimum(z + 1, pieces - 1), jnp.maximum(z - 1, 0)
     back = pieces - 1 - z
@@ -384,14 +392,14 @@
 
     def halo_copy():
         return pltpu.make_async_remote_copy(
-            src_ref=gnorm, dst_ref=hrecv,
-            send_sem=halo_send, recv_sem=halo_recv, device_id={"tensor": left}, device_id_type=MESH,
+            src_ref=gnorm, dst_ref=hrecv.at[phase], send_sem=halo_send, recv_sem=halo_recv.at[phase],
+            device_id={"tensor": left}, device_id_type=MESH,
         )
 
     def state_copy(group):
         return pltpu.make_async_remote_copy(
-            src_ref=outgoing.at[group], dst_ref=incoming.at[group],
-            send_sem=send.at[group], recv_sem=recv.at[group], device_id={"tensor": left}, device_id_type=MESH,
+            src_ref=outgoing.at[group], dst_ref=incoming.at[phase, group],
+            send_sem=send.at[group], recv_sem=recv.at[phase, group], device_id={"tensor": left}, device_id_type=MESH,
         )
 
     place = Place(bits)
@@ -411,15 +419,15 @@
             device_id={"dp": place.partner(half, step)}, device_id_type=MESH,
         )
 
-    def z_copy(group, half):
-        column = group // (pieces // 2)
+    def z_copy(group, half, turn):
+        column = lax.div(group, pieces // 2)
         return pltpu.make_async_remote_copy(
             src_ref=own.at[(group,) + place.mine() + (slice(None), slice(None), pl.ds(half * LANES, LANES))],
-            dst_ref=got_z.at[z, column], send_sem=z_send.at[group, half], recv_sem=z_recv.at[z, column],
+            dst_ref=got_z.at[turn, z, column], send_sem=z_send.at[group, half], recv_sem=z_recv.at[turn, z, column],
             device_id={"tensor": quarter(group, half, pieces)}, device_id_type=MESH,
         )
 
-    def advance(group, step):
+    def advance(group, step, turn):
         @pl.when(jnp.logical_and(group >= 0, group < groups))
         def _():
             for half in range(2):
@@ -433,7 +441,7 @@
 
                     @pl.when(quarter(group, half, pieces) != z)
                     def _(half=half):
-                        z_copy(group, half).start()
+                        z_copy(group, half, turn).start()
 
     def misc_copy(step):
         return pltpu.make_async_remote_copy(
@@ -442,13 +450,14 @@
             device_id={"dp": place.partner(False, step)}, device_id_type=MESH,
         )
 
-    def misc_z(k):
+    def misc_z(k, turn, source):
         return pltpu.make_async_remote_copy(
-            src_ref=own_m.at[place.mine()], dst_ref=got_m.at[z], send_sem=mz_send.at[k], recv_sem=mz_recv.at[z],
+            src_ref=own_m.at[place.mine()], dst_ref=got_m.at[turn, source], send_sem=mz_send.at[k],
+            recv_sem=mz_recv.at[turn, source],
             device_id={"tensor": lax.rem(z + k, pieces)}, device_id_type=MESH,
         )
 
-    def misc_advance(step):
+    def misc_advance(step, turn):
         if step:
             misc_copy(step - 1).wait_recv()
             at = place.region(False, step - 1, True)
@@ -457,13 +466,13 @@
             misc_copy(step).start()
         else:
             for k in range(1, pieces):
-                misc_z(k).start()
-            got_m[z] = own_m[place.mine()]
-
-    def drain(late):
+                misc_z(k, turn, z).start()
+            got_m[turn, z] = own_m[place.mine()]
+
+    def drain(late, turn):
         for step in reversed(range(1, bits + 1)):
             if late <= step:
-                advance(groups - 1 + late - step, step)
+                advance(jnp.int32(groups - 1 + late - step), step, turn)
 
     def few_copy(step):
         return pltpu.make_async_remote_copy(
@@ -471,13 +480,14 @@
             recv_sem=few_recv.at[step], device_id={"dp": place.partner(False, step)}, device_id_type=MESH,
         )
 
-    def few_line(k, source):
+    def few_line(k, turn, source):
         return pltpu.make_async_remote_copy(
-            src_ref=few_total.at[bits], dst_ref=few_z.at[source], send_sem=fz_send.at[k], recv_sem=fz_recv.at[source],
+            src_ref=few_total.at[bits], dst_ref=few_z.at[turn, source], send_sem=fz_send.at[k],
+            recv_sem=fz_recv.at[turn, source],
             device_id={"tensor": lax.rem(z + k, pieces)}, device_id_type=MESH,
         )
 
-    def few_advance(step):
+    def few_advance(step, turn):
         if step:
             few_copy(step - 1).wait_recv()
             few_total[step] = few_total[step - 1] + few_got[step - 1]
@@ -485,37 +495,112 @@
             few_copy(step).start()
         else:
             for k in range(1, pieces):
-                few_line(k, z).start()
-            few_z[z] = few_total[bits]
-
-    def load_blocks():
+                few_line(k, turn, z).start()
+            few_z[turn, z] = few_total[bits]
+
+    def finish_few(turn):
+        for n in range(1, pieces):
+            few_line(n, turn, lax.rem(z + n, pieces)).wait_recv()
+            misc_z(n, turn, lax.rem(z + n, pieces)).wait_recv()
+        total, misc = few_z[turn, 0], got_m[turn, 0].astype(F32)
+        for source in range(1, pieces):
+            total = total + few_z[turn, source]
+            misc = misc + got_m[turn, source].astype(F32)
+        small_ref[LAYERS - 1 - turn] = total
+        gm_ref[LAYERS - 1 - turn] = misc
+        for step in range(bits):
+            misc_copy(step).wait_send()
+            few_copy(step).wait_send()
+        for n in range(1, pieces):
+            misc_z(n, turn, z).wait_send()
+            few_line(n, turn, z).wait_send()
+
+    def finish_group(group, turn):
+        column = lax.div(group, pieces // 2)
+        for half in range(2):
+
+            @pl.when(quarter(group, half, pieces) == z)
+            def _(half=half):
+                total = own[(group,) + place.mine() + (slice(None), slice(None), pl.ds(half * LANES, LANES))]
+                total = total.astype(F32)
+                for n in range(1, pieces):
+                    source = lax.rem(z + n, pieces)
+                    pltpu.make_async_remote_copy(
+                        src_ref=got_z.at[turn, source, column], dst_ref=got_z.at[turn, source, column],
+                        send_sem=z_send.at[group, half], recv_sem=z_recv.at[turn, source, column],
+                        device_id={"tensor": source}, device_id_type=MESH,
+                    ).wait_recv()
+                    total = total + got_z[turn, source, column].astype(F32)
+                at = pl.multiple_of(column * LANES, LANES)
+                gw_ref[LAYERS - 1 - turn, :, :, pl.ds(at, LANES)] = total
+
+            @pl.when(quarter(group, half, pieces) != z)
+            def _(half=half):
+                z_copy(group, half, turn).wait_send()
+
+            for step in range(bits):
+                sum_copy(group, step, half).wait_send()
+
+    def load(x, g):
         found = []
-        for k in range(depth // GC):
-            cols = pl.ds(k * GC, GC)
-            found.append(pltpu.make_async_copy(x_ref.at[:, cols], xs.at[k], load_sem.at[0, k]))
-            found.append(pltpu.make_async_copy(g_ref.at[:, cols], fs.at[k], load_sem.at[1, k]))
+        for n in range(depth // GC):
+            cols = pl.ds(n * GC, GC)
+            found.append(pltpu.make_async_copy(x.at[:, cols], xs.at[n], load_sem.at[0, n]))
+            if g is not None:
+                found.append(pltpu.make_async_copy(g.at[:, cols], fs.at[n], load_sem.at[1, n]))
         return found
 
+    def of_layer(pick):
+        chosen = pick(0)
+        for n in range(1, LAYERS):
+            chosen = jnp.where(layer == n, pick(n), chosen)
+        return chosen
+
+    def out_weights():
+        return of_layer(lambda n: side(weights[n][2:4], 0))
+
+    def in_weights(which):
+        return of_layer(lambda n: side(weights[n][:2], which))
+
     def taps():
-        return shared_taps(csw_ref, csb_ref, layer)
+        return jnp.concatenate([csw_ref[layer], csb_ref[pl.ds(layer, 1), :]], axis=0)
 
     def shared_conv():
         return conv(lambda k: shared_ref[pl.ds(HALO - k, tokens), :], keep_ref, taps(), tokens)
 
-    @pl.when(i == 0)
+    @pl.when(jnp.logical_and(phase == 0, i == 0))
     def _():
         greet(place, z, pieces)
-        put_heads(rows_ref, heads_ref)
 
         @pl.when(z == pieces - 1)
         def _():
             incoming[...] = jnp.zeros(incoming.shape, BF)
 
-        copies = [pltpu.make_async_copy(next_ref, gx_ref, next_sem)] + load_blocks()
+        copies = [pltpu.make_async_copy(line_refs[LAYERS], gx_ref, next_sem)] + load(line_refs[LAYERS - 1], g_ref)
         for copy in copies:
             copy.start()
         for copy in copies:
             copy.wait()
+
+    for turn in range(1, LAYERS):
+
+        @pl.when(jnp.logical_and(phase == turn, i == 0))
+        def _(turn=turn):
+            copies = load(line_refs[LAYERS - 1 - turn], None)
+            copies.append(pltpu.make_async_copy(gx_ref, mid_ref, next_sem))
+            for copy in copies:
+                copy.start()
+            for n in range(depth // GC):
+                fs[n] = gx_ref[:, n * GC : (n + 1) * GC]
+            for copy in copies:
+                copy.wait()
+            copy = pltpu.make_async_copy(line_refs[LAYERS - turn], gx_ref, next_sem)
+            copy.start()
+            copy.wait()
+
+    @pl.when(i == 0)
+    def _():
+        put_heads(rows_ref, heads_ref)
         dots = jnp.zeros((tokens, 1), F32)
         for k in range(depth // GC):
             cols = slice(k * GC, (k + 1) * GC)
@@ -556,7 +641,14 @@
         xs[slot] = x
         fs[slot] = part + x * (1.0 - part)
         r = twice(r_ref[...])
-        gm = dot_nn(gb[...], side((oa, ob), 0))
+
+        for turn in range(1, LAYERS):
+
+            @pl.when(phase == turn)
+            def _(turn=turn):
+                finish_group(group, turn - 1)
+
+        gm = dot_nn(gb[...], out_weights())
         scan = y_ref[0] + gp[6:7] * x
         gate = gate_ref[0]
         part = sigmoid(gate)
@@ -570,7 +662,7 @@
         dy = ggated * silu
         dys[slot] = dy.astype(BF)
         dgs[slot] = (ggated * scan * (part + silu * (1.0 - part))).astype(BF)
-        small_ref[pl.ds(group * 8, 8), :] = jnp.concatenate(
+        small_ref[layer, pl.ds(group * 8, 8), :] = jnp.concatenate(
             [
                 jnp.zeros((5, GC), F32),
                 jnp.sum(gm * normal, axis=0, keepdims=True),
@@ -579,15 +671,31 @@
             ],
             axis=0,
         )
-        spreader = spread(group)
+        spreader, collector = spread(group), collect(group)
         state = jnp.zeros((STATE, GC), F32)
         for c in reversed(range(chunks)):
             rows = pl.ds(c * CH, CH)
             reached = (dys[slot, rows, :].astype(F32) * dot_nn(terms[2, rows, :], spreader)).astype(BF)
+            sp[rows, :] += dot_nn(split2(dys[slot, rows, :].astype(F32) * y_ref[0, rows, :]), collector)
             new = dot_nn(outbt[c], reached)
             state = ke[group, c : c + 1] * state + new
         fold[slot] = state
 
+    for turn in range(1, LAYERS):
+        for late in range(1, max(bits, skew) + 1):
+            place_at = min(late, skew) - 1
+
+            @pl.when(jnp.logical_and(phase == turn, i == place_at))
+            def _(turn=turn, late=late):
+                drain(late, turn - 1)
+                if late <= bits:
+                    few_advance(late, turn - 1)
+                    misc_advance(late, turn - 1)
+
+        @pl.when(jnp.logical_and(phase == turn, i == skew))
+        def _(turn=turn):
+            finish_few(turn - 1)
+
     j = i - back
 
     @pl.when(jnp.logical_and(j >= 0, j < groups))
@@ -601,7 +709,7 @@
             total = ke[j, 0:1]
             for c in range(1, chunks):
                 total = total * ke[j, c : c + 1]
-            outgoing[j] = (total * incoming[j].astype(F32) + fold[lax.rem(j, skew + 1)]).astype(BF)
+            outgoing[j] = (total * incoming[phase, j].astype(F32) + fold[lax.rem(j, skew + 1)]).astype(BF)
             state_copy(j).start()
 
     @pl.when(i >= skew)
@@ -611,7 +719,7 @@
         gp = side_params((qa, qb))
         spreader, collector = spread(group), collect(group)
         turn_sums(col, group)
-        grad = incoming[group].astype(F32)
+        grad = incoming[phase, group].astype(F32)
         ends = [None] * chunks
         for c in reversed(range(chunks)):
             rows = pl.ds(c * CH, CH)
@@ -647,19 +755,19 @@
             dgt[c] += pairs_total
             within = jnp.concatenate(parts, axis=1)
             whole = within + later
-            lowered = dy * yb_ref[0, rows, :] - sized.astype(BF).astype(F32) * within
+            lowered = sized.astype(BF).astype(F32) * within
             sd[rows, :] += dot_nn(split2(whole * x), collector)
-            sp[rows, :] += dot_nn(split2(lowered), collector)
+            sp[rows, :] -= dot_nn(split2(lowered), collector)
             sq[rows, :] += dot_nn(split2(sized * later), collector)
             dxd[rows, :] = (whole * steps + gp[6:7] * dy) * fs[slot, rows, :]
         for step in reversed(range(1, bits + 1)):
-            advance(group - step, step)
+            advance(group - step, step, phase)
         ends.append(jnp.zeros((8 - chunks, GC), F32))
         se[...] += dot_nn(split2(jnp.concatenate(ends, axis=0)), collector)
         wide, sums = conv_back(
             dxd[...], lambda k: valb_ref[0, pl.ds(HALO - k, tokens), :], keep_ref, gp, tokens
         )
-        small_ref[pl.ds(group * 8, 8), :] += jnp.concatenate(sums + [jnp.zeros((3, GC), F32)], axis=0)
+        small_ref[layer, pl.ds(group * 8, 8), :] += jnp.concatenate(sums + [jnp.zeros((3, GC), F32)], axis=0)
         wide = wide.astype(BF)
         dgate = dgs[slot]
         shape = place.dims + (-1, GC)
@@ -667,15 +775,21 @@
         own[(group,) + place.all + (1,)] = (
             (dot_nn(nxt[...], wide[HALO:]) + dot_nn(nht[...], wide[:HALO])).astype(BF).reshape(shape)
         )
-        advance(group, 0)
-        back_wide = dot_nt(wide, side((wa, wb), 1))
+        advance(group, 0, phase)
+        back_wide = dot_nt(wide, in_weights(1))
         gnorm[...] += back_wide[:HALO]
-        gx_ref[...] += back_wide[HALO:] + dot_nt(dgate, side((wa, wb), 0))
+        gx_ref[...] += back_wide[HALO:] + dot_nt(dgate, in_weights(0))
 
     @pl.when(i == groups + skew - 1)
     def _():
-        for copy in load_blocks():
-            copy.start()
+        for turn in range(LAYERS):
+
+            @pl.when(phase == turn)
+            def _(turn=turn):
+                for copy in load(line_refs[LAYERS - 1 - turn], mid_ref if turn else g_ref):
+                    copy.start()
+                pltpu.make_async_copy(weights[LAYERS - 1 - turn][4], own_m, next_sem).start()
+
         upper = (iota2((CH, CH), 0) <= iota2((CH, CH), 1)).astype(F32)
         before = (iota2((CH, CH), 0) > iota2((CH, CH), 1)).astype(F32)
         raw, steps, rates, _, _, _, _ = step_terms(step_ref[...], heads_ref, carried_ref, tail_ref, kept_ref, tokens)
@@ -696,107 +810,54 @@
         part = sigmoid(mixed)
         dmixed = jnp.concatenate(dmaps, axis=0) * (part + mixed * part * (1.0 - part))
         wide, sums = conv_back(dmixed, lambda k: shared_ref[pl.ds(HALO - k, tokens), :], keep_ref, taps(), tokens)
-        small_ref[pl.ds(groups * 8, 8), :] = jnp.concatenate(sums + [jnp.zeros((3, 2 * STATE), F32)], axis=0)
+        small_ref[layer, pl.ds(groups * 8, 8), :] = jnp.concatenate(sums + [jnp.zeros((3, 2 * STATE), F32)], axis=0)
         wide = wide.astype(BF)
         dstep = dstep.astype(BF)
-        back_wide = dot_nt(wide, few_ref[:, :, : 2 * STATE].reshape(depth, 2 * STATE))
+        pltpu.make_async_copy(weights[0][4], own_m, next_sem).wait()
+        back_wide = dot_nt(wide, own_m[..., : 2 * STATE].reshape(depth, 2 * STATE))
         gnorm[...] += back_wide[:HALO]
 
         @pl.when(z > 0)
         def _():
             halo_copy().start()
 
-        gx_ref[...] += back_wide[HALO:] + dot_nt(dstep, few_ref[:, :, 2 * STATE :].reshape(depth, LANES))
-        drain(1)
+        gx_ref[...] += back_wide[HALO:] + dot_nt(dstep, own_m[..., 2 * STATE :].reshape(depth, LANES))
+        at_end = phase == LAYERS - 1
+
+        @pl.when(at_end)
+        def _():
+            drain(1, LAYERS - 1)
+
         misc = jnp.concatenate(
             [dot_nn(nxt[...], wide[HALO:]) + dot_nn(nht[...], wide[:HALO]), dot_nn(nxt[...], dstep)], axis=1
         )
         own_m[...] = misc.astype(BF).reshape(own_m.shape)
-        misc_advance(0)
+        misc_advance(0, phase)
 
         @pl.when(z < pieces - 1)
         def _():
             halo_copy().wait_recv()
-            gx_ref[pl.ds(tokens - HALO, HALO), :] += hrecv[...]
-
-        for copy in load_blocks():
+            gx_ref[pl.ds(tokens - HALO, HALO), :] += hrecv[phase]
+
+        for copy in load(line_refs[0], g_ref):
             copy.wait()
         blocks = [(k, slice(k * GC, (k + 1) * GC)) for k in range(depth // GC)]
+        gain = gain_ref[pl.ds(layer, 1), :]
         power = inside = jnp.zeros((tokens, 1), F32)
         for k, cols in blocks:
             power = power + jnp.sum(xs[k] * xs[k], axis=1, keepdims=True)
-            gained = gx_ref[:, cols] * gain_ref[layer : layer + 1, cols]
+            gained = gx_ref[:, cols] * gain[:, cols]
             inside = inside + jnp.sum(gained * xs[k], axis=1, keepdims=True)
         q = lax.rsqrt(power * (1.0 / depth) + EPS)
         inside = inside * (q * q * q) * (1.0 / depth)
         cuts = [jnp.sum(gx_ref[:, cols] * xs[k] * q, axis=0, keepdims=True) for k, cols in blocks]
-        few_total[0, pl.ds(0, groups * 8 + 8), :] = small_ref[pl.ds(0, groups * 8 + 8), :]
+        few_total[0, pl.ds(0, groups * 8 + 8), :] = small_ref[layer, pl.ds(0, groups * 8 + 8), :]
         few_total[0, pl.ds(groups * 8 + 8, 8), :] = jnp.concatenate(
             cuts + [head_sums, jnp.zeros((7 - len(cuts), GC), F32)], axis=0
         )
-        few_advance(0)
-        misc_advance(1)
+        few_advance(0, phase)
         for k, cols in blocks:
-            gx_ref[:, cols] = fs[k] + q * (gx_ref[:, cols] * gain_ref[layer : layer + 1, cols]) - xs[k] * inside
-        for step in range(2, bits + 1):
-            drain(step)
-            few_advance(step - 1)
-            misc_advance(step)
-        few_advance(bits)
-        for k in range(1, pieces):
-            few_line(k, lax.rem(z + k, pieces)).wait_recv()
-        total = few_z[0]
-        for source in range(1, pieces):
-            total = total + few_z[source]
-        small_ref[...] = total
-        for k in range(1, pieces):
-            source = lax.rem(z + k, pieces)
-            pltpu.make_async_remote_copy(
-                src_ref=own_m.at[place.mine()], dst_ref=got_m.at[source], send_sem=mz_send.at[k],
-                recv_sem=mz_recv.at[source], device_id={"tensor": source}, device_id_type=MESH,
-            ).wait_recv()
-        total = got_m[0].astype(F32)
-        for source in range(1, pieces):
-            total = total + got_m[source].astype(F32)
-        gm_ref[...] = total
-        upper_half = z >= pieces // 2
-        first = jnp.where(upper_half, pieces - 1 - z, z)
-        for column in range(groups // (pieces // 2)):
-            group = first + column * (pieces // 2)
-            for k in range(1, pieces):
-                source = lax.rem(z + k, pieces)
-                pltpu.make_async_remote_copy(
-                    src_ref=got_z.at[source, column], dst_ref=got_z.at[source, column],
-                    send_sem=z_send.at[0, 0], recv_sem=z_recv.at[source, column],
-                    device_id={"tensor": source}, device_id_type=MESH,
-                ).wait_recv()
-            for half in range(2):
-
-                @pl.when(upper_half if half else jnp.logical_not(upper_half))
-                def _(half=half, group=group, column=column):
-                    total = own[(group,) + place.mine() + (slice(None), slice(None), pl.ds(half * LANES, LANES))]
-                    total = total.astype(F32)
-                    for k in range(1, pieces):
-                        total = total + got_z[lax.rem(z + k, pieces), column].astype(F32)
-                    gw_ref[:, :, column * LANES : (column + 1) * LANES] = total
-
-        for group in range(groups):
-            for step in range(bits):
-                for half in range(2):
-                    sum_copy(group, step, half).wait_send()
-
-            for half in range(2):
-
-                @pl.when(quarter(group, half, pieces) != z)
-                def _(group=group, half=half):
-                    z_copy(group, half).wait_send()
-
-        for step in range(bits):
-            misc_copy(step).wait_send()
-            few_copy(step).wait_send()
-        for k in range(1, pieces):
-            misc_z(k).wait_send()
-            few_line(k, z).wait_send()
+            gx_ref[:, cols] = fs[k] + q * (gx_ref[:, cols] * gain[:, cols]) - xs[k] * inside
 
         @pl.when(z > 0)
         def _():
@@ -804,13 +865,26 @@
             for group in range(groups):
                 state_copy(group).wait_send()
 
+        @pl.when(at_end)
+        def _():
+            turn = LAYERS - 1
+            misc_advance(1, turn)
+            for step in range(2, bits + 1):
+                drain(step, turn)
+                few_advance(step - 1, turn)
+                misc_advance(step, turn)
+            few_advance(bits, turn)
+            finish_few(turn)
+            for group in range(groups):
+                finish_group(jnp.int32(group), turn)
+
 
 def whole(shape):
     return pl.BlockSpec(shape, lambda i: (0,) * len(shape), pipeline_mode=pl.Buffered(1))
 
 
 def quarter(group, half, pieces):
-    at = group % (pieces // 2)
+    at = lax.rem(group, pieces // 2) if pieces > 2 else 0 * group
     return pieces - 1 - at if half else at
 
 
@@ -832,7 +906,7 @@
         return [make(0), make(1)]
 
     def column(i, at):
-        return at(i) // (pieces // 2)
+        return lax.div(at(i), pieces // 2)
 
     def pair(at):
         return both(
@@ -871,21 +945,32 @@
     return pl.BlockSpec(shape, lambda i: place, pipeline_mode=pl.Buffered(1))
 
 
-def layer_forward(dims, bits, layer, x, gain, w, few, pack, csw, csb, masks, later):
+def layer_forward(dims, bits, layer, x, gain, w, few, pack, csw, csb, masks, later, earlier):
     pieces, groups, tokens, skew = dims
     keep, bias, _, carried, tail, kept = masks
     chunks = tokens // CH
     depth = x.shape[1]
     ext = tokens + HALO
     slots = skew + 1
-    early, late, block, pair, single, params = group_specs(dims, w.shape)
+    early, late, _, pair, single, params = group_specs(dims, w.shape)
+
+    def block(rows, at):
+        return pl.BlockSpec((None, 1, rows, GC), lambda i: (layer, at(i), 0, 0))
+
+    def mine(shape):
+        return fixed((None,) + shape, (layer,) + (0,) * len(shape))
+
     anywhere = pl.BlockSpec(memory_space=pl.ANY)
     near = pl.BlockSpec(memory_space=pltpu.VMEM)
     gathers = later is not None
     cut = (2,) * bits
-    buffers, sems = gather_scratch(pieces, bits, w.shape[3])
+    buffers, sems = plane_scratch(pieces, bits, w.shape[3])
     if gathers:
         later_few, later = later
+    first = 19 + 2 * gathers
+    aliases = {first + k: 1 + k for k in range(len(earlier))}
+    if gathers:
+        aliases[20] = 11
     return pl.pallas_call(
         partial(forward_kernel, dims + (bits, layer, gathers)),
         grid=(groups + skew,),
@@ -894,26 +979,26 @@
             whole(few.shape), *params(layer, early), *params(layer, late), fixed((pieces, 1, 8, 2 * LANES), (0, layer, 0, 0)),
             whole(csw.shape), whole(csb.shape),
             whole(keep.shape), whole(bias.shape), whole(carried.shape), whole(tail.shape), whole(kept.shape),
-        ] + [near, anywhere] * gathers,
+        ] + [near, anywhere] * gathers + [anywhere] * len(earlier),
         out_specs=[
-            whole((tokens, depth)), whole((depth, tokens)), whole((depth, HALO)),
+            whole((tokens, depth)), mine((depth, tokens)), mine((depth, HALO)),
             block(tokens, early), block(ext, early), block(tokens, late),
-            pl.BlockSpec((1, chunks, STATE, GC), lambda i: (late(i), 0, 0, 0)),
-            whole((ext, 2 * STATE)), whole((tokens, LANES)), whole((tokens, LANES)),
+            pl.BlockSpec((None, 1, chunks, STATE, GC), lambda i: (layer, late(i), 0, 0, 0)),
+            mine((ext, 2 * STATE)), mine((tokens, LANES)), mine((tokens, LANES)),
         ] + [near, anywhere] * gathers,
         out_shape=[
             jax.ShapeDtypeStruct((tokens, depth), F32),
-            jax.ShapeDtypeStruct((depth, tokens), BF),
-            jax.ShapeDtypeStruct((depth, HALO), BF),
-            jax.ShapeDtypeStruct((groups, tokens, GC), F32),
-            jax.ShapeDtypeStruct((groups, ext, GC), F32),
-            jax.ShapeDtypeStruct((groups, tokens, GC), F32),
-            jax.ShapeDtypeStruct((groups, chunks, STATE, GC), BF),
-            jax.ShapeDtypeStruct((ext, 2 * STATE), F32),
-            jax.ShapeDtypeStruct((tokens, LANES), F32),
-            jax.ShapeDtypeStruct((tokens, LANES), F32),
+            jax.ShapeDtypeStruct((LAYERS, depth, tokens), BF),
+            jax.ShapeDtypeStruct((LAYERS, depth, HALO), BF),
+            jax.ShapeDtypeStruct((LAYERS, groups, tokens, GC), F32),
+            jax.ShapeDtypeStruct((LAYERS, groups, ext, GC), F32),
+            jax.ShapeDtypeStruct((LAYERS, groups, tokens, GC), F32),
+            jax.ShapeDtypeStruct((LAYERS, groups, chunks, STATE, GC), BF),
+            jax.ShapeDtypeStruct((LAYERS, ext, 2 * STATE), F32),
+            jax.ShapeDtypeStruct((LAYERS, tokens, LANES), F32),
+            jax.ShapeDtypeStruct((LAYERS, tokens, LANES), F32),
         ] + (
-            [jax.ShapeDtypeStruct(cut + later_few.shape, BF), jax.ShapeDtypeStruct(cut + (pieces,) + later.shape, BF)]
+            [jax.ShapeDtypeStruct(cut + later_few.shape, BF), jax.ShapeDtypeStruct(later.shape, BF)]
             if gathers
             else []
         ),
@@ -942,6 +1027,7 @@
             pltpu.SemaphoreType.DMA((groups,)),
             pltpu.SemaphoreType.DMA((groups,)),
         ] + (buffers + sems if gathers else []),
+        input_output_aliases=aliases,
         compiler_params=pltpu.CompilerParams(
             collective_id=layer, has_side_effects=True, vmem_limit_bytes=VMEM_LIMIT_FORWARD,
             dimension_semantics=("arbitrary",),
@@ -949,45 +1035,90 @@
         name="layer_forward",
     )(
         x, gain, w, w, w, w, few, pack, pack, pack, pack, pack, csw, csb, keep, bias, carried, tail, kept,
-        *([later_few, later] if gathers else []),
+        *([later_few, later] if gathers else []), *earlier,
     )
 
 
-def layer_backward(dims, bits, layer, g, x, after, gain, saved, w, few, pack, csw, csb, masks):
+def layers_backward(dims, bits, g, line, gain, saved, weights, pack, csw, csb, masks):
     pieces, groups, tokens, skew = dims
     keep, _, biast, carried, tail, kept = masks
     nxt, nht, gate, val, y, states, shared, step_in, r = saved
     anywhere = pl.BlockSpec(memory_space=pl.ANY)
     chunks = tokens // CH
-    depth = x.shape[1]
-    _, _, _, share, wide = w.shape
+    depth = g.shape[1]
+    wall = weights[0][0]
+    _, _, _, share, wide = wall.shape
     ext = tokens + HALO
     slots = max(skew + 1, depth // GC)
     few_shape = (groups * 8 + 16, GC)
     halves_of = [(2,) * (bits - 1 - step) for step in range(bits)]
-    early, late, block, pair, single, params = group_specs(dims, w.shape)
+    steps = groups + skew
+    early, late, *_ = group_specs(dims, wall.shape)
+
+    def in_turn(layer, at):
+        turn = LAYERS - 1 - layer
+        return lambda ph, i: at(jnp.where(ph == turn, i, jnp.where(ph < turn, 0, steps - 1)))
+
+    def block(rows, at):
+        return pl.BlockSpec((None, 1, rows, GC), lambda ph, i: (LAYERS - 1 - ph, at(i), 0, 0))
+
+    def of_layer(v):
+        return pl.BlockSpec(
+            (None,) + v.shape[1:], lambda ph, i: (LAYERS - 1 - ph,) + (0,) * (v.ndim - 1),
+            pipeline_mode=pl.Buffered(1),
+        )
+
+    def weight_blocks(count, first, at):
+        def spec(half):
+            def place(ph, i):
+                group = at(ph, i)
+                return 0, quarter(group, half, pieces), first, 0, lax.div(group, pieces // 2)
+
+            return pl.BlockSpec((wall.shape[0], 1, count, share, LANES), place)
+
+        return [spec(half) for half in range(2)]
+
+    def group_params(at):
+        def spec(half):
+            def place(ph, i):
+                group = at(i)
+                return quarter(group, half, pieces), LAYERS - 1 - ph, 0, lax.div(group, pieces // 2)
+
+            return pl.BlockSpec((1, 1, 8, LANES), place)
+
+        return [spec(half) for half in range(2)]
+
+    def whole(shape):
+        return pl.BlockSpec(shape, lambda ph, i: (0,) * len(shape), pipeline_mode=pl.Buffered(1))
+
+    weight_specs, weight_args = [], []
+    for layer in range(LAYERS):
+        w, few = weights[layer]
+        weight_specs += weight_blocks(2, 0, in_turn(layer, late)) + weight_blocks(1, 2, in_turn(layer, early)) + [anywhere]
+        weight_args += [w, w, w, w, few]
     return pl.pallas_call(
-        partial(backward_kernel, dims + (bits, layer)),
-        grid=(groups + skew,),
-        in_specs=[
-            anywhere, anywhere, anywhere, whole(gain.shape),
-            whole(nxt.shape), whole(nht.shape), whole((tokens, LANES)), *pair(late), *single(early),
-            whole(few.shape), *params(layer, early), *params(layer, late), fixed((pieces, 1, 8, 2 * LANES), (0, layer, 0, 0)),
+        partial(backward_kernel, dims + (bits,)),
+        grid=(LAYERS, steps),
+        in_specs=[anywhere] * (LAYERS + 2) + weight_specs + [
+            whole(gain.shape), of_layer(nxt), of_layer(nht), of_layer(r),
+            *group_params(early), *group_params(late),
+            pl.BlockSpec((pieces, 1, 8, 2 * LANES), lambda ph, i: (0, LAYERS - 1 - ph, 0, 0)),
             whole(csw.shape), whole(csb.shape),
             whole(keep.shape), whole(biast.shape), whole(carried.shape), whole(tail.shape), whole(kept.shape),
-            block(tokens, early), block(ext, early), block(tokens, early), block(ext, late), block(tokens, late),
-            pl.BlockSpec((1, chunks, STATE, GC), lambda i: (late(i), 0, 0, 0)),
-            whole((ext, 2 * STATE)), whole((tokens, LANES)),
+            block(tokens, early), block(ext, early), block(tokens, early), block(ext, late),
+            pl.BlockSpec((None, 1, chunks, STATE, GC), lambda ph, i: (LAYERS - 1 - ph, late(i), 0, 0, 0)),
+            of_layer(shared), of_layer(step_in),
         ],
         out_specs=[
-            whole((tokens, depth)), whole((3, share, wide)), whole((share, 2 * STATE + LANES)),
-            whole((groups * 8 + 16, GC)),
+            whole((tokens, depth)), whole((LAYERS, 3, share, wide)), whole((LAYERS, share, 2 * STATE + LANES)),
+            whole((LAYERS,) + few_shape), anywhere,
         ],
         out_shape=[
             jax.ShapeDtypeStruct((tokens, depth), F32),
-            jax.ShapeDtypeStruct((3, share, wide), F32),
-            jax.ShapeDtypeStruct((share, 2 * STATE + LANES), F32),
-            jax.ShapeDtypeStruct((groups * 8 + 16, GC), F32),
+            jax.ShapeDtypeStruct((LAYERS, 3, share, wide), F32),
+            jax.ShapeDtypeStruct((LAYERS, share, 2 * STATE + LANES), F32),
+            jax.ShapeDtypeStruct((LAYERS,) + few_shape, F32),
+            jax.ShapeDtypeStruct((tokens, depth), F32),
         ],
         scratch_shapes=[
             pltpu.VMEM((tokens, depth), BF),
@@ -1006,7 +1137,7 @@
             pltpu.VMEM((slots, tokens, GC), F32),
             pltpu.VMEM((slots, tokens, GC), BF),
             pltpu.VMEM((slots, STATE, GC), F32),
-            pltpu.VMEM((groups, STATE, GC), BF),
+            pltpu.VMEM((LAYERS, groups, STATE, GC), BF),
             pltpu.VMEM((groups, STATE, GC), BF),
             pltpu.VMEM((HALO, depth), F32),
             pltpu.VMEM((chunks, CH, STATE), F32),
@@ -1017,43 +1148,43 @@
             pltpu.VMEM((tokens, LANES), F32),
             pltpu.VMEM((8, LANES), F32),
             pltpu.VMEM((tokens, GC), F32),
-            pltpu.VMEM((HALO, depth), F32),
+            pltpu.VMEM((LAYERS, HALO, depth), F32),
             pltpu.VMEM((groups,) + (2,) * bits + (3, share, GC), BF),
             pltpu.VMEM((2,) * bits + (share, 2 * STATE + LANES), BF),
-            pltpu.VMEM((pieces, 2 * groups // pieces, 3, share, LANES), BF),
-            pltpu.VMEM((pieces, share, 2 * STATE + LANES), BF),
+            pltpu.VMEM((LAYERS, pieces, 2 * groups // pieces, 3, share, LANES), BF),
+            pltpu.VMEM((LAYERS, pieces, share, 2 * STATE + LANES), BF),
             pltpu.SemaphoreType.DMA,
-            pltpu.SemaphoreType.DMA,
+            pltpu.SemaphoreType.DMA((LAYERS,)),
             pltpu.SemaphoreType.DMA((groups,)),
-            pltpu.SemaphoreType.DMA((groups,)),
+            pltpu.SemaphoreType.DMA((LAYERS, groups)),
             pltpu.SemaphoreType.DMA((groups, bits, 2)),
             pltpu.SemaphoreType.DMA((groups, bits, 2)),
             pltpu.SemaphoreType.DMA((groups, 2)),
-            pltpu.SemaphoreType.DMA((pieces, 2 * groups // pieces)),
+            pltpu.SemaphoreType.DMA((LAYERS, pieces, 2 * groups // pieces)),
             pltpu.SemaphoreType.DMA((bits,)),
             pltpu.SemaphoreType.DMA((bits,)),
             pltpu.SemaphoreType.DMA((pieces,)),
-            pltpu.SemaphoreType.DMA((pieces,)),
+            pltpu.SemaphoreType.DMA((LAYERS, pieces)),
             pltpu.SemaphoreType.DMA,
             pltpu.SemaphoreType.DMA((2, depth // GC)),
             pltpu.VMEM((8, LANES), F32),
             pltpu.VMEM((bits + 1,) + few_shape, F32),
             pltpu.VMEM((bits,) + few_shape, F32),
-            pltpu.VMEM((pieces,) + few_shape, F32),
+            pltpu.VMEM((LAYERS, pieces) + few_shape, F32),
             pltpu.SemaphoreType.DMA((bits,)),
             pltpu.SemaphoreType.DMA((bits,)),
             pltpu.SemaphoreType.DMA((pieces,)),
-            pltpu.SemaphoreType.DMA((pieces,)),
+            pltpu.SemaphoreType.DMA((LAYERS, pieces)),
             *[pltpu.VMEM((SLOTS,) + dims_left + (3, share, GC), BF) for dims_left in halves_of],
             *[pltpu.VMEM(dims_left + (share, 2 * STATE + LANES), BF) for dims_left in halves_of],
         ],
         compiler_params=pltpu.CompilerParams(
-            collective_id=3 + layer, has_side_effects=True, vmem_limit_bytes=VMEM_LIMIT, dimension_semantics=("arbitrary",)
+            collective_id=3, has_side_effects=True, vmem_limit_bytes=VMEM_LIMIT, dimension_semantics=("arbitrary", "arbitrary")
         ),
-        name="layer_backward",
+        name="layers_backward",
     )(
-        g, x, after, gain, nxt, nht, r, w, w, w, w, few, pack, pack, pack, pack, pack, csw, csb, keep, biast, carried, tail, kept,
-        gate, val, y, val, y, states, shared, step_in,
+        g, *line, *weight_args, gain, nxt, nht, r, pack, pack, pack, pack, pack, csw, csb, keep, biast, carried, tail,
+        kept, gate, val, y, val, states, shared, step_in,
     )
 
 
@@ -1062,46 +1193,69 @@
     return [sum(jnp.where(z == at, table[at][p], 0) for at in range(pieces)) for p in range(pieces)]
 
 
-class Gather:
+class Line:
+    def __init__(self, place, z, pieces, mine, wall, own_sem, z_send, z_recv):
+        self.place, self.z, self.pieces, self.mine, self.wall = place, z, pieces, mine, wall
+        self.z_send, self.z_recv = z_send, z_recv
+        self.order = near_first(z, pieces)
+        self.own = pltpu.make_async_copy(mine, wall.at[place.mine() + (z,)], own_sem)
+
+    def z_copy(self, zi, up):
+        src = self.mine if zi is self.z else self.wall.at[self.place.mine() + (zi,)]
+        return pltpu.make_async_remote_copy(
+            src_ref=src, dst_ref=self.wall.at[self.place.mine() + (zi,)], send_sem=self.z_send.at[int(up), zi],
+            recv_sem=self.z_recv.at[zi], device_id={"tensor": self.z + (1 if up else -1)}, device_id_type=MESH,
+        )
+
+    def pass_on(self, zi, act):
+        z, last = self.z, self.pieces - 1
+
+        @pl.when(jnp.logical_and(zi <= z, z < last))
+        def _():
+            act(self.z_copy(zi, True))
+
+        @pl.when(jnp.logical_and(zi >= z, z > 0))
+        def _():
+            act(self.z_copy(zi, False))
+
+    def start(self):
+        self.pass_on(self.z, lambda copy: copy.start())
+        self.own.start()
+
+    def arrive(self, p):
+        zi = self.order[p]
+        pltpu.make_async_remote_copy(
+            src_ref=self.mine, dst_ref=self.wall.at[self.place.mine() + (zi,)], send_sem=self.z_send.at[0, zi],
+            recv_sem=self.z_recv.at[zi], device_id={"tensor": zi}, device_id_type=MESH,
+        ).wait_recv()
+        self.pass_on(zi, lambda copy: copy.start())
+
+    def finish(self):
+        for p in range(self.pieces):
+            self.pass_on(self.order[p], lambda copy: copy.wait_send())
+
+
+class Plane:
     def __init__(self, place, z, pieces, mine, wall, few, few_z, few_all, *sems):
         self.place, self.z, self.pieces, self.bits = place, z, pieces, place.bits
         self.mine, self.wall, self.few, self.few_z, self.few_all = mine, wall, few, few_z, few_all
-        self.own_sem, self.z_send, self.z_recv, self.d_send, self.d_recv, *sems = sems
-        self.t_send, self.t_recv, self.f_send, self.f_recv = sems
-        wide = mine.shape[-1]
+        self.d_send, self.d_recv, self.t_send, self.t_recv, self.f_send, self.f_recv = sems
+        wide = wall.shape[-1]
         self.cols = [pl.ds(0, wide // 2), pl.ds(wide // 2, wide // 2)]
         self.few_cols = [pl.ds(0, 2 * STATE), pl.ds(2 * STATE, LANES)]
         self.order = near_first(z, pieces)
         rest = list(range(1, self.bits))
         self.paths = [rest + [0], rest[::-1] + [0]]
-        self.own = pltpu.make_async_copy(mine, wall.at[place.mine() + (z,)], self.own_sem)
-
-    def z_copy(self, zi, up):
-        src = self.mine if zi is self.z else self.wall.at[self.place.mine() + (zi,)]
-        return pltpu.make_async_remote_copy(
-            src_ref=src, dst_ref=self.wall.at[self.place.mine() + (zi,)], send_sem=self.z_send.at[int(up), zi],
-            recv_sem=self.z_recv.at[zi], device_id={"tensor": self.z + (1 if up else -1)}, device_id_type=MESH,
-        )
 
     def d_copy(self, p, half, step):
         path = self.paths[half]
         cols = (slice(None), slice(None), self.cols[half])
         ref = self.wall.at[self.place.along(path[:step]) + (self.order[p],) + cols]
         return pltpu.make_async_remote_copy(
-            src_ref=ref if p or step else self.mine.at[cols], dst_ref=ref, send_sem=self.d_send.at[p, half, step], recv_sem=self.d_recv.at[p, half, step],
+            src_ref=self.mine.at[cols] if self.mine is not None and p + step == 0 else ref, dst_ref=ref,
+            send_sem=self.d_send.at[p, half, step], recv_sem=self.d_recv.at[p, half, step],
             device_id={"dp": self.place.flip(path[step])}, device_id_type=MESH,
         )
-
-    def pass_on(self, zi, act):
-        z, last = self.z, self.pieces - 1
-
-        @pl.when(jnp.logical_and(zi <= z, z < last))
-        def _():
-            act(self.z_copy(zi, True))
-
-        @pl.when(jnp.logical_and(zi >= z, z > 0))
-        def _():
-            act(self.z_copy(zi, False))
 
     def line_copy(self, k):
         return pltpu.make_async_remote_copy(
@@ -1130,47 +1284,22 @@
             if step < self.bits:
                 self.few_copy(half, step).start()
 
-    def start(self):
+    def start(self, p):
         for half in range(2):
-            self.d_copy(0, half, 0).start()
-        self.pass_on(self.z, lambda copy: copy.start())
-        self.own.start()
+            self.d_copy(p, half, 0).start()
+
+    def start_few(self):
         for k in range(1, self.pieces):
             self.line_copy(k).start()
 
-    def arrive(self, p):
-        zi = self.order[p]
-        pltpu.make_async_remote_copy(
-            src_ref=self.mine, dst_ref=self.wall.at[self.place.mine() + (zi,)], send_sem=self.z_send.at[0, zi],
-            recv_sem=self.z_recv.at[zi], device_id={"tensor": zi}, device_id_type=MESH,
-        ).wait_recv()
-        self.pass_on(zi, lambda copy: copy.start())
-        for half in range(2):
-            self.d_copy(p, half, 0).start()
-
     def double(self, p, step):
-        if p == 0 and step == 1:
-            self.own.wait()
         for half in range(2):
             self.d_copy(p, half, step - 1).wait_recv()
             if step < self.bits:
                 self.d_copy(p, half, step).start()
 
-    def events(self):
-        found = []
-        for p in range(self.pieces):
-            if p:
-                found.append((10.0 * p, partial(self.arrive, p)))
-            for step in range(1, self.bits + 1):
-                late = 0.0 if step < self.bits - 1 else 0.8
-                found.append((10.0 * p + 9.5 * step + late, partial(self.double, p, step)))
-        for step in range(self.bits + 1):
-            found.append((5.0 + 8.0 * step, partial(self.few_event, step)))
-        return sorted(found, key=lambda event: event[0])
-
     def finish(self):
         for p in range(self.pieces):
-            self.pass_on(self.order[p], lambda copy: copy.wait_send())
             for half in range(2):
                 for step in range(self.bits):
                     self.d_copy(p, half, step).wait_send()
@@ -1223,15 +1352,17 @@
 
 
 def gather_kernel(
-    dims, starts, tokens_ref, cotangent_ref, cvw, cvb, gate_gain, skip, bias_in, decay, bc, dt, mine, wall, x_all, g_all,
-    few_out, few_later, pack_out, keep, bias, biast, carried, tail, kept,
+    dims, starts, tokens_ref, cotangent_ref, cvw, cvb, gate_gain, skip, bias_in, decay, bc, dt, mine, later,
+    wall, wall_later, x_all, g_all, few_out, few_later, pack_out, keep, bias, biast, carried, tail, kept,
     x_wide, g_wide, pack, pack_all, few, few_z, few_all, wide_sem, pk_send, pk_recv, *sems,
 ):
     pieces, tokens, bits = dims
     place = Place(bits)
     z = lax.axis_index("tensor")
     greet(place, z, pieces)
-    gather = Gather(place, z, pieces, mine, wall, few, few_z, few_all, *sems)
+    line = Line(place, z, pieces, mine, wall, *sems[:3])
+    line_later = Line(place, z, pieces, later, wall_later, *sems[3:6])
+    plane = Plane(place, z, pieces, mine, wall, few, few_z, few_all, *sems[6:])
 
     heads = skip.shape[1]
     upper_half = z >= pieces // 2
@@ -1255,7 +1386,9 @@
             few[...] = wide
         else:
             few_later[...] = wide
-    gather.start()
+    plane.start(0)
+    line.start()
+    plane.start_few()
     channel = iota2((1, cvb.shape[1]), 1) // HD
     for layer in range(LAYERS):
         skips = jnp.zeros(channel.shape, F32)
@@ -1281,9 +1414,34 @@
         wides.append(pltpu.make_async_copy(wide, out, wide_sem.at[k]))
         wides[k].start()
     write_masks(z, tokens, starts, keep, bias, biast, carried, tail, kept)
-    for _, act in gather.events():
+
+    def arrive(p):
+        line.arrive(p)
+        plane.start(p)
+        if p == min(2, pieces - 1):
+            line_later.start()
+
+    def double(p, step):
+        if p == 0 and step == 1:
+            line.own.wait()
+        plane.double(p, step)
+
+    events = []
+    for p in range(pieces):
+        if p:
+            events.append((10.0 * p, partial(arrive, p)))
+            events.append((10.0 * (2 + p) + 5.0, partial(line_later.arrive, p)))
+        for step in range(1, bits + 1):
+            late = 0.0 if step < bits - 1 else 0.8
+            events.append((10.0 * p + 9.5 * step + late, partial(double, p, step)))
+    for step in range(bits + 1):
+        events.append((5.0 + 8.0 * step, partial(plane.few_event, step)))
+    for _, act in sorted(events, key=lambda event: event[0]):
         act()
-    gather.finish()
+    line_later.own.wait()
+    line.finish()
+    line_later.finish()
+    plane.finish()
     for copy in wides:
         copy.wait()
     for k in range(1, pieces):
@@ -1292,29 +1450,34 @@
     pack_out[...] = pack_all[...]
 
 
-def gather_scratch(pieces, bits, share):
+def line_sems(pieces):
+    dma = pltpu.SemaphoreType.DMA
+    return [dma, dma((2, pieces)), dma((pieces,))]
+
+
+def plane_scratch(pieces, bits, share):
     dma = pltpu.SemaphoreType.DMA
     return [pltpu.VMEM((pieces, share, LANES), BF), pltpu.VMEM((2,) * bits + (share, 2 * STATE + LANES), BF)], [
-        dma, dma((2, pieces)), dma((pieces,)), dma((pieces, 2, bits)), dma((pieces, 2, bits)),
-        dma((pieces,)), dma((pieces,)), dma((2, bits)), dma((2, bits)),
+        dma((pieces, 2, bits)), dma((pieces, 2, bits)), dma((pieces,)), dma((pieces,)), dma((2, bits)), dma((2, bits)),
     ]
 
 
-def gather_first(dims, starts, x, g, params, bc, dt, share):
+def gather_first(dims, starts, x, g, params, bc, dt, share, later):
     pieces, tokens, bits = dims
     cut = (2,) * bits
     chunks = tokens // CH
     dma = pltpu.SemaphoreType.DMA
     anywhere = pl.BlockSpec(memory_space=pl.ANY)
     near = pl.BlockSpec(memory_space=pltpu.VMEM)
-    buffers, sems = gather_scratch(pieces, bits, share.shape[1])
+    buffers, sems = plane_scratch(pieces, bits, share.shape[1])
     pack = (LAYERS, 8, params[1].shape[1])
     few = (share.shape[1], 2 * STATE + LANES)
     return pl.pallas_call(
         partial(gather_kernel, dims),
-        in_specs=[pl.BlockSpec(memory_space=pltpu.SMEM)] + [near] * 10 + [anywhere],
-        out_specs=[anywhere] * 3 + [near] * 9,
+        in_specs=[pl.BlockSpec(memory_space=pltpu.SMEM)] + [near] * 10 + [anywhere] * 2,
+        out_specs=[anywhere] * 4 + [near] * 9,
         out_shape=[
+            jax.ShapeDtypeStruct(cut + (pieces,) + share.shape, BF),
             jax.ShapeDtypeStruct(cut + (pieces,) + share.shape, BF),
             jax.ShapeDtypeStruct(x.shape, F32),
             jax.ShapeDtypeStruct(g.shape, F32),
@@ -1331,10 +1494,10 @@
         scratch_shapes=[
             pltpu.VMEM(x.shape, F32), pltpu.VMEM(g.shape, F32), pltpu.VMEM(pack, F32), pltpu.VMEM((pieces,) + pack, F32),
             pltpu.VMEM(few, BF),
-        ] + buffers + [dma((2,)), dma((pieces,)), dma((pieces,))] + sems,
+        ] + buffers + [dma((2,)), dma((pieces,)), dma((pieces,))] + line_sems(pieces) * 2 + sems,
         compiler_params=pltpu.CompilerParams(collective_id=2, has_side_effects=True, vmem_limit_bytes=VMEM_LIMIT),
         name="gather_first",
-    )(starts, x, g, *params, bc, dt, share)
+    )(starts, x, g, *params, bc, dt, share, later)
 
 
 def local(
@@ -1354,21 +1517,20 @@
         jnp.concatenate([jnp.swapaxes(gate_value_weight[layer], 0, 1), w_out[layer][None]], axis=0)
         for layer in range(LAYERS)
     ]
-    wall, x, grad, few_all, few_later, pack, *masks = gather_first(
+    wall, wall_later, x, grad, few_all, few_later, pack, *masks = gather_first(
         (pieces, count, bits), starts, tokens, cotangent,
-        (conv_value_w, conv_value_b, gate_gain, skip_gain, step_bias, decay_log), w_bc, w_dt, shares[0],
+        (conv_value_w, conv_value_b, gate_gain, skip_gain, step_bias, decay_log), w_bc, w_dt, *shares,
     )
     line, saved, weights = [x], [], []
     for layer in range(LAYERS):
-        weights.append((wall.reshape((dp,) + wall.shape[bits:]), few_all.reshape((dp,) + few_all.shape[bits:])))
-        later = (few_later, shares[layer + 1]) if layer + 1 < LAYERS else None
-        x, *kept = layer_forward(
-            dims, bits, layer, x, norm_gain, *weights[-1], pack, conv_shared_w, conv_shared_b, masks, later
+        weights.append((wall.reshape((dp,) + wall.shape[bits:]), few_all))
+        later = (few_later, wall_later) if layer + 1 < LAYERS else None
+        x, *saved = layer_forward(
+            dims, bits, layer, x, norm_gain, *weights[-1], pack, conv_shared_w, conv_shared_b, masks, later, saved
         )
         if later is not None:
-            *kept, few_all, wall = kept
+            *saved, few_all, wall = saved
         line.append(x)
-        saved.append(kept)
     upper_half = z >= pieces // 2
     at = jnp.where(upper_half, pieces - 1 - z, z)
 
@@ -1378,19 +1540,9 @@
         v = lax.dynamic_index_in_dim(v, upper_half.astype(jnp.int32), axis=v.ndim - 2, keepdims=False)
         return v.reshape(v.shape[:-2] + (few,))
 
-    big, small = [None] * LAYERS, [None] * LAYERS
-    for layer in reversed(range(LAYERS)):
-        grad, gw, gm, small[layer] = layer_backward(
-            dims, bits, layer, grad, line[layer], line[layer + 1], norm_gain, saved[layer], *weights[layer], pack,
-            conv_shared_w, conv_shared_b, masks,
-        )
-        gdt = own_heads(gm[:, 2 * STATE :])
-        big[layer] = (jnp.swapaxes(gw[:2], 0, 1), gm[:, : 2 * STATE], gdt, gw[2])
-    small = jnp.stack(small)
-
-    def stacked(member):
-        return jnp.stack([big[layer][member] for layer in range(LAYERS)], axis=0)
-
+    grad, gw, gm, small, _ = layers_backward(
+        dims, bits, grad, line, norm_gain, saved, weights, pack, conv_shared_w, conv_shared_b, masks
+    )
     rows = small[:, : groups * 8].reshape(LAYERS, 2 * groups // pieces, pieces // 2, 8, 2, LANES)
     rows = lax.dynamic_index_in_dim(rows, at, axis=2, keepdims=False)
     rows = lax.dynamic_index_in_dim(rows, upper_half.astype(jnp.int32), axis=3, keepdims=False)
@@ -1400,7 +1552,8 @@
     cuts = depth // GC
     gheads = own_heads(ends[:, cuts].reshape(LAYERS, 2, LANES))
     return (
-        x.astype(BF), grad, stacked(0), stacked(1), stacked(2), stacked(3), ends[:, :cuts].reshape(LAYERS, depth),
+        x.astype(BF), grad, jnp.swapaxes(gw[:, :2], 1, 2), gm[:, :, : 2 * STATE], own_heads(gm[:, :, 2 * STATE :]),
+        gw[:, 2], ends[:, :cuts].reshape(LAYERS, depth),
         rows[:, :4], rows[:, 4], gcs[:, :4], gcs[:, 4], gheads[:, 0], gheads[:, 1],
         jnp.sum(rows[:, 6].reshape(LAYERS, few, HD), axis=2), rows[:, 5],
     )

time: 473 us -> 435 us (0.920); the launches traced: 464 us -> 434 us
  Pallas kernels: 444 us -> 416 us
  other arithmetic: 8 us -> 2.73 us
    pallas_call x2, Pallas kernels: 127 us -> 103 us  [layer_forward(): pl.pallas_call(partial(forward_kernel, dims + (bits, layer, gathers)), gr...]
    pallas_call x2 -> x1, Pallas kernels: 237 us -> 230 us  [layers_backward(): pl.pallas_call(partial(backward_kernel, dims + (bits,)), grid=(LAYERS, st...]
    another operation x7 -> x0, other arithmetic: 5.27 us -> none  [the longest x3 3 us: local(): small = jnp.stack(small)]
where the time goes in v3:
time: 435 us; the launch traced here: 434 us
  Pallas kernels  416 us (96%)
  local copies, waits for them, and re-layouts  14.5 us (3%)
    pallas_call x1, Pallas kernels, layers_backward(): pl.pallas_call(partial(backward_kernel, dims + (bits,)), grid=(LAYERS, st...  230 us
    pallas_call x2, Pallas kernels, layer_forward(): pl.pallas_call(partial(forward_kernel, dims + (bits, layer, gathers)), gr...  103 us
    pallas_call x1, Pallas kernels, gather_first(): pl.pallas_call(partial(gather_kernel, dims), in_specs=[pl.BlockSpec(memor...  83.4 us

profile of v3, /device:TPU:0, one launch (start us, length us, event | category | flops | bytes accessed | tf_op | source)
XLA Modules:
  0.0 434.3 jit_solution(14556101160951972078)
XLA Ops:
  0.7 1.4 fusion
  2.2 0.9 pad_maximum_fusion
  3.2 0.7 copy.56.dt
  3.9 83.4 %gather_first.1 = (bf16[2,2,2,4,3,128,512]{6,5,4,3,2,1,0:T(8,128)(2,1)}, bf16[2,2,2,4,3,128,512]{6,5,4,3,2,1,0:T(8,128)(2,1)}, f32[512,1024]{1,0:T(8,128)}, f32[...) custom-call(s32[1,4]{1,0:T(1,128)} %starts.1, ...), custom_call_target="tpu_custom_call" | custom-call | tf_op jit(solution)/shard_map/gather_first/pallas_call | solution.py:1475
  87.3 67.7 %layer_forward.2 = (f32[512,1024]{1,0:T(8,128)}, bf16[2,1024,512]{2,1,0:T(8,128)(2,1)}, bf16[2,1024,16]{2,1,0:T(8,128)(2,1)}, f32[2,8,512,256]{3,2,1,0:T(8,128)}...) custom-call(f32[512,1024]{1,0:T(8,128)} %get-tuple-element.54.x_ref., ...), custom_call_target="tpu_custom_call", output_to_operand_aliasing={{11}: (20, {})} | custom-call | tf_op jit(solution)/shard_map/layer_forward/pallas_call | solution.py:974
  155.0 35.0 %layer_forward.3 = (f32[512,1024]{1,0:T(8,128)}, bf16[2,1024,512]{2,1,0:T(8,128)(2,1)}, bf16[2,1024,16]{2,1,0:T(8,128)(2,1)}, f32[2,8,512,256]{3,2,1,0:T(8,128)}...) custom-call(f32[512,1024]{1,0:T(8,128)} %get-tuple-element.65.x_ref., ...), custom_call_target="tpu_custom_call", output_to_operand_aliasing={{1}: (19, {}), {2}: (20, {}), {3}: (21, {}), {4}: (22, {}),... | custom-call | tf_op jit(solution)/shard_map/layer_forward/pallas_call | solution.py:974
  190.0 230.2 %layers_backward.1 = (f32[512,1024]{1,0:T(8,128)}, f32[2,3,128,512]{3,2,1,0:T(8,128)}, f32[2,128,384]{2,1,0:T(8,128)}, f32[2,80,256]{2,1,0:T(8,128)}, f32[512,1024]{1,0:T(8,128)}) custom-call(f32[512,1024]{1,0:T(8,128)} %get-tuple-element.78.g_ref, f32[512,1024]{1,0:T(8,128)} %get-tuple-element.54.x_ref.refs_0_, ...), custom_call_target="tpu_custom_call" | custom-call | tf_op jit(solution)/shard_map/layers_backward/pallas_call | solution.py:1099
  420.2 1.3 slice_bitcast_fusion
  421.6 1.8 copy.59
  423.4 1.9 slice_bitcast_fusion.1
  425.2 0.7 slice.73
  426.1 0.7 reduce_sum.9
  426.8 0.6 copy.74
  427.4 0.6 copy.75
  428.0 0.6 slice.88
  428.6 0.6 constant_dynamic-slice_fusion
  429.3 0.1 reshape.72
  429.4 0.1 reshape.73
  429.5 0.6 fusion.5
  430.1 0.6 fusion.3
  430.7 0.6 copy.66
  431.3 0.6 copy.76
  431.9 1.1 convert_element_type.8
  433.0 1.3 copy.88
  (23 shorter events, 0.3 us)
Async XLA Ops:
  0.6 1.5 copy-start.3
  0.7 2.5 copy-start.5
  421.5 3.7 copy-start.2
  421.6 4.4 %copy-start.4 = (f32[2,80,256]{2,1,0:T(8,128)S(1)}, f32[2,80,256]{2,1,0:T(8,128)}, u32[]{:S(2)}) copy-start(f32[2,80,256]{2,1,0:T(8,128)} %get-tuple-element.92) | copy-start | bytes 491524
  421.6 10.3 %copy-start = (f32[512,1024]{1,0:T(8,128)S(1)}, f32[512,1024]{1,0:T(8,128)}, u32[]{:S(2)}) copy-start(f32[512,1024]{1,0:T(8,128)} %get-tuple-element.77.refs_2_) | copy-start | bytes 6291460
  429.5 3.5 copy-start.1

commit v4 on v3

--- a/solution.py
+++ b/solution.py
@@ -11,6 +11,7 @@
 EPS = 1e-05
 HALO = 16
 CH = 128
+TILE = 64
 GC = 256
 HD = 64
 HG = GC // HD
@@ -67,10 +68,18 @@
 
 
 def conv(load, keep_ref, weights, tokens):
+    return conv_rows(load, keep_ref, weights, pl.ds(0, tokens))
+
+
+def conv_rows(load, keep_ref, weights, rows):
     total = weights[4:5] + weights[0:1] * load(0)
     for k in range(1, 4):
-        total = total + weights[k : k + 1] * (load(k) * twice(keep_ref[k - 1]))
+        total = total + weights[k : k + 1] * (load(k) * twice(keep_ref[k - 1, rows, :]))
     return total
+
+
+def tiles(tokens):
+    return range(0, tokens, TILE)
 
 
 def conv_back(grad, load, keep_ref, weights, tokens):
@@ -240,10 +249,13 @@
         slot = lax.rem(group, skew + 1)
         gate_ref[0] = dot_nn(nx[pl.ds(HALO, tokens), :], side((wa, wb), 0))
         val_ref[0] = dot_nn(nx[...], side((wa, wb), 1))
-        mixed = conv(lambda k: val_ref[0, pl.ds(HALO - k, tokens), :], keep_ref, side_params((pa, pb)), tokens)
-        xs[slot] = mixed * sigmoid(mixed)
-        gate = gate_ref[0]
-        gs[slot] = gate * sigmoid(gate)
+        gp = side_params((pa, pb))
+        for start in tiles(tokens):
+            rows = pl.ds(start, TILE)
+            mixed = conv_rows(lambda k: val_ref[0, pl.ds(HALO + start - k, TILE), :], keep_ref, gp, rows)
+            xs[slot, rows, :] = mixed * sigmoid(mixed)
+            gate = gate_ref[0, rows, :]
+            gs[slot, rows, :] = gate * sigmoid(gate)
         turn_sums(col, group)
         spreader = spread(group)
         state = jnp.zeros((STATE, GC), F32)
@@ -375,12 +387,13 @@
     gain_ref, nxt, nht, r_ref, pa, pb, qa, qb, rows_ref, *refs = refs
     csw_ref, csb_ref, keep_ref, biast_ref, carried_ref, tail_ref, kept_ref, *refs = refs
     gate_ref, val_ref, y_ref, valb_ref, state_ref, shared_ref, step_ref, *refs = refs
-    gx_ref, gw_ref, gm_ref, small_ref, mid_ref, *refs = refs
+    gx_ref, gw_ref, go_ref, gm_ref, rows_ref_out, small_ref, mid_ref, *refs = refs
     gb, gbt, r2, inb, outb, outbt, crosst, col, row, terms, ke, *refs = refs
-    dys, xs, fs, dgs, fold, incoming, outgoing, gnorm, dct, dbt, dgt, sd, sp, sq, se, dxd, hrecv, *refs = refs
+    dys, xs, fs, dgs, fold, incoming, outgoing, gnorm, dct, dbt, dgt, sd, sp, sq, se, dxd, turned, hrecv, *refs = refs
     own, own_m, got_z, got_m, halo_send, halo_recv, send, recv, sum_send, sum_recv, z_send, z_recv, *refs = refs
     msum_send, msum_recv, mz_send, mz_recv, next_sem, load_sem, heads_ref, *refs = refs
-    few_total, few_got, few_z, few_send, few_recv, fz_send, fz_recv, *got = refs
+    rows_now, row_total, row_got, row_z, map_total, map_got, map_z, end_total, end_got, end_z, *refs = refs
+    few_send, few_recv, fz_send, fz_recv, *got = refs
     chunks = tokens // CH
     phase, i = pl.program_id(0), pl.program_id(1)
     layer = LAYERS - 1 - phase
@@ -406,11 +419,16 @@
     parts, parts_m = got[:bits], got[bits:]
 
     def part(step, group, half):
-        left = (slice(None),) * (bits - 1 - step + 2)
-        return (lax.rem(group, SLOTS),) + left + (pl.ds(half * LANES, LANES),)
+        return lax.rem(group, SLOTS), half
 
     def held(step, group, half, keep):
-        return (group,) + place.region(half, step, keep) + (slice(None), slice(None), pl.ds(half * LANES, LANES))
+        return (group, half) + place.region(half, step, keep)
+
+    def put_gradient(group, which, value):
+        rows = own.shape[-2] // 3
+        for half in range(2):
+            cut = value[:, half * LANES : (half + 1) * LANES].astype(BF).reshape(place.dims + (rows, LANES))
+            own[(group, half) + place.all + (pl.ds(which * rows, rows),)] = cut
 
     def sum_copy(group, step, half):
         return pltpu.make_async_remote_copy(
@@ -422,7 +440,7 @@
     def z_copy(group, half, turn):
         column = lax.div(group, pieces // 2)
         return pltpu.make_async_remote_copy(
-            src_ref=own.at[(group,) + place.mine() + (slice(None), slice(None), pl.ds(half * LANES, LANES))],
+            src_ref=own.at[(group, half) + place.mine()],
             dst_ref=got_z.at[turn, z, column], send_sem=z_send.at[group, half], recv_sem=z_recv.at[turn, z, column],
             device_id={"tensor": quarter(group, half, pieces)}, device_id_type=MESH,
         )
@@ -474,46 +492,87 @@
             if late <= step:
                 advance(jnp.int32(groups - 1 + late - step), step, turn)
 
-    def few_copy(step):
-        return pltpu.make_async_remote_copy(
-            src_ref=few_total.at[step], dst_ref=few_got.at[step], send_sem=few_send.at[step],
-            recv_sem=few_recv.at[step], device_id={"dp": place.partner(False, step)}, device_id_type=MESH,
-        )
-
-    def few_line(k, turn, source):
-        return pltpu.make_async_remote_copy(
-            src_ref=few_total.at[bits], dst_ref=few_z.at[turn, source], send_sem=fz_send.at[k],
-            recv_sem=fz_recv.at[turn, source],
-            device_id={"tensor": lax.rem(z + k, pieces)}, device_id_type=MESH,
-        )
-
-    def few_advance(step, turn):
+    def put_rows(group, rows, adds):
+        rows = jnp.concatenate(rows, axis=0)
+        at = lax.rem(group, pieces // 2), pl.ds(pl.multiple_of(lax.div(group, pieces // 2) * 8, 8), 8)
+        for half in range(2):
+            cut = rows[:, half * LANES : (half + 1) * LANES]
+            if adds:
+                cut = cut + rows_now[at[0], half, at[1], :]
+            rows_now[at[0], half, at[1], :] = cut
+
+    def quarter_of(at):
+        upper_half = at >= pieces // 2
+        return jnp.where(upper_half, pieces - 1 - at, at), jnp.where(upper_half, 1, 0)
+
+    def few_copies(step, early):
+        refs = [(row_total, row_got), (map_total, map_got)] if early else [(end_total, end_got)]
+        first = 0 if early else 2
+        return [
+            pltpu.make_async_remote_copy(
+                src_ref=total.at[step], dst_ref=other.at[step], send_sem=few_send.at[first + n, step],
+                recv_sem=few_recv.at[first + n, step], device_id={"dp": place.partner(False, step)}, device_id_type=MESH,
+            )
+            for n, (total, other) in enumerate(refs)
+        ]
+
+    def few_lines(k, turn, source, early):
+        target = lax.rem(z + k, pieces)
+        pairs = [(end_total.at[bits], end_z)]
+        if early:
+            pairs = [(row_total.at[(bits,) + quarter_of(target)], row_z), (map_total.at[bits], map_z)]
+        first = 0 if early else 2
+        return [
+            pltpu.make_async_remote_copy(
+                src_ref=ref, dst_ref=other.at[turn, source], send_sem=fz_send.at[first + n, k],
+                recv_sem=fz_recv.at[turn, first + n, source], device_id={"tensor": target}, device_id_type=MESH,
+            )
+            for n, (ref, other) in enumerate(pairs)
+        ]
+
+    def few_advance(step, turn, early):
         if step:
-            few_copy(step - 1).wait_recv()
-            few_total[step] = few_total[step - 1] + few_got[step - 1]
+            for copy in few_copies(step - 1, early):
+                copy.wait_recv()
+            for total, other in [(row_total, row_got), (map_total, map_got)] if early else [(end_total, end_got)]:
+                total[step] = total[step - 1] + other[step - 1]
         if step < bits:
-            few_copy(step).start()
+            for copy in few_copies(step, early):
+                copy.start()
         else:
             for k in range(1, pieces):
-                few_line(k, turn, z).start()
-            few_z[turn, z] = few_total[bits]
+                for copy in few_lines(k, turn, z, early):
+                    copy.start()
+            if early:
+                row_z[turn, z] = row_total[(bits,) + quarter_of(z)]
+                map_z[turn, z] = map_total[bits]
+            else:
+                end_z[turn, z] = end_total[bits]
 
     def finish_few(turn):
         for n in range(1, pieces):
-            few_line(n, turn, lax.rem(z + n, pieces)).wait_recv()
-            misc_z(n, turn, lax.rem(z + n, pieces)).wait_recv()
-        total, misc = few_z[turn, 0], got_m[turn, 0].astype(F32)
+            source = lax.rem(z + n, pieces)
+            for copy in few_lines(n, turn, source, True) + few_lines(n, turn, source, False):
+                copy.wait_recv()
+            misc_z(n, turn, source).wait_recv()
+        misc = got_m[turn, 0].astype(F32)
+        sums = [ref[turn, 0] for ref in (row_z, map_z, end_z)]
         for source in range(1, pieces):
-            total = total + few_z[turn, source]
+            sums = [total + ref[turn, source] for total, ref in zip(sums, (row_z, map_z, end_z))]
             misc = misc + got_m[turn, source].astype(F32)
-        small_ref[LAYERS - 1 - turn] = total
-        gm_ref[LAYERS - 1 - turn] = misc
+        layer_done = LAYERS - 1 - turn
+        rows_ref_out[layer_done] = sums[0]
+        small_ref[layer_done, pl.ds(0, 8), :] = sums[1]
+        small_ref[layer_done, pl.ds(8, 8), :] = sums[2]
+        gm_ref[layer_done] = misc
         for step in range(bits):
             misc_copy(step).wait_send()
-            few_copy(step).wait_send()
+            for copy in few_copies(step, True) + few_copies(step, False):
+                copy.wait_send()
         for n in range(1, pieces):
             misc_z(n, turn, z).wait_send()
-            few_line(n, turn, z).wait_send()
+            for copy in few_lines(n, turn, z, True) + few_lines(n, turn, z, False):
+                copy.wait_send()
 
     def finish_group(group, turn):
         column = lax.div(group, pieces // 2)
@@ -521,8 +580,7 @@
 
             @pl.when(quarter(group, half, pieces) == z)
             def _(half=half):
-                total = own[(group,) + place.mine() + (slice(None), slice(None), pl.ds(half * LANES, LANES))]
-                total = total.astype(F32)
+                total = own[(group, half) + place.mine()].astype(F32)
                 for n in range(1, pieces):
                     source = lax.rem(z + n, pieces)
                     pltpu.make_async_remote_copy(
@@ -532,7 +590,9 @@
                     ).wait_recv()
                     total = total + got_z[turn, source, column].astype(F32)
                 at = pl.multiple_of(column * LANES, LANES)
-                gw_ref[LAYERS - 1 - turn, :, :, pl.ds(at, LANES)] = total
+                total = total.reshape(3, -1, LANES)
+                gw_ref[LAYERS - 1 - turn, :, :, pl.ds(at, LANES)] = total[:2]
+                go_ref[LAYERS - 1 - turn, :, pl.ds(at, LANES)] = total[2]
 
             @pl.when(quarter(group, half, pieces) != z)
             def _(half=half):
@@ -635,12 +695,6 @@
         group = i
         slot = lax.rem(group, skew + 1)
         gp = side_params((pa, pb))
-        mixed = conv(lambda k: val_ref[0, pl.ds(HALO - k, tokens), :], keep_ref, gp, tokens)
-        part = sigmoid(mixed)
-        x = mixed * part
-        xs[slot] = x
-        fs[slot] = part + x * (1.0 - part)
-        r = twice(r_ref[...])
 
         for turn in range(1, LAYERS):
 
@@ -648,29 +702,32 @@
             def _(turn=turn):
                 finish_group(group, turn - 1)
 
-        gm = dot_nn(gb[...], out_weights())
-        scan = y_ref[0] + gp[6:7] * x
-        gate = gate_ref[0]
-        part = sigmoid(gate)
-        silu = gate * part
-        gated = scan * silu
-        normal = gated * r
-        own[(group,) + place.all + (2,)] = (
-            dot_nn(gbt[...], (normal * gp[5:6]).astype(BF)).astype(BF).reshape(place.dims + (-1, GC))
-        )
-        ggated = r * gp[5:6] * gm - gated * twice(r2[...])
-        dy = ggated * silu
-        dys[slot] = dy.astype(BF)
-        dgs[slot] = (ggated * scan * (part + silu * (1.0 - part))).astype(BF)
-        small_ref[layer, pl.ds(group * 8, 8), :] = jnp.concatenate(
-            [
-                jnp.zeros((5, GC), F32),
-                jnp.sum(gm * normal, axis=0, keepdims=True),
-                jnp.sum(dy * x, axis=0, keepdims=True),
-                jnp.zeros((1, GC), F32),
-            ],
-            axis=0,
-        )
+        dxd[...] = dot_nn(gb[...], out_weights())
+        gain_sum = skip_sum = jnp.zeros((1, GC), F32)
+        for start in tiles(tokens):
+            rows = pl.ds(start, TILE)
+            mixed = conv_rows(lambda k: val_ref[0, pl.ds(HALO + start - k, TILE), :], keep_ref, gp, rows)
+            part = sigmoid(mixed)
+            x = mixed * part
+            xs[slot, rows, :] = x
+            fs[slot, rows, :] = part + x * (1.0 - part)
+            r = twice(r_ref[rows, :])
+            gm = dxd[rows, :]
+            scan = y_ref[0, rows, :] + gp[6:7] * x
+            gate = gate_ref[0, rows, :]
+            part = sigmoid(gate)
+            silu = gate * part
+            gated = scan * silu
+            normal = gated * r
+            turned[rows, :] = (normal * gp[5:6]).astype(BF)
+            ggated = r * gp[5:6] * gm - gated * twice(r2[rows, :])
+            dy = ggated * silu
+            dys[slot, rows, :] = dy.astype(BF)
+            dgs[slot, rows, :] = (ggated * scan * (part + silu * (1.0 - part))).astype(BF)
+            gain_sum = gain_sum + jnp.sum(gm * normal, axis=0, keepdims=True)
+            skip_sum = skip_sum + jnp.sum(dy * x, axis=0, keepdims=True)
+        put_gradient(group, 2, dot_nn(gbt[...], turned[...]))
+        put_rows(group, [jnp.zeros((5, GC), F32), gain_sum, skip_sum, jnp.zeros((1, GC), F32)], False)
         spreader, collector = spread(group), collect(group)
         state = jnp.zeros((STATE, GC), F32)
         for c in reversed(range(chunks)):
@@ -689,7 +746,8 @@
             def _(turn=turn, late=late):
                 drain(late, turn - 1)
                 if late <= bits:
-                    few_advance(late, turn - 1)
+                    few_advance(late, turn - 1, True)
+                    few_advance(late, turn - 1, False)
                     misc_advance(late, turn - 1)
 
         @pl.when(jnp.logical_and(phase == turn, i == skew))
@@ -767,18 +825,15 @@
         wide, sums = conv_back(
             dxd[...], lambda k: valb_ref[0, pl.ds(HALO - k, tokens), :], keep_ref, gp, tokens
         )
-        small_ref[layer, pl.ds(group * 8, 8), :] += jnp.concatenate(sums + [jnp.zeros((3, GC), F32)], axis=0)
+        put_rows(group, sums + [jnp.zeros((3, GC), F32)], True)
         wide = wide.astype(BF)
         dgate = dgs[slot]
-        shape = place.dims + (-1, GC)
-        own[(group,) + place.all + (0,)] = dot_nn(nxt[...], dgate).astype(BF).reshape(shape)
-        own[(group,) + place.all + (1,)] = (
-            (dot_nn(nxt[...], wide[HALO:]) + dot_nn(nht[...], wide[:HALO])).astype(BF).reshape(shape)
-        )
+        put_gradient(group, 0, dot_nn(nxt[...], dgate))
+        put_gradient(group, 1, dot_nn(nxt[...], wide[HALO:]) + dot_nn(nht[...], wide[:HALO]))
         advance(group, 0, phase)
-        back_wide = dot_nt(wide, in_weights(1))
-        gnorm[...] += back_wide[:HALO]
-        gx_ref[...] += back_wide[HALO:] + dot_nt(dgate, in_weights(0))
+        both = jnp.concatenate([in_weights(0), in_weights(1)], axis=1)
+        gnorm[...] += dot_nt(wide[:HALO], both[:, GC:])
+        gx_ref[...] += dot_nt(jnp.concatenate([dgate, wide[HALO:]], axis=1), both)
 
     @pl.when(i == groups + skew - 1)
     def _():
@@ -810,7 +865,9 @@
         part = sigmoid(mixed)
         dmixed = jnp.concatenate(dmaps, axis=0) * (part + mixed * part * (1.0 - part))
         wide, sums = conv_back(dmixed, lambda k: shared_ref[pl.ds(HALO - k, tokens), :], keep_ref, taps(), tokens)
-        small_ref[layer, pl.ds(groups * 8, 8), :] = jnp.concatenate(sums + [jnp.zeros((3, 2 * STATE), F32)], axis=0)
+        row_total[0] = rows_now[...]
+        map_total[0] = jnp.concatenate(sums + [jnp.zeros((3, 2 * STATE), F32)], axis=0)
+        few_advance(0, phase, True)
         wide = wide.astype(BF)
         dstep = dstep.astype(BF)
         pltpu.make_async_copy(weights[0][4], own_m, next_sem).wait()
@@ -851,11 +908,8 @@
         q = lax.rsqrt(power * (1.0 / depth) + EPS)
         inside = inside * (q * q * q) * (1.0 / depth)
         cuts = [jnp.sum(gx_ref[:, cols] * xs[k] * q, axis=0, keepdims=True) for k, cols in blocks]
-        few_total[0, pl.ds(0, groups * 8 + 8), :] = small_ref[layer, pl.ds(0, groups * 8 + 8), :]
-        few_total[0, pl.ds(groups * 8 + 8, 8), :] = jnp.concatenate(
-            cuts + [head_sums, jnp.zeros((7 - len(cuts), GC), F32)], axis=0
-        )
-        few_advance(0, phase)
+        end_total[0] = jnp.concatenate(cuts + [head_sums, jnp.zeros((7 - len(cuts), GC), F32)], axis=0)
+        few_advance(0, phase, False)
         for k, cols in blocks:
             gx_ref[:, cols] = fs[k] + q * (gx_ref[:, cols] * gain[:, cols]) - xs[k] * inside
 
@@ -868,12 +922,14 @@
         @pl.when(at_end)
         def _():
             turn = LAYERS - 1
+            few_advance(1, turn, True)
             misc_advance(1, turn)
             for step in range(2, bits + 1):
                 drain(step, turn)
-                few_advance(step - 1, turn)
+                few_advance(step, turn, True)
+                few_advance(step - 1, turn, False)
                 misc_advance(step, turn)
-            few_advance(bits, turn)
+            few_advance(bits, turn, False)
             finish_few(turn)
             for group in range(groups):
                 finish_group(jnp.int32(group), turn)
@@ -1050,7 +1106,9 @@
     _, _, _, share, wide = wall.shape
     ext = tokens + HALO
     slots = max(skew + 1, depth // GC)
-    few_shape = (groups * 8 + 16, GC)
+    columns = 2 * groups // pieces
+    row_shape = (pieces // 2, 2, columns * 8, LANES)
+    few_shape = (8, GC)
     halves_of = [(2,) * (bits - 1 - step) for step in range(bits)]
     steps = groups + skew
     early, late, *_ = group_specs(dims, wall.shape)
@@ -1110,14 +1168,17 @@
             of_layer(shared), of_layer(step_in),
         ],
         out_specs=[
-            whole((tokens, depth)), whole((LAYERS, 3, share, wide)), whole((LAYERS, share, 2 * STATE + LANES)),
-            whole((LAYERS,) + few_shape), anywhere,
+            whole((tokens, depth)), whole((LAYERS, 2, share, wide)), whole((LAYERS, share, wide)),
+            whole((LAYERS, share, 2 * STATE + LANES)),
+            whole((LAYERS, columns * 8, LANES)), whole((LAYERS, 16, GC)), anywhere,
         ],
         out_shape=[
             jax.ShapeDtypeStruct((tokens, depth), F32),
-            jax.ShapeDtypeStruct((LAYERS, 3, share, wide), F32),
+            jax.ShapeDtypeStruct((LAYERS, 2, share, wide), F32),
+            jax.ShapeDtypeStruct((LAYERS, share, wide), F32),
             jax.ShapeDtypeStruct((LAYERS, share, 2 * STATE + LANES), F32),
-            jax.ShapeDtypeStruct((LAYERS,) + few_shape, F32),
+            jax.ShapeDtypeStruct((LAYERS, columns * 8, LANES), F32),
+            jax.ShapeDtypeStruct((LAYERS, 16, GC), F32),
             jax.ShapeDtypeStruct((tokens, depth), F32),
         ],
         scratch_shapes=[
@@ -1148,10 +1209,11 @@
             pltpu.VMEM((tokens, LANES), F32),
             pltpu.VMEM((8, LANES), F32),
             pltpu.VMEM((tokens, GC), F32),
+            pltpu.VMEM((tokens, GC), BF),
             pltpu.VMEM((LAYERS, HALO, depth), F32),
-            pltpu.VMEM((groups,) + (2,) * bits + (3, share, GC), BF),
+            pltpu.VMEM((groups, 2) + (2,) * bits + (3 * share, LANES), BF),
             pltpu.VMEM((2,) * bits + (share, 2 * STATE + LANES), BF),
-            pltpu.VMEM((LAYERS, pieces, 2 * groups // pieces, 3, share, LANES), BF),
+            pltpu.VMEM((LAYERS, pieces, 2 * groups // pieces, 3 * share, LANES), BF),
             pltpu.VMEM((LAYERS, pieces, share, 2 * STATE + LANES), BF),
             pltpu.SemaphoreType.DMA,
             pltpu.SemaphoreType.DMA((LAYERS,)),
@@ -1168,14 +1230,21 @@
             pltpu.SemaphoreType.DMA,
             pltpu.SemaphoreType.DMA((2, depth // GC)),
             pltpu.VMEM((8, LANES), F32),
+            pltpu.VMEM(row_shape, F32),
+            pltpu.VMEM((bits + 1,) + row_shape, F32),
+            pltpu.VMEM((bits,) + row_shape, F32),
+            pltpu.VMEM((LAYERS, pieces) + row_shape[2:], F32),
             pltpu.VMEM((bits + 1,) + few_shape, F32),
             pltpu.VMEM((bits,) + few_shape, F32),
             pltpu.VMEM((LAYERS, pieces) + few_shape, F32),
-            pltpu.SemaphoreType.DMA((bits,)),
-            pltpu.SemaphoreType.DMA((bits,)),
-            pltpu.SemaphoreType.DMA((pieces,)),
-            pltpu.SemaphoreType.DMA((LAYERS, pieces)),
-            *[pltpu.VMEM((SLOTS,) + dims_left + (3, share, GC), BF) for dims_left in halves_of],
+            pltpu.VMEM((bits + 1,) + few_shape, F32),
+            pltpu.VMEM((bits,) + few_shape, F32),
+            pltpu.VMEM((LAYERS, pieces) + few_shape, F32),
+            pltpu.SemaphoreType.DMA((3, bits)),
+            pltpu.SemaphoreType.DMA((3, bits)),
+            pltpu.SemaphoreType.DMA((3, pieces)),
+            pltpu.SemaphoreType.DMA((LAYERS, 3, pieces)),
+            *[pltpu.VMEM((SLOTS, 2) + dims_left + (3 * share, LANES), BF) for dims_left in halves_of],
             *[pltpu.VMEM(dims_left + (share, 2 * STATE + LANES), BF) for dims_left in halves_of],
         ],
         compiler_params=pltpu.CompilerParams(
@@ -1435,7 +1504,7 @@
             late = 0.0 if step < bits - 1 else 0.8
             events.append((10.0 * p + 9.5 * step + late, partial(double, p, step)))
     for step in range(bits + 1):
-        events.append((5.0 + 8.0 * step, partial(plane.few_event, step)))
+        events.append((12.0 + 10.0 * step, partial(plane.few_event, step)))
     for _, act in sorted(events, key=lambda event: event[0]):
         act()
     line_later.own.wait()
@@ -1474,7 +1543,7 @@
     few = (share.shape[1], 2 * STATE + LANES)
     return pl.pallas_call(
         partial(gather_kernel, dims),
-        in_specs=[pl.BlockSpec(memory_space=pltpu.SMEM)] + [near] * 10 + [anywhere] * 2,
+        in_specs=[pl.BlockSpec(memory_space=pltpu.SMEM)] + [near] * 12,
         out_specs=[anywhere] * 4 + [near] * 9,
         out_shape=[
             jax.ShapeDtypeStruct(cut + (pieces,) + share.shape, BF),
@@ -1540,20 +1609,16 @@
         v = lax.dynamic_index_in_dim(v, upper_half.astype(jnp.int32), axis=v.ndim - 2, keepdims=False)
         return v.reshape(v.shape[:-2] + (few,))
 
-    grad, gw, gm, small, _ = layers_backward(
+    grad, gw, go, gm, rows, small, _ = layers_backward(
         dims, bits, grad, line, norm_gain, saved, weights, pack, conv_shared_w, conv_shared_b, masks
     )
-    rows = small[:, : groups * 8].reshape(LAYERS, 2 * groups // pieces, pieces // 2, 8, 2, LANES)
-    rows = lax.dynamic_index_in_dim(rows, at, axis=2, keepdims=False)
-    rows = lax.dynamic_index_in_dim(rows, upper_half.astype(jnp.int32), axis=3, keepdims=False)
-    rows = jnp.swapaxes(rows, 1, 2).reshape(LAYERS, 8, own)
-    gcs = small[:, groups * 8 : groups * 8 + 8]
-    ends = small[:, groups * 8 + 8 :]
+    rows = jnp.swapaxes(rows.reshape(LAYERS, -1, 8, LANES), 1, 2).reshape(LAYERS, 8, own)
+    gcs, ends = small[:, :8], small[:, 8:]
     cuts = depth // GC
     gheads = own_heads(ends[:, cuts].reshape(LAYERS, 2, LANES))
     return (
-        x.astype(BF), grad, jnp.swapaxes(gw[:, :2], 1, 2), gm[:, :, : 2 * STATE], own_heads(gm[:, :, 2 * STATE :]),
-        gw[:, 2], ends[:, :cuts].reshape(LAYERS, depth),
+        x.astype(BF), grad, jnp.swapaxes(gw, 1, 2), gm[:, :, : 2 * STATE], own_heads(gm[:, :, 2 * STATE :]),
+        go, ends[:, :cuts].reshape(LAYERS, depth),
         rows[:, :4], rows[:, 4], gcs[:, :4], gcs[:, 4], gheads[:, 0], gheads[:, 1],
         jnp.sum(rows[:, 6].reshape(LAYERS, few, HD), axis=2), rows[:, 5],
     )

time: 435 us -> 423 us (0.972)
  Pallas kernels: 416 us -> 401 us
    pallas_call x1, Pallas kernels: 230 us -> 222 us  [layers_backward(): pl.pallas_call(partial(backward_kernel, dims + (bits,)), grid=(LAYERS, st...]
    pallas_call x1, Pallas kernels: 83.4 us -> 76.6 us  [gather_first(): pl.pallas_call(partial(gather_kernel, dims), in_specs=[pl.BlockSpec(memor...]
where the time goes in v4:
time: 423 us; the launch traced here: 422 us
  Pallas kernels  401 us (95%)
  local copies, waits for them, and re-layouts  18 us (4%)
    pallas_call x1, Pallas kernels, layers_backward(): pl.pallas_call(partial(backward_kernel, dims + (bits,)), grid=(LAYERS, st...  222 us
    pallas_call x2, Pallas kernels, layer_forward(): pl.pallas_call(partial(forward_kernel, dims + (bits, layer, gathers)), gr...  102 us
    pallas_call x1, Pallas kernels, gather_first(): pl.pallas_call(partial(gather_kernel, dims), in_specs=[pl.BlockSpec(memor...  76.6 us

profile of v4, /device:TPU:0, one launch (start us, length us, event | category | flops | bytes accessed | tf_op | source)
XLA Modules:
  0.0 422.4 jit_solution(13101742505177941631)
XLA Ops:
  0.7 1.4 fusion
  2.1 1.0 fusion.1
  3.1 0.9 pad_maximum_fusion
  4.1 0.7 copy.50.dt
  4.8 76.6 %gather_first.1 = (bf16[2,2,2,4,3,128,512]{6,5,4,3,2,1,0:T(8,128)(2,1)}, bf16[2,2,2,4,3,128,512]{6,5,4,3,2,1,0:T(8,128)(2,1)}, f32[512,1024]{1,0:T(8,128)}, f32[...) custom-call(s32[1,4]{1,0:T(1,128)} %starts.1, ...), custom_call_target="tpu_custom_call" | custom-call | tf_op jit(solution)/shard_map/gather_first/pallas_call | solution.py:1544
  81.4 65.7 %layer_forward.2 = (f32[512,1024]{1,0:T(8,128)}, bf16[2,1024,512]{2,1,0:T(8,128)(2,1)}, bf16[2,1024,16]{2,1,0:T(8,128)(2,1)}, f32[2,8,512,256]{3,2,1,0:T(8,128)}...) custom-call(f32[512,1024]{1,0:T(8,128)} %get-tuple-element.56.x_ref., ...), custom_call_target="tpu_custom_call", output_to_operand_aliasing={{11}: (20, {})} | custom-call | tf_op jit(solution)/shard_map/layer_forward/pallas_call | solution.py:1030
  147.1 36.6 %layer_forward.3 = (f32[512,1024]{1,0:T(8,128)}, bf16[2,1024,512]{2,1,0:T(8,128)(2,1)}, bf16[2,1024,16]{2,1,0:T(8,128)(2,1)}, f32[2,8,512,256]{3,2,1,0:T(8,128)}...) custom-call(f32[512,1024]{1,0:T(8,128)} %get-tuple-element.67.x_ref., ...), custom_call_target="tpu_custom_call", output_to_operand_aliasing={{1}: (19, {}), {2}: (20, {}), {3}: (21, {}), {4}: (22, {}),... | custom-call | tf_op jit(solution)/shard_map/layer_forward/pallas_call | solution.py:1030
  183.7 222.0 %layers_backward.1 = (f32[512,1024]{1,0:T(8,128)}, f32[2,2,128,512]{3,2,1,0:T(8,128)}, f32[2,128,512]{2,1,0:T(8,128)}, f32[2,128,384]{2,1,0:T(8,128)}, f32[2,32,...) custom-call(f32[512,1024]{1,0:T(8,128)} %get-tuple-element.80.g_ref, ...), custom_call_target="tpu_custom_call" | custom-call | tf_op jit(solution)/shard_map/layers_backward/pallas_call | solution.py:1157
  405.8 3.2 copy.53
  409.0 1.7 slice.63
  410.6 1.0 slice.64
  411.7 0.6 constant_dynamic-slice_fusion
  412.3 0.8 copy.52
  413.1 0.6 copy.54
  413.7 0.6 slice_bitcast_fusion.1
  414.4 0.7 reduce_sum.9
  415.0 0.7 fusion.2
  416.0 0.6 fusion.4
  416.6 1.4 fusion.3
  418.0 0.6 copy.58
  418.6 0.6 copy.64
  419.2 1.1 convert_element_type.7
  420.3 1.3 copy.77
  421.6 0.8 copy.78
  (17 shorter events, 0.5 us)
Async XLA Ops:
  0.6 3.4 copy-start.3
  405.8 13.4 %copy-start = (f32[512,1024]{1,0:T(8,128)S(1)}, f32[512,1024]{1,0:T(8,128)}, u32[]{:S(2)}) copy-start(f32[512,1024]{1,0:T(8,128)} %get-tuple-element.79.refs_2_) | copy-start | bytes 6291460
  410.6 11.0 %copy-start.2 = (f32[2,128,512]{2,1,0:T(8,128)S(1)}, f32[2,128,512]{2,1,0:T(8,128)}, u32[]{:S(2)}) copy-start(f32[2,128,512]{2,1,0:T(8,128)} %get-tuple-element.162) | copy-start | bytes 1572868
  416.0 4.3 %copy-start.1 = (f32[512,1024]{1,0:T(8,128)S(1)}, f32[512,1024]{1,0:T(8,128)}, u32[]{:S(2)}) copy-start(f32[512,1024]{1,0:T(8,128)} %get-tuple-element.158) | copy-start | bytes 6291460

commit v5 on v4

--- a/solution.py
+++ b/solution.py
@@ -816,7 +816,7 @@
             lowered = sized.astype(BF).astype(F32) * within
             sd[rows, :] += dot_nn(split2(whole * x), collector)
             sp[rows, :] -= dot_nn(split2(lowered), collector)
-            sq[rows, :] += dot_nn(split2(sized * later), collector)
+            sq[rows, :] += dot_nn((sized * later).astype(BF), collector[:GC])
             dxd[rows, :] = (whole * steps + gp[6:7] * dy) * fs[slot, rows, :]
         for step in reversed(range(1, bits + 1)):
             advance(group - step, step, phase)
@@ -930,8 +930,10 @@
                 few_advance(step - 1, turn, False)
                 misc_advance(step, turn)
             few_advance(bits, turn, False)
+            for group in range(groups - 2):
+                finish_group(jnp.int32(group), turn)
             finish_few(turn)
-            for group in range(groups):
+            for group in range(groups - 2, groups):
                 finish_group(jnp.int32(group), turn)
 
 

time: 423 us -> 421 us (level)
  no operation moved by 1% of the time
where the time goes in v5:
time: 421 us; the launch traced here: 420 us
  Pallas kernels  399 us (95%)
  local copies, waits for them, and re-layouts  18 us (4%)
    pallas_call x1, Pallas kernels, layers_backward(): pl.pallas_call(partial(backward_kernel, dims + (bits,)), grid=(LAYERS, st...  220 us
    pallas_call x2, Pallas kernels, layer_forward(): pl.pallas_call(partial(forward_kernel, dims + (bits, layer, gathers)), gr...  102 us
    pallas_call x1, Pallas kernels, gather_first(): pl.pallas_call(partial(gather_kernel, dims), in_specs=[pl.BlockSpec(memor...  76.6 us

profile of v5, /device:TPU:0, one launch (start us, length us, event | category | flops | bytes accessed | tf_op | source)
XLA Modules:
  0.0 420.2 jit_solution(4846163067732093796)
XLA Ops:
  0.7 1.4 fusion
  2.1 1.0 fusion.1
  3.1 0.9 pad_maximum_fusion
  4.1 0.7 copy.50.dt
  4.8 76.6 %gather_first.1 = (bf16[2,2,2,4,3,128,512]{6,5,4,3,2,1,0:T(8,128)(2,1)}, bf16[2,2,2,4,3,128,512]{6,5,4,3,2,1,0:T(8,128)(2,1)}, f32[512,1024]{1,0:T(8,128)}, f32[...) custom-call(s32[1,4]{1,0:T(1,128)} %starts.1, ...), custom_call_target="tpu_custom_call" | custom-call | tf_op jit(solution)/shard_map/gather_first/pallas_call | solution.py:1546
  81.4 65.7 %layer_forward.2 = (f32[512,1024]{1,0:T(8,128)}, bf16[2,1024,512]{2,1,0:T(8,128)(2,1)}, bf16[2,1024,16]{2,1,0:T(8,128)(2,1)}, f32[2,8,512,256]{3,2,1,0:T(8,128)}...) custom-call(f32[512,1024]{1,0:T(8,128)} %get-tuple-element.56.x_ref., ...), custom_call_target="tpu_custom_call", output_to_operand_aliasing={{11}: (20, {})} | custom-call | tf_op jit(solution)/shard_map/layer_forward/pallas_call | solution.py:1032
  147.1 36.6 %layer_forward.3 = (f32[512,1024]{1,0:T(8,128)}, bf16[2,1024,512]{2,1,0:T(8,128)(2,1)}, bf16[2,1024,16]{2,1,0:T(8,128)(2,1)}, f32[2,8,512,256]{3,2,1,0:T(8,128)}...) custom-call(f32[512,1024]{1,0:T(8,128)} %get-tuple-element.67.x_ref., ...), custom_call_target="tpu_custom_call", output_to_operand_aliasing={{1}: (19, {}), {2}: (20, {}), {3}: (21, {}), {4}: (22, {}),... | custom-call | tf_op jit(solution)/shard_map/layer_forward/pallas_call | solution.py:1032
  183.7 219.8 %layers_backward.1 = (f32[512,1024]{1,0:T(8,128)}, f32[2,2,128,512]{3,2,1,0:T(8,128)}, f32[2,128,512]{2,1,0:T(8,128)}, f32[2,128,384]{2,1,0:T(8,128)}, f32[2,32,...) custom-call(f32[512,1024]{1,0:T(8,128)} %get-tuple-element.80.g_ref, ...), custom_call_target="tpu_custom_call" | custom-call | tf_op jit(solution)/shard_map/layers_backward/pallas_call | solution.py:1159
  403.6 3.2 copy.53
  406.7 1.7 slice.63
  408.4 1.0 slice.64
  409.4 0.6 constant_dynamic-slice_fusion
  410.1 0.8 copy.52
  410.9 0.6 copy.54
  411.5 0.6 slice_bitcast_fusion.1
  412.2 0.7 reduce_sum.9
  412.8 0.7 fusion.2
  413.8 0.6 fusion.4
  414.4 1.4 fusion.3
  415.8 0.6 copy.58
  416.4 0.6 copy.64
  416.9 1.1 convert_element_type.7
  418.1 1.3 copy.77
  419.4 0.8 copy.78
  (17 shorter events, 0.5 us)
Async XLA Ops:
  0.6 3.4 copy-start.3
  403.6 13.4 %copy-start = (f32[512,1024]{1,0:T(8,128)S(1)}, f32[512,1024]{1,0:T(8,128)}, u32[]{:S(2)}) copy-start(f32[512,1024]{1,0:T(8,128)} %get-tuple-element.79.refs_2_) | copy-start | bytes 6291460
  408.4 11.0 %copy-start.2 = (f32[2,128,512]{2,1,0:T(8,128)S(1)}, f32[2,128,512]{2,1,0:T(8,128)}, u32[]{:S(2)}) copy-start(f32[2,128,512]{2,1,0:T(8,128)} %get-tuple-element.162) | copy-start | bytes 1572868
  413.8 4.3 %copy-start.1 = (f32[512,1024]{1,0:T(8,128)S(1)}, f32[512,1024]{1,0:T(8,128)}, u32[]{:S(2)}) copy-start(f32[512,1024]{1,0:T(8,128)} %get-tuple-element.158) | copy-start | bytes 6291460
